TPU v7x, 1024 devices: a whole 8x8x8 slice. The times are simulated.
1024 devices in a mesh: dp: 8 (over x_hi, core), mp: 128 (over y, z, x_lo).
Axes of the slice: x: 8 (x_hi: 4, x_lo: 2; x = x_hi * 2 + x_lo), y: 8, z: 8, core: 2. Of those that a mesh axis runs over, the one named last changes fastest.
Arguments:
- patches: bfloat16 [8, 192, 6144], P('dp', None, 'mp'), may hold values from -550 to 550
- keep_list: int32 [8, 128], P('dp'), may hold values from 0 to 191, as said below
- norm_gain: float32 [6144], replicated, may hold values from 0.1 to 1.9
- up_weight: bfloat16 [6144, 24576], P(None, 'mp'), may hold values from -0.078125 to 0.078125
- hidden_grad: bfloat16 [8, 128, 24576], P('dp', None, 'mp'), may hold values from -0.3984375 to 0.3984375
Outputs:
- hidden: bfloat16 [8, 128, 24576], P('dp', None, 'mp')
- weight_grad: float32 [6144, 24576], P('dp', 'mp')
Inputs may be any that keep to these rules, and one draw needn't show every extreme that they name: `keep_list`: each image's list is increasing and always holds 0 and 191.
All inputs are finite; a program needn't handle non-finite values.
Results may differ from a plain program's by a relative error of at most 0.0055.
Values may be sent and summed in bfloat16 or wider, within the bound.
No kernel may reach another device: no remote copies, remote signals or barrier semaphores. Data moves between devices by JAX's collectives and lax.ppermute only.
A program may use at most 32 MiB of HBM per device.

v0:
```python
import jax
import jax.numpy as jnp
from jax import lax
from jax.sharding import PartitionSpec as P

epsilon = 1e-06


def normalize(tokens, norm_gain):
    values = tokens.astype(jnp.float32)
    average = jnp.mean(values, axis=-1, keepdims=True)
    centered = values - average
    variance = jnp.mean(centered * centered, axis=-1, keepdims=True)
    return (centered * lax.rsqrt(variance + epsilon) * norm_gain).astype(jnp.bfloat16)


def gelu_pair(preact):
    normal_cdf = 0.5 * (1.0 + jax.scipy.special.erf(preact * 0.7071067811865476))
    density = jnp.exp(-0.5 * preact * preact) * 0.3989422804014327
    return (preact * normal_cdf, normal_cdf + preact * density)


def shards(patches, keep_list, norm_gain, up_weight, hidden_grad):
    piece = lax.all_gather(patches, "mp", axis=2, tiled=True)
    piece = jnp.take_along_axis(piece, keep_list[:, :, None], axis=1)
    normed = normalize(piece, norm_gain)
    flat_normed = normed[0]
    preact = jnp.dot(flat_normed, up_weight, preferred_element_type=jnp.float32)
    activated, slope_full = gelu_pair(preact)
    slope_rows = (hidden_grad[0].astype(jnp.float32) * slope_full).astype(jnp.bfloat16)
    hidden_rows = activated.astype(jnp.bfloat16)
    weight_grad = lax.psum_scatter(
        lax.dot_general(
            flat_normed, slope_rows, (((0,), (0,)), ((), ())), preferred_element_type=jnp.float32
        ),
        "dp",
        scatter_dimension=0,
        tiled=True,
    )
    return (hidden_rows[None], weight_grad)


def solution(mesh):
    placed = (P("dp", None, "mp"), P("dp", None), P(), P(None, "mp"), P("dp", None, "mp"))
    return jax.shard_map(
        shards,
        mesh=mesh,
        in_specs=placed,
        out_specs=(P("dp", None, "mp"), P("dp", "mp")),
        check_vma=False,
    )
```

profile of v0, /device:TPU:1, one launch (start us, length us, event | category | flops | bytes accessed | tf_op | source)
XLA Modules:
  0.0 704.6 jit_solution(605754681301354936)
XLA Ops:
  7.2 0.0 copy-start
  7.2 0.0 all-gather.2.cloned.1.call-start
  7.2 0.7 all-gather.2.cloned.1.call-update
  7.9 0.0 reduce-scatter.2.cloned.1.call-start
  8.0 0.7 fusion.14
  8.6 0.7 compare_and_fusion
  9.3 518.1 %all-gather.2.cloned.1.call-done = bf16[1,192,6144]{1,2,0:T(8,128)(2,1)} async-done(((bf16[1,192,48]{1,2,0:T(8,128)(2,1)}), bf16[1,192,6144]{1,2,0:T(8,128)(2,1)}) %all-gather.2.cloned.1.call-update) | async-done | bytes 2359312 | tf_op jit(solution)/shard_map/all_gather | solution.py:24
  527.4 4.6 copy.8
  532.0 6.1 gather_fusion
  538.1 0.0 copy-start.1
  538.1 0.0 copy-start.3
  538.1 2.0 convert_reduce_fusion
  540.1 0.0 copy-done.1
  540.1 0.7 fusion.1
  540.8 0.0 copy-done
  540.8 0.0 copy-done.3
  540.8 0.0 copy-start.2
  540.8 1.0 fusion.17
  541.8 0.0 copy-done.2
  541.9 3.1 fusion.9
  544.9 0.0 reduce-scatter.2.cloned.1.call-update
  545.0 0.7 fusion.8
  545.6 152.1 %reduce-scatter.2.cloned.1.call-done = f32[768,192]{0,1:T(8,128)} async-done(((f32[6144,192]{0,1:T(8,128)}), f32[768,192]{0,1:T(8,128)}) %reduce-scatter.2.cloned.1.call-update) | async-done | bytes 589840 | tf_op jit(solution)/shard_map/reduce_scatter | solution.py:32
  (3 shorter events, 0.0 us)
Async XLA Ops:
  7.2 533.6 %copy-start = (bf16[6144,192]{0,1:T(8,128)(2,1)S(1)}, bf16[6144,192]{0,1:T(8,128)(2,1)}, u32[]{:S(2)}) copy-start(bf16[6144,192]{0,1:T(8,128)(2,1)} %param.8) | copy-start | bytes 7077892
  7.2 520.2 %all-gather.2.cloned.1.call-start = ((), (), s32[]{:S(2)}) async-start(), calls=%async_computation.1 | async-start | bytes 3170304 | tf_op jit(solution)/shard_map/all_gather | solution.py:24
  7.9 689.8 %reduce-scatter.2.cloned.1.call-start = ((), (), s32[]{:S(2)}) async-start(), calls=%async_computation.2 | async-start | bytes 5308416 | tf_op jit(solution)/shard_map/reduce_scatter | solution.py:32
  538.1 2.0 copy-start.1
  538.1 2.7 copy-start.3
  540.8 1.0 copy-start.2
Sparse Core Ops, SparseCore 0:
  10.7 516.6 all-gather.1
  545.1 152.5 reduce-scatter.1
where the time goes:
time: 705 us
  waiting for transfers between devices  671 us (95%)
  between operations  14.1 us (2%)
  local copies, waits for them, and re-layouts  10.7 us (2%)
    all_gather x1, waiting for transfers between devices, shards(): piece = lax.all_gather(patches, 'mp', axis=2, tiled=True)  518 us
    reduce_scatter x1, waiting for transfers between devices, shards(): lax.psum_scatter(lax.dot_general(flat_normed, slope_rows, (((0,), (0,)),...  152 us
  transfers between devices with their start and end apart: 2, of which 2 were waited for; matrix products, arithmetic and copies ran while one was open for 0% of the time, Pallas kernels for 0%

commit v1 on v0

v1 whole, which is shorter than its diff:
```python
import functools

import jax
import jax.numpy as jnp
from jax import lax
from jax.experimental import pallas as pl
from jax.experimental.pallas import tpu as pltpu
from jax.sharding import PartitionSpec as P


epsilon = 1e-06
D = 6144
KEEP = 128
BF = jnp.bfloat16
F32 = jnp.float32
AXES = ("dp", "mp")


def flat(x_hi, core, y, z, x_lo):
    return (x_hi * 2 + core) * 128 + (y % 8) * 16 + (z % 8) * 2 + x_lo


def everyone():
    for x_hi in range(4):
        for core in range(2):
            for y in range(8):
                for z in range(8):
                    for x_lo in range(2):
                        yield x_hi, core, y, z, x_lo


def ring_pairs(step):
    pairs = []
    for x_hi, core, y, z, x_lo in everyone():
        to = (y + step, z) if core == 0 else (y, z + step)
        pairs.append((flat(x_hi, core, y, z, x_lo), flat(x_hi, core, to[0], to[1], x_lo)))
    return pairs


def swap_pairs():
    return [
        (flat(x_hi, core, y, z, x_lo), flat(y // 2, y % 2, x_hi * 2 + core, z, x_lo))
        for x_hi, core, y, z, x_lo in everyone()
    ]


def first_groups():
    groups = []
    for x_hi in range(4):
        for core in range(2):
            for fixed in range(8):
                groups.append(
                    [
                        flat(x_hi, core, *((fixed, run) if core == 0 else (run, fixed)), x_lo)
                        for run in range(8)
                        for x_lo in range(2)
                    ]
                )
    return groups


def gelu_pair(preact):
    normal_cdf = 0.5 * (1.0 + lax.erf(preact * 0.7071067811865476))
    density = jnp.exp(-0.5 * preact * preact) * 0.3989422804014327
    return (preact * normal_cdf, normal_cdf + preact * density)


def tiles(where, pieces, part):
    me = where[1]
    for k, refs in enumerate(pieces):
        shift = (0, -1, -2, -3, 1, 2, 3, 4)[k]
        ring = lax.rem(me + (shift + 8), 8)
        for j in range(8):
            for half in range(2):
                if len(refs) == 1:
                    yield refs[0].at[2 * j + half, part], ring, j, half
                else:
                    yield refs[j // 4].at[2 * (j % 4) + half, part], ring, j, half


def forward_kernel(where, *refs):
    pieces = [refs[k : k + 1] for k in range(7)] + [refs[7:9]]
    weight, gain, hidden_grad, hidden, payload, rows = refs[9:]
    on_y = where[0] == 0
    total = jnp.zeros((8, KEEP), F32)
    for tile, ring, j, half in tiles(where, pieces, 0):
        value = tile[...]
        place = jnp.where(on_y, ring * 768 + j * 96, j * 768 + ring * 96) + half * 48
        rows[pl.ds(pl.multiple_of(place, 16), 48), :] = value
        total += jnp.sum(value.astype(F32).reshape(6, 8, KEEP), axis=0)
    average = jnp.sum(total, axis=0, keepdims=True) * (1.0 / D)
    total = jnp.zeros((8, KEEP), F32)
    for start in range(0, D, 256):
        centered = rows[start : start + 256, :].astype(F32) - average
        total += jnp.sum((centered * centered).reshape(32, 8, KEEP), axis=0)
    variance = jnp.sum(total, axis=0, keepdims=True) * (1.0 / D)
    scale = lax.rsqrt(variance + epsilon)
    preact = jnp.zeros((192, KEEP), F32)
    for start in range(0, D, 256):
        centered = rows[start : start + 256, :].astype(F32) - average
        normed = (centered * scale * gain[start : start + 256, :]).astype(BF)
        preact += jnp.dot(weight[:, start : start + 256], normed, preferred_element_type=F32)
    activated, slope_full = gelu_pair(preact)
    hidden[...] = activated.astype(BF)
    payload[0:192, :] = (hidden_grad[...].astype(F32) * slope_full).astype(BF)
    lines = []
    for value in (average, scale):
        for _ in range(3):
            top = value.astype(BF).astype(F32)
            lines.append(top)
            value = value - top
    lines.append(jnp.zeros((10, KEEP), F32))
    payload[192:208, :] = jnp.concatenate(lines, axis=0).astype(BF)


def grad_kernel(where, *refs):
    pieces = [refs[k : k + 1] for k in range(7)] + [refs[7:9]]
    payload, gain, out, normed, slopes, averages, scales = refs[9:]
    on_y = where[0] == 0
    for image in range(8):
        ref = payload.at[image % 2, image // 2]
        slopes[:, image * KEEP : (image + 1) * KEEP] = ref[0:192, :]
        lines = ref[192:208, :].astype(F32)
        averages[image : image + 1, :] = lines[0:1] + lines[1:2] + lines[2:3]
        scales[image : image + 1, :] = lines[3:4] + lines[4:5] + lines[5:6]
    for tile, ring, j, half in tiles(where, pieces, 1):
        image = jnp.where(on_y, ring, j)
        place = pl.multiple_of(jnp.where(on_y, j * 96, ring * 96) + half * 48, 16)
        centered = tile[...].astype(F32) - averages[pl.ds(image, 1), :]
        value = centered * scales[pl.ds(image, 1), :] * gain[pl.ds(place, 48), :]
        normed[pl.ds(place, 48), pl.ds(pl.multiple_of(image * KEEP, KEEP), KEEP)] = value.astype(BF)
    out[...] = lax.dot_general(
        slopes[...], normed[...], (((1,), (1,)), ((), ())), preferred_element_type=F32
    )


VMEM = pl.BlockSpec(memory_space=pltpu.VMEM)
SMEM = pl.BlockSpec(memory_space=pltpu.SMEM)


def shards(patches, keep_list, norm_gain, up_weight, hidden_grad):
    dp, mp = lax.axis_index("dp"), lax.axis_index("mp")
    core = dp % 2
    where = jnp.stack([core, jnp.where(core == 0, mp // 16, (mp // 2) % 8)]).astype(jnp.int32)
    gain_all = jnp.broadcast_to(norm_gain[:, None], (D, KEEP))
    gain_block = jnp.broadcast_to(lax.dynamic_slice(norm_gain, (dp * 768,), (768,))[:, None], (768, KEEP))

    picked = (lax.broadcasted_iota(jnp.int32, (192, KEEP), 0) == keep_list).astype(BF)
    own = jnp.dot(patches[0].T, picked, preferred_element_type=F32).astype(BF)
    other = lax.ppermute(own, AXES, swap_pairs())
    both = jnp.broadcast_to(jnp.stack([own, other])[None], (16, 2, 48, KEEP))
    both = lax.all_to_all(both, AXES, 0, 0, axis_index_groups=first_groups())
    ahead = functools.partial(lax.ppermute, axis_name=AXES, perm=ring_pairs(1))
    back = functools.partial(lax.ppermute, axis_name=AXES, perm=ring_pairs(-1))
    f1, b1 = ahead(both), back(both)
    f2, b2 = ahead(f1), back(b1)
    f3, b3 = ahead(f2), back(b2)
    f4, b4 = ahead(f3[:8]), back(b3[8:])
    pieces = (both, f1, f2, f3, b1, b2, b3, f4, b4)

    hidden, payload = pl.pallas_call(
        forward_kernel,
        out_shape=(jax.ShapeDtypeStruct((192, KEEP), BF), jax.ShapeDtypeStruct((208, KEEP), BF)),
        in_specs=[SMEM] + [VMEM] * 12,
        out_specs=(VMEM, VMEM),
        scratch_shapes=[pltpu.VMEM((D, KEEP), BF)],
        compiler_params=pltpu.CompilerParams(vmem_limit_bytes=24 * 2**20),
        name="forward",
    )(where, *pieces, up_weight.T, gain_all, hidden_grad[0].T)

    payload = lax.all_to_all(
        jnp.broadcast_to(payload[None], (4, 208, KEEP)), "dp", 0, 0, axis_index_groups=[[0, 2, 4, 6], [1, 3, 5, 7]]
    )
    payload = lax.all_gather(payload, "dp", axis_index_groups=[[0, 1], [2, 3], [4, 5], [6, 7]])

    grad = pl.pallas_call(
        grad_kernel,
        out_shape=jax.ShapeDtypeStruct((192, 768), F32),
        in_specs=[SMEM] + [VMEM] * 11,
        out_specs=VMEM,
        scratch_shapes=[
            pltpu.VMEM((768, 1024), BF),
            pltpu.VMEM((192, 1024), BF),
            pltpu.VMEM((8, KEEP), F32),
            pltpu.VMEM((8, KEEP), F32),
        ],
        compiler_params=pltpu.CompilerParams(vmem_limit_bytes=24 * 2**20),
        name="weight_grad",
    )(where, *pieces, payload, gain_block)
    return (hidden.T[None], grad.T)


def solution(mesh):
    placed = (P("dp", None, "mp"), P("dp", None), P(), P(None, "mp"), P("dp", None, "mp"))
    return jax.shard_map(
        shards,
        mesh=mesh,
        in_specs=placed,
        out_specs=(P("dp", None, "mp"), P("dp", "mp")),
        check_vma=False,
    )
```

time: 705 us -> 116 us (0.16)
  waiting for transfers between devices: 671 us -> 20.4 us
  starting transfers between devices: 0.08 us -> 47.8 us
  blocking collectives: 0 us -> 35.1 us
  between operations: 14.1 us -> 0.85 us
    all_gather x1 -> x0, waiting for transfers between devices: 518 us -> none  [shards(): piece = lax.all_gather(patches, 'mp', axis=2, tiled=True)]
    reduce_scatter x1 -> x0, waiting for transfers between devices: 152 us -> none  [shards(): lax.psum_scatter(lax.dot_general(flat_normed, slope_rows, (((0,), (0,)),...]
    ppermute x0 -> x9, starting transfers between devices: none -> 44.5 us  [the longest x2 19 us: shards(): f1, b1 = (ahead(both), back(both))]
    all_to_all x0 -> x1, blocking collectives: none -> 25.5 us  [shards(): both = lax.all_to_all(both, AXES, 0, 0, axis_index_groups=first_groups())]
    ppermute x0 -> x9, waiting for transfers between devices: none -> 13 us  [the longest x2 3.23 us: shards(): f1, b1 = (ahead(both), back(both))]
    all_gather x0 -> x1, blocking collectives: none -> 9.57 us  [shards(): lax.all_gather(payload, 'dp', axis_index_groups=[[0, 1], [2, 3], [4, 5],...]
    all_to_all x0 -> x1, waiting for transfers between devices: none -> 7.4 us  [shards(): lax.all_to_all(jnp.broadcast_to(payload[None], (4, 208, KEEP)), 'dp', 0,...]
  transfers between devices with their start and end apart: 2 -> 10, of which waited for: 2 -> 7; matrix products, arithmetic and copies ran while one was open for 0% -> 1% of each run, Pallas kernels for 0% -> 0%
where the time goes in v1:
time: 116 us
  starting transfers between devices  47.8 us (41%)
  blocking collectives  35.1 us (30%)
  waiting for transfers between devices  20.4 us (18%)
  Pallas kernels  5.67 us (5%)
  local copies, waits for them, and re-layouts  4.73 us (4%)
    all_to_all x1, blocking collectives, shards(): both = lax.all_to_all(both, AXES, 0, 0, axis_index_groups=first_groups())  25.5 us
    ppermute x2, starting transfers between devices, shards(): f1, b1 = (ahead(both), back(both))  19 us
    all_gather x1, blocking collectives, shards(): lax.all_gather(payload, 'dp', axis_index_groups=[[0, 1], [2, 3], [4, 5],...  9.57 us
    all_to_all x1, waiting for transfers between devices, shards(): lax.all_to_all(jnp.broadcast_to(payload[None], (4, 208, KEEP)), 'dp', 0,...  7.4 us
    ppermute x2, starting transfers between devices, shards(): f3, b3 = (ahead(f2), back(b2))  7.06 us
    ppermute x2, starting transfers between devices, shards(): f4, b4 = (ahead(f3[:8]), back(b3[8:]))  6.93 us
    ppermute x2, starting transfers between devices, shards(): f2, b2 = (ahead(f1), back(b1))  6.77 us
    ppermute x1, starting transfers between devices, shards(): other = lax.ppermute(own, AXES, swap_pairs())  4.7 us
  transfers between devices with their start and end apart: 10, of which 7 were waited for; matrix products, arithmetic and copies ran while one was open for 1% of the time, Pallas kernels for 0%

profile of v1, /device:TPU:1, one launch (start us, length us, event | category | flops | bytes accessed | tf_op | source)
XLA Modules:
  0.0 115.5 jit_solution(16530206013928242676)
XLA Ops:
  0.7 0.7 copy-done
  1.4 0.8 convolution_convert_fusion
  2.2 4.7 %collective-permute-start = (bf16[48,128]{1,0:T(8,128)(2,1)S(1)}, bf16[48,128]{1,0:T(8,128)(2,1)S(1)}, u32[]{:S(2)}, u32[]{:S(2)}) collective-permute-start(bf16[48,128]{1,0:T(8,128)(2,1)S(1)} %bitcast.23), channel_id=1, source_target_pairs={{0,0},{1,1},{2,2},{3,3},{4,4},{5,5},{6,6},{7,7},{8,8},{9,9},{10,10... | collective-permute-start | bytes 36872 | tf_op jit(solution)/shard_map/ppermute | solution.py:150
  6.9 1.4 %collective-permute-done = bf16[48,128]{1,0:T(8,128)(2,1)S(1)} collective-permute-done((bf16[48,128]{1,0:T(8,128)(2,1)S(1)}, bf16[48,128]{1,0:T(8,128)(2,1)S(1)}, u32[]{:S(2)}, u32[]{:S(2)}) %collective-permute-start) | collective-permute-done | bytes 12320 | tf_op jit(solution)/shard_map/ppermute | solution.py:150
  8.3 25.5 %all_to_all.10.refs_0_ = bf16[16,2,48,128]{3,2,1,0:T(8,128)(2,1)S(1)} all-to-all(bf16[16,2,48,128]{3,2,1,0:T(8,128)(2,1)S(1)} %broadcast_in_dim.10), channel_id=1, replica_groups={{0,1,2,3,4,5,6,7,8,9,10,11,12,13,14,15},{16,17,18,19,20,21,22,23,24,25,..., dimensions={0} | all-to-all | bytes 786432 | tf_op jit(solution)/shard_map/all_to_all | solution.py:152
  33.8 4.9 %collective-permute-start.1 = (bf16[16,2,48,128]{3,2,1,0:T(8,128)(2,1)S(1)}, bf16[16,2,48,128]{3,2,1,0:T(8,128)(2,1)S(1)}, u32[]{:S(2)}, u32[]{:S(2)}) collective-permute-start(bf16[16,2,48,128]{3,2,1,0:T(8,128)(2,1)S(1)} %all_to_all.10.refs_0_), channel_id=1, source_target_pairs={{0,16},{1,17},{2,18},{3,19},{4,20},{5,21},{6,22},{7,23},{8,24},{9,... | collective-permute-start | bytes 1179656 | tf_op jit(solution)/shard_map/ppermute | solution.py:155
  38.7 14.1 %collective-permute-start.4 = (bf16[16,2,48,128]{3,2,1,0:T(8,128)(2,1)S(1)}, bf16[16,2,48,128]{3,2,1,0:T(8,128)(2,1)S(1)}, u32[]{:S(2)}, u32[]{:S(2)}) collective-permute-start(bf16[16,2,48,128]{3,2,1,0:T(8,128)(2,1)S(1)} %all_to_all.10.refs_0_), channel_id=1, source_target_pairs={{0,112},{1,113},{2,114},{3,115},{4,116},{5,117},{6,118},{7,119},{8... | collective-permute-start | bytes 1179656 | tf_op jit(solution)/shard_map/ppermute | solution.py:155
  52.9 3.2 %collective-permute-done.1.refs_1_ = bf16[16,2,48,128]{3,2,1,0:T(8,128)(2,1)S(1)} collective-permute-done((bf16[16,2,48,128]{3,2,1,0:T(8,128)(2,1)S(1)}, bf16[16,2,48,128]{3,2,1,0:T(8,128)(2,1)S(1)}, u32[]{:S(2)}, u32[]{:S(2)}) %collective-permute-start.1) | collective-permute-done | bytes 393248 | tf_op jit(solution)/shard_map/ppermute | solution.py:155
  56.1 1.9 %collective-permute-start.2 = (bf16[16,2,48,128]{3,2,1,0:T(8,128)(2,1)S(1)}, bf16[16,2,48,128]{3,2,1,0:T(8,128)(2,1)S(1)}, u32[]{:S(2)}, u32[]{:S(2)}) collective-permute-start(bf16[16,2,48,128]{3,2,1,0:T(8,128)(2,1)S(1)} %collective-permute-done.1.refs_1_), channel_id=1, source_target_pairs={{0,16},{1,17},{2,18},{3,19},{4,20},{5,21},{6,22},{7,23},{8,24},{9,... | collective-permute-start | bytes 1179656 | tf_op jit(solution)/shard_map/ppermute | solution.py:156
  58.0 4.9 %collective-permute-start.5 = (bf16[16,2,48,128]{3,2,1,0:T(8,128)(2,1)S(1)}, bf16[16,2,48,128]{3,2,1,0:T(8,128)(2,1)S(1)}, u32[]{:S(2)}, u32[]{:S(2)}) collective-permute-start(bf16[16,2,48,128]{3,2,1,0:T(8,128)(2,1)S(1)} %collective-permute-done.4.refs_4_), channel_id=1, source_target_pairs={{0,112},{1,113},{2,114},{3,115},{4,116},{5,117},{6,118},{7,119},{8... | collective-permute-start | bytes 1179656 | tf_op jit(solution)/shard_map/ppermute | solution.py:156
  62.9 2.9 %collective-permute-done.2.refs_2_ = bf16[16,2,48,128]{3,2,1,0:T(8,128)(2,1)S(1)} collective-permute-done((bf16[16,2,48,128]{3,2,1,0:T(8,128)(2,1)S(1)}, bf16[16,2,48,128]{3,2,1,0:T(8,128)(2,1)S(1)}, u32[]{:S(2)}, u32[]{:S(2)}) %collective-permute-start.2) | collective-permute-done | bytes 393248 | tf_op jit(solution)/shard_map/ppermute | solution.py:156
  65.8 1.9 %collective-permute-start.3 = (bf16[16,2,48,128]{3,2,1,0:T(8,128)(2,1)S(1)}, bf16[16,2,48,128]{3,2,1,0:T(8,128)(2,1)S(1)}, u32[]{:S(2)}, u32[]{:S(2)}) collective-permute-start(bf16[16,2,48,128]{3,2,1,0:T(8,128)(2,1)S(1)} %collective-permute-done.2.refs_2_), channel_id=1, source_target_pairs={{0,16},{1,17},{2,18},{3,19},{4,20},{5,21},{6,22},{7,23},{8,24},{9,... | collective-permute-start | bytes 1179656 | tf_op jit(solution)/shard_map/ppermute | solution.py:157
  67.7 5.2 %collective-permute-start.6 = (bf16[16,2,48,128]{3,2,1,0:T(8,128)(2,1)S(1)}, bf16[16,2,48,128]{3,2,1,0:T(8,128)(2,1)S(1)}, u32[]{:S(2)}, u32[]{:S(2)}) collective-permute-start(bf16[16,2,48,128]{3,2,1,0:T(8,128)(2,1)S(1)} %collective-permute-done.5.refs_5_), channel_id=1, source_target_pairs={{0,112},{1,113},{2,114},{3,115},{4,116},{5,117},{6,118},{7,119},{8... | collective-permute-start | bytes 1179656 | tf_op jit(solution)/shard_map/ppermute | solution.py:157
  72.9 2.6 %collective-permute-done.3.refs_3_ = bf16[16,2,48,128]{3,2,1,0:T(8,128)(2,1)S(1)} collective-permute-done((bf16[16,2,48,128]{3,2,1,0:T(8,128)(2,1)S(1)}, bf16[16,2,48,128]{3,2,1,0:T(8,128)(2,1)S(1)}, u32[]{:S(2)}, u32[]{:S(2)}) %collective-permute-start.3) | collective-permute-done | bytes 393248 | tf_op jit(solution)/shard_map/ppermute | solution.py:157
  75.5 1.9 %collective-permute-start.7 = (bf16[8,2,48,128]{3,2,1,0:T(8,128)(2,1)S(1)}, bf16[8,2,48,128]{3,2,1,0:T(8,128)(2,1)S(1)}, u32[]{:S(2)}, u32[]{:S(2)}) collective-permute-start(bf16[8,2,48,128]{3,2,1,0:T(8,128)(2,1)S(1)} %slice.8), channel_id=1, source_target_pairs={{0,16},{1,17},{2,18},{3,19},{4,20},{5,21},{6,22},{7,23},{8,24},{9,... | collective-permute-start | bytes 589832 | tf_op jit(solution)/shard_map/ppermute | solution.py:158
  78.3 5.0 %collective-permute-start.8 = (bf16[8,2,48,128]{3,2,1,0:T(8,128)(2,1)}, bf16[8,2,48,128]{3,2,1,0:T(8,128)(2,1)S(1)}, u32[]{:S(2)}, u32[]{:S(2)}) collective-permute-start(bf16[8,2,48,128]{3,2,1,0:T(8,128)(2,1)} %slice.9), channel_id=1, source_target_pairs={{0,112},{1,113},{2,114},{3,115},{4,116},{5,117},{6,118},{7,119},{8... | collective-permute-start | bytes 589832 | tf_op jit(solution)/shard_map/ppermute | solution.py:158
  83.5 2.7 %collective-permute-done.8.refs_8_ = bf16[8,2,48,128]{3,2,1,0:T(8,128)(2,1)S(1)} collective-permute-done((bf16[8,2,48,128]{3,2,1,0:T(8,128)(2,1)}, bf16[8,2,48,128]{3,2,1,0:T(8,128)(2,1)S(1)}, u32[]{:S(2)}, u32[]{:S(2)}) %collective-permute-start.8) | collective-permute-done | bytes 196640 | tf_op jit(solution)/shard_map/ppermute | solution.py:158
  86.2 1.6 %broadcast_in_dim.11.refs_10_ = f32[6144,128]{1,0:T(8,128)S(1)} broadcast(f32[6144]{0:T(1024)} %param.7), dimensions={0} | broadcast | bytes 3170304 | tf_op jit(solution)/shard_map/broadcast_in_dim | solution.py:145
  87.8 3.0 %forward.1 = (bf16[192,128]{1,0:T(8,128)(2,1)}, bf16[208,128]{1,0:T(8,128)(2,1)S(1)}) custom-call(s32[2]{0:T(128)S(1)} %pad_add_fusion.where, bf16[16,2,48,128]{3,2,1,0:T(8,128)(2,1)S(1)} %all_to_all.10.refs_0_, bf16[16,2,48,128]{3,2,1,0:T(8,128)(2,1)S(1)} %collective-permute-done.1.refs_1_, bf16[16,2,48,128]{3,2,1,0:T(8,128)(2,1)S(1)} %collective-permute-done.2.refs_2_, ...), custom_call_target="tpu_custom_call" | custom-call | tf_op jit(solution)/shard_map/forward/pallas_call | solution.py:161
  91.6 3.4 %all-to-all-start.1 = ((bf16[4,208,128]{2,1,0:T(8,128)(2,1)}), bf16[4,208,128]{2,1,0:T(8,128)(2,1)S(1)}, u32[]{:S(2)}, u32[]{:S(2)}) async-start(bf16[4,208,128]{2,1,0:T(8,128)(2,1)} %broadcast_in_dim.13), calls=%async_computation.1 | async-start | bytes 425984 | tf_op jit(solution)/shard_map/all_to_all | solution.py:171
  94.9 0.8 dynamic_slice.3
  95.7 7.4 %all-to-all-done.1 = bf16[4,208,128]{2,1,0:T(8,128)(2,1)S(1)} async-done(((bf16[4,208,128]{2,1,0:T(8,128)(2,1)}), bf16[4,208,128]{2,1,0:T(8,128)(2,1)S(1)}, u32[]{:S(2)}, u32[]{:S(2)}) %all-to-all-start.1) | async-done | bytes 213024 | tf_op jit(solution)/shard_map/all_to_all | solution.py:171
  103.1 9.6 %all-gather = bf16[8,208,128]{2,1,0:T(8,128)(2,1)S(1)} all-gather(bf16[4,208,128]{2,1,0:T(8,128)(2,1)S(1)} %all-to-all-done.1), channel_id=2, replica_groups={{0,128},{256,384},{512,640},{768,896},{1,129},{257,385},{513,641},{769,..., dimensions={0}, use_global_device_ids=true | all-gather | bytes 638976 | tf_op jit(solution)/shard_map/all_gather | solution.py:174
  112.9 2.7 %weight_grad.1 = f32[192,768]{1,0:T(8,128)} custom-call(s32[2]{0:T(128)S(1)} %pad_add_fusion.where, bf16[16,2,48,128]{3,2,1,0:T(8,128)(2,1)S(1)} %all_to_all.10.refs_0_, bf16[16,2,48,128]{3,2,1,0:T(8,128)(2,1)S(1)} %collective-permute-done.1.refs_1_, bf16[16,2,48,128]{3,2,1,0:T(8,128)(2,1)S(1)} %collective-permute-done.2.refs_2_, ...), custom_call_target="tpu_custom_call" | custom-call | tf_op jit(solution)/shard_map/weight_grad/pallas_call | solution.py:176
  (16 shorter events, 1.9 us)
Async XLA Ops:
  0.6 0.7 copy-start
  0.6 87.2 %copy-start.2 = (bf16[1,128,192]{1,2,0:T(8,128)(2,1)S(1)}, bf16[1,128,192]{1,2,0:T(8,128)(2,1)}, u32[]{:S(2)}) copy-start(bf16[1,128,192]{1,2,0:T(8,128)(2,1)} %param.9) | copy-start | bytes 147460
  2.2 6.1 %collective-permute-start = (bf16[48,128]{1,0:T(8,128)(2,1)S(1)}, bf16[48,128]{1,0:T(8,128)(2,1)S(1)}, u32[]{:S(2)}, u32[]{:S(2)}) collective-permute-start(bf16[48,128]{1,0:T(8,128)(2,1)S(1)} %bitcast.23), channel_id=1, source_target_pairs={{0,0},{1,1},{2,2},{3,3},{4,4},{5,5},{6,6},{7,7},{8,8},{9,9},{10,10... | collective-permute-start | bytes 36872 | tf_op jit(solution)/shard_map/ppermute | solution.py:150
  33.8 22.2 %collective-permute-start.1 = (bf16[16,2,48,128]{3,2,1,0:T(8,128)(2,1)S(1)}, bf16[16,2,48,128]{3,2,1,0:T(8,128)(2,1)S(1)}, u32[]{:S(2)}, u32[]{:S(2)}) collective-permute-start(bf16[16,2,48,128]{3,2,1,0:T(8,128)(2,1)S(1)} %all_to_all.10.refs_0_), channel_id=1, source_target_pairs={{0,16},{1,17},{2,18},{3,19},{4,20},{5,21},{6,22},{7,23},{8,24},{9,... | collective-permute-start | bytes 1179656 | tf_op jit(solution)/shard_map/ppermute | solution.py:155
  38.7 19.3 %collective-permute-start.4 = (bf16[16,2,48,128]{3,2,1,0:T(8,128)(2,1)S(1)}, bf16[16,2,48,128]{3,2,1,0:T(8,128)(2,1)S(1)}, u32[]{:S(2)}, u32[]{:S(2)}) collective-permute-start(bf16[16,2,48,128]{3,2,1,0:T(8,128)(2,1)S(1)} %all_to_all.10.refs_0_), channel_id=1, source_target_pairs={{0,112},{1,113},{2,114},{3,115},{4,116},{5,117},{6,118},{7,119},{8... | collective-permute-start | bytes 1179656 | tf_op jit(solution)/shard_map/ppermute | solution.py:155
  56.1 9.7 %collective-permute-start.2 = (bf16[16,2,48,128]{3,2,1,0:T(8,128)(2,1)S(1)}, bf16[16,2,48,128]{3,2,1,0:T(8,128)(2,1)S(1)}, u32[]{:S(2)}, u32[]{:S(2)}) collective-permute-start(bf16[16,2,48,128]{3,2,1,0:T(8,128)(2,1)S(1)} %collective-permute-done.1.refs_1_), channel_id=1, source_target_pairs={{0,16},{1,17},{2,18},{3,19},{4,20},{5,21},{6,22},{7,23},{8,24},{9,... | collective-permute-start | bytes 1179656 | tf_op jit(solution)/shard_map/ppermute | solution.py:156
  58.0 9.7 %collective-permute-start.5 = (bf16[16,2,48,128]{3,2,1,0:T(8,128)(2,1)S(1)}, bf16[16,2,48,128]{3,2,1,0:T(8,128)(2,1)S(1)}, u32[]{:S(2)}, u32[]{:S(2)}) collective-permute-start(bf16[16,2,48,128]{3,2,1,0:T(8,128)(2,1)S(1)} %collective-permute-done.4.refs_4_), channel_id=1, source_target_pairs={{0,112},{1,113},{2,114},{3,115},{4,116},{5,117},{6,118},{7,119},{8... | collective-permute-start | bytes 1179656 | tf_op jit(solution)/shard_map/ppermute | solution.py:156
  65.8 9.7 %collective-permute-start.3 = (bf16[16,2,48,128]{3,2,1,0:T(8,128)(2,1)S(1)}, bf16[16,2,48,128]{3,2,1,0:T(8,128)(2,1)S(1)}, u32[]{:S(2)}, u32[]{:S(2)}) collective-permute-start(bf16[16,2,48,128]{3,2,1,0:T(8,128)(2,1)S(1)} %collective-permute-done.2.refs_2_), channel_id=1, source_target_pairs={{0,16},{1,17},{2,18},{3,19},{4,20},{5,21},{6,22},{7,23},{8,24},{9,... | collective-permute-start | bytes 1179656 | tf_op jit(solution)/shard_map/ppermute | solution.py:157
  67.7 9.9 %collective-permute-start.6 = (bf16[16,2,48,128]{3,2,1,0:T(8,128)(2,1)S(1)}, bf16[16,2,48,128]{3,2,1,0:T(8,128)(2,1)S(1)}, u32[]{:S(2)}, u32[]{:S(2)}) collective-permute-start(bf16[16,2,48,128]{3,2,1,0:T(8,128)(2,1)S(1)} %collective-permute-done.5.refs_5_), channel_id=1, source_target_pairs={{0,112},{1,113},{2,114},{3,115},{4,116},{5,117},{6,118},{7,119},{8... | collective-permute-start | bytes 1179656 | tf_op jit(solution)/shard_map/ppermute | solution.py:157
  75.5 7.9 %collective-permute-start.7 = (bf16[8,2,48,128]{3,2,1,0:T(8,128)(2,1)S(1)}, bf16[8,2,48,128]{3,2,1,0:T(8,128)(2,1)S(1)}, u32[]{:S(2)}, u32[]{:S(2)}) collective-permute-start(bf16[8,2,48,128]{3,2,1,0:T(8,128)(2,1)S(1)} %slice.8), channel_id=1, source_target_pairs={{0,16},{1,17},{2,18},{3,19},{4,20},{5,21},{6,22},{7,23},{8,24},{9,... | collective-permute-start | bytes 589832 | tf_op jit(solution)/shard_map/ppermute | solution.py:158
  78.3 7.9 %collective-permute-start.8 = (bf16[8,2,48,128]{3,2,1,0:T(8,128)(2,1)}, bf16[8,2,48,128]{3,2,1,0:T(8,128)(2,1)S(1)}, u32[]{:S(2)}, u32[]{:S(2)}) collective-permute-start(bf16[8,2,48,128]{3,2,1,0:T(8,128)(2,1)} %slice.9), channel_id=1, source_target_pairs={{0,112},{1,113},{2,114},{3,115},{4,116},{5,117},{6,118},{7,119},{8... | collective-permute-start | bytes 589832 | tf_op jit(solution)/shard_map/ppermute | solution.py:158
  83.3 4.5 %copy-start.1 = (bf16[6144,192]{0,1:T(8,128)(2,1)S(1)}, bf16[6144,192]{0,1:T(8,128)(2,1)}, u32[]{:S(2)}) copy-start(bf16[6144,192]{0,1:T(8,128)(2,1)} %param.8) | copy-start | bytes 7077892
  91.6 11.6 %all-to-all-start.1 = ((bf16[4,208,128]{2,1,0:T(8,128)(2,1)}), bf16[4,208,128]{2,1,0:T(8,128)(2,1)S(1)}, u32[]{:S(2)}, u32[]{:S(2)}) async-start(bf16[4,208,128]{2,1,0:T(8,128)(2,1)} %broadcast_in_dim.13), calls=%async_computation.1 | async-start | bytes 425984 | tf_op jit(solution)/shard_map/all_to_all | solution.py:171

commit v2 on v1

--- a/solution.py
+++ b/solution.py
@@ -40,6 +40,28 @@
 def swap_pairs():
     return [
         (flat(x_hi, core, y, z, x_lo), flat(y // 2, y % 2, x_hi * 2 + core, z, x_lo))
+        for x_hi, core, y, z, x_lo in everyone()
+    ]
+
+
+def ring_groups():
+    groups = []
+    for x_hi in range(4):
+        for core in range(2):
+            for fixed in range(8):
+                for x_lo in range(2):
+                    groups.append(
+                        [
+                            flat(x_hi, core, *((run, fixed) if core == 0 else (fixed, run)), x_lo)
+                            for run in range(8)
+                        ]
+                    )
+    return groups
+
+
+def x_pairs(step):
+    return [
+        (flat(x_hi, core, y, z, x_lo), flat((x_hi + step) % 4, core, y, z, x_lo))
         for x_hi, core, y, z, x_lo in everyone()
     ]
 
@@ -65,17 +87,14 @@
     return (preact * normal_cdf, normal_cdf + preact * density)
 
 
-def tiles(where, pieces, part):
-    me = where[1]
+def tiles(me, pieces):
     for k, refs in enumerate(pieces):
         shift = (0, -1, -2, -3, 1, 2, 3, 4)[k]
         ring = lax.rem(me + (shift + 8), 8)
         for j in range(8):
             for half in range(2):
-                if len(refs) == 1:
-                    yield refs[0].at[2 * j + half, part], ring, j, half
-                else:
-                    yield refs[j // 4].at[2 * (j % 4) + half, part], ring, j, half
+                ref, row = (refs[0], j) if len(refs) == 1 else (refs[j // 4], j % 4)
+                yield ref.at[2 * row + half], ring, j, half
 
 
 def forward_kernel(where, *refs):
@@ -83,7 +102,7 @@
     weight, gain, hidden_grad, hidden, payload, rows = refs[9:]
     on_y = where[0] == 0
     total = jnp.zeros((8, KEEP), F32)
-    for tile, ring, j, half in tiles(where, pieces, 0):
+    for tile, ring, j, half in tiles(where[1], pieces):
         value = tile[...]
         place = jnp.where(on_y, ring * 768 + j * 96, j * 768 + ring * 96) + half * 48
         rows[pl.ds(pl.multiple_of(place, 16), 48), :] = value
@@ -113,20 +132,18 @@
     payload[192:208, :] = jnp.concatenate(lines, axis=0).astype(BF)
 
 
-def grad_kernel(where, *refs):
-    pieces = [refs[k : k + 1] for k in range(7)] + [refs[7:9]]
-    payload, gain, out, normed, slopes, averages, scales = refs[9:]
+def grad_kernel(where, blocks, payload, gain, out, normed, slopes, averages, scales):
     on_y = where[0] == 0
     for image in range(8):
-        ref = payload.at[image % 2, image // 2]
+        ref = payload.at[image % 2, lax.rem(where[2] + (4 - image // 2), 4)]
         slopes[:, image * KEEP : (image + 1) * KEEP] = ref[0:192, :]
         lines = ref[192:208, :].astype(F32)
         averages[image : image + 1, :] = lines[0:1] + lines[1:2] + lines[2:3]
         scales[image : image + 1, :] = lines[3:4] + lines[4:5] + lines[5:6]
-    for tile, ring, j, half in tiles(where, pieces, 1):
+    for ring, j, half in ((ring, j, half) for ring in range(8) for j in range(8) for half in range(2)):
         image = jnp.where(on_y, ring, j)
         place = pl.multiple_of(jnp.where(on_y, j * 96, ring * 96) + half * 48, 16)
-        centered = tile[...].astype(F32) - averages[pl.ds(image, 1), :]
+        centered = blocks[ring, 2 * j + half].astype(F32) - averages[pl.ds(image, 1), :]
         value = centered * scales[pl.ds(image, 1), :] * gain[pl.ds(place, 48), :]
         normed[pl.ds(place, 48), pl.ds(pl.multiple_of(image * KEEP, KEEP), KEEP)] = value.astype(BF)
     out[...] = lax.dot_general(
@@ -141,7 +158,7 @@
 def shards(patches, keep_list, norm_gain, up_weight, hidden_grad):
     dp, mp = lax.axis_index("dp"), lax.axis_index("mp")
     core = dp % 2
-    where = jnp.stack([core, jnp.where(core == 0, mp // 16, (mp // 2) % 8)]).astype(jnp.int32)
+    where = jnp.stack([core, jnp.where(core == 0, mp // 16, (mp // 2) % 8), dp // 2]).astype(jnp.int32)
     gain_all = jnp.broadcast_to(norm_gain[:, None], (D, KEEP))
     gain_block = jnp.broadcast_to(lax.dynamic_slice(norm_gain, (dp * 768,), (768,))[:, None], (768, KEEP))
 
@@ -152,11 +169,13 @@
     both = lax.all_to_all(both, AXES, 0, 0, axis_index_groups=first_groups())
     ahead = functools.partial(lax.ppermute, axis_name=AXES, perm=ring_pairs(1))
     back = functools.partial(lax.ppermute, axis_name=AXES, perm=ring_pairs(-1))
-    f1, b1 = ahead(both), back(both)
+    blocks = lax.all_gather(both[:, 1], AXES, axis_index_groups=ring_groups())
+    own = both[:, 0]
+    f1, b1 = ahead(own), back(own)
     f2, b2 = ahead(f1), back(b1)
     f3, b3 = ahead(f2), back(b2)
     f4, b4 = ahead(f3[:8]), back(b3[8:])
-    pieces = (both, f1, f2, f3, b1, b2, b3, f4, b4)
+    pieces = (own, f1, f2, f3, b1, b2, b3, f4, b4)
 
     hidden, payload = pl.pallas_call(
         forward_kernel,
@@ -168,15 +187,13 @@
         name="forward",
     )(where, *pieces, up_weight.T, gain_all, hidden_grad[0].T)
 
-    payload = lax.all_to_all(
-        jnp.broadcast_to(payload[None], (4, 208, KEEP)), "dp", 0, 0, axis_index_groups=[[0, 2, 4, 6], [1, 3, 5, 7]]
-    )
+    payload = jnp.stack([payload] + [lax.ppermute(payload, AXES, x_pairs(step)) for step in (1, 2, 3)])
     payload = lax.all_gather(payload, "dp", axis_index_groups=[[0, 1], [2, 3], [4, 5], [6, 7]])
 
     grad = pl.pallas_call(
         grad_kernel,
         out_shape=jax.ShapeDtypeStruct((192, 768), F32),
-        in_specs=[SMEM] + [VMEM] * 11,
+        in_specs=[SMEM] + [VMEM] * 3,
         out_specs=VMEM,
         scratch_shapes=[
             pltpu.VMEM((768, 1024), BF),
@@ -186,7 +203,7 @@
         ],
         compiler_params=pltpu.CompilerParams(vmem_limit_bytes=24 * 2**20),
         name="weight_grad",
-    )(where, *pieces, payload, gain_block)
+    )(where, blocks, payload, gain_block)
     return (hidden.T[None], grad.T)
 
 

time: 116 us -> 128 us (1.10); the launches traced: 116 us -> 126 us
  between operations: 0.85 us -> 14.3 us
  waiting for transfers between devices: 20.4 us -> 10.9 us
  starting transfers between devices: 47.8 us -> 54.9 us
    ppermute x2 -> x5, starting transfers between devices: 19 us -> 29 us  [the longest x2 19.1 us: shards(): f1, b1 = (ahead(own), back(own))]
    all_to_all x1 -> x0, waiting for transfers between devices: 7.4 us -> none  [shards(): lax.all_to_all(jnp.broadcast_to(payload[None], (4, 208, KEEP)), 'dp', 0,...]
    all_to_all x1 -> x0, starting transfers between devices: 3.38 us -> none  [shards(): lax.all_to_all(jnp.broadcast_to(payload[None], (4, 208, KEEP)), 'dp', 0,...]
    ppermute x2, waiting for transfers between devices: 2.93 us -> 1 us  [shards(): f2, b2 = (ahead(f1), back(b1))]
    unnamed x6 -> x10, local copies, waits for them, and re-layouts: 0.74 us -> 2.1 us
    ppermute x2 -> x5, waiting for transfers between devices: 3.23 us -> 4.12 us  [the longest x3 3 us: shards(): lax.ppermute(payload, AXES, x_pairs(step))]
  transfers between devices with their start and end apart: 10 -> 13, of which waited for: 7 -> 8; matrix products, arithmetic and copies ran while one was open for 1% -> 1% of each run, Pallas kernels for 0% -> 3%
where the time goes in v2:
time: 128 us; the launch traced here: 126 us
  starting transfers between devices  54.9 us (43%)
  blocking collectives  35 us (27%)
  between operations  14.3 us (11%)
  waiting for transfers between devices  10.9 us (9%)
  Pallas kernels  6.24 us (5%)
  local copies, waits for them, and re-layouts  3.98 us (3%)
    all_to_all x1, blocking collectives, shards(): both = lax.all_to_all(both, AXES, 0, 0, axis_index_groups=first_groups())  25.5 us
    ppermute x2, starting transfers between devices, shards(): f1, b1 = (ahead(own), back(own))  19.1 us
    ppermute x3, starting transfers between devices, shards(): lax.ppermute(payload, AXES, x_pairs(step))  9.95 us
    all_gather x1, blocking collectives, shards(): lax.all_gather(payload, 'dp', axis_index_groups=[[0, 1], [2, 3], [4, 5],...  9.51 us
    ppermute x2, starting transfers between devices, shards(): f4, b4 = (ahead(f3[:8]), back(b3[8:]))  7.24 us
    ppermute x2, starting transfers between devices, shards(): f3, b3 = (ahead(f2), back(b2))  6.96 us
    ppermute x2, starting transfers between devices, shards(): f2, b2 = (ahead(f1), back(b1))  6.87 us
    ppermute x1, starting transfers between devices, shards(): other = lax.ppermute(own, AXES, swap_pairs())  4.7 us
  transfers between devices with their start and end apart: 13, of which 8 were waited for; matrix products, arithmetic and copies ran while one was open for 1% of the time, Pallas kernels for 3%

profile of v2, /device:TPU:1, one launch (start us, length us, event | category | flops | bytes accessed | tf_op | source)
XLA Modules:
  0.0 126.2 jit_solution(212774699497560669)
XLA Ops:
  8.7 4.7 %collective-permute-start = (bf16[48,128]{1,0:T(8,128)(2,1)S(1)}, bf16[48,128]{1,0:T(8,128)(2,1)S(1)}, u32[]{:S(2)}, u32[]{:S(2)}) collective-permute-start(bf16[48,128]{1,0:T(8,128)(2,1)S(1)} %bitcast.38), channel_id=1, source_target_pairs={{0,0},{1,1},{2,2},{3,3},{4,4},{5,5},{6,6},{7,7},{8,8},{9,9},{10,10... | collective-permute-start | bytes 36872 | tf_op jit(solution)/shard_map/ppermute | solution.py:167
  13.4 1.4 %collective-permute-done = bf16[48,128]{1,0:T(8,128)(2,1)S(1)} collective-permute-done((bf16[48,128]{1,0:T(8,128)(2,1)S(1)}, bf16[48,128]{1,0:T(8,128)(2,1)S(1)}, u32[]{:S(2)}, u32[]{:S(2)}) %collective-permute-start) | collective-permute-done | bytes 12320 | tf_op jit(solution)/shard_map/ppermute | solution.py:167
  14.8 25.5 %all_to_all.5 = bf16[16,2,48,128]{3,2,1,0:T(8,128)(2,1)S(1)} all-to-all(bf16[16,2,48,128]{3,2,1,0:T(8,128)(2,1)S(1)} %broadcast_in_dim.8), channel_id=1, replica_groups={{0,1,2,3,4,5,6,7,8,9,10,11,12,13,14,15},{16,17,18,19,20,21,22,23,24,25,..., dimensions={0} | all-to-all | bytes 786432 | tf_op jit(solution)/shard_map/all_to_all | solution.py:169
  41.1 5.0 %collective-permute-start.1 = (bf16[16,48,128]{2,1,0:T(8,128)(2,1)S(1)}, bf16[16,48,128]{2,1,0:T(8,128)(2,1)S(1)}, u32[]{:S(2)}, u32[]{:S(2)}) collective-permute-start(bf16[16,48,128]{2,1,0:T(8,128)(2,1)S(1)} %get-tuple-element.7.refs_0_), channel_id=1, source_target_pairs={{0,16},{1,17},{2,18},{3,19},{4,20},{5,21},{6,22},{7,23},{8,24},{9,... | collective-permute-start | bytes 589832 | tf_op jit(solution)/shard_map/ppermute | solution.py:174
  46.2 14.0 %collective-permute-start.4 = (bf16[16,48,128]{2,1,0:T(8,128)(2,1)S(1)}, bf16[16,48,128]{2,1,0:T(8,128)(2,1)S(1)}, u32[]{:S(2)}, u32[]{:S(2)}) collective-permute-start(bf16[16,48,128]{2,1,0:T(8,128)(2,1)S(1)} %get-tuple-element.7.refs_0_), channel_id=1, source_target_pairs={{0,112},{1,113},{2,114},{3,115},{4,116},{5,117},{6,118},{7,119},{8... | collective-permute-start | bytes 589832 | tf_op jit(solution)/shard_map/ppermute | solution.py:174
  60.2 1.1 collective-permute-done.1.refs_1_
  61.3 1.9 %collective-permute-start.2 = (bf16[16,48,128]{2,1,0:T(8,128)(2,1)S(1)}, bf16[16,48,128]{2,1,0:T(8,128)(2,1)}, u32[]{:S(2)}, u32[]{:S(2)}) collective-permute-start(bf16[16,48,128]{2,1,0:T(8,128)(2,1)S(1)} %collective-permute-done.1.refs_1_), channel_id=1, source_target_pairs={{0,16},{1,17},{2,18},{3,19},{4,20},{5,21},{6,22},{7,23},{8,24},{9,... | collective-permute-start | bytes 589832 | tf_op jit(solution)/shard_map/ppermute | solution.py:175
  63.2 5.0 %collective-permute-start.5 = (bf16[16,48,128]{2,1,0:T(8,128)(2,1)S(1)}, bf16[16,48,128]{2,1,0:T(8,128)(2,1)}, u32[]{:S(2)}, u32[]{:S(2)}) collective-permute-start(bf16[16,48,128]{2,1,0:T(8,128)(2,1)S(1)} %collective-permute-done.4.refs_4_), channel_id=1, source_target_pairs={{0,112},{1,113},{2,114},{3,115},{4,116},{5,117},{6,118},{7,119},{8... | collective-permute-start | bytes 589832 | tf_op jit(solution)/shard_map/ppermute | solution.py:175
  68.2 1.0 collective-permute-done.2.refs_2_
  69.2 1.9 %collective-permute-start.3 = (bf16[16,48,128]{2,1,0:T(8,128)(2,1)}, bf16[16,48,128]{2,1,0:T(8,128)(2,1)S(1)}, u32[]{:S(2)}, u32[]{:S(2)}) collective-permute-start(bf16[16,48,128]{2,1,0:T(8,128)(2,1)} %collective-permute-done.2.refs_2_), channel_id=1, source_target_pairs={{0,16},{1,17},{2,18},{3,19},{4,20},{5,21},{6,22},{7,23},{8,24},{9,... | collective-permute-start | bytes 589832 | tf_op jit(solution)/shard_map/ppermute | solution.py:176
  71.1 5.1 %collective-permute-start.6 = (bf16[16,48,128]{2,1,0:T(8,128)(2,1)}, bf16[16,48,128]{2,1,0:T(8,128)(2,1)S(1)}, u32[]{:S(2)}, u32[]{:S(2)}) collective-permute-start(bf16[16,48,128]{2,1,0:T(8,128)(2,1)} %collective-permute-done.5.refs_5_), channel_id=1, source_target_pairs={{0,112},{1,113},{2,114},{3,115},{4,116},{5,117},{6,118},{7,119},{8... | collective-permute-start | bytes 589832 | tf_op jit(solution)/shard_map/ppermute | solution.py:176
  76.3 1.9 %collective-permute-done.3.refs_3_ = bf16[16,48,128]{2,1,0:T(8,128)(2,1)S(1)} collective-permute-done((bf16[16,48,128]{2,1,0:T(8,128)(2,1)}, bf16[16,48,128]{2,1,0:T(8,128)(2,1)S(1)}, u32[]{:S(2)}, u32[]{:S(2)}) %collective-permute-start.3) | collective-permute-done | bytes 196640 | tf_op jit(solution)/shard_map/ppermute | solution.py:176
  78.1 1.9 %collective-permute-start.7 = (bf16[8,48,128]{2,1,0:T(8,128)(2,1)S(1)}, bf16[8,48,128]{2,1,0:T(8,128)(2,1)S(1)}, u32[]{:S(2)}, u32[]{:S(2)}) collective-permute-start(bf16[8,48,128]{2,1,0:T(8,128)(2,1)S(1)} %slice.17), channel_id=1, source_target_pairs={{0,16},{1,17},{2,18},{3,19},{4,20},{5,21},{6,22},{7,23},{8,24},{9,... | collective-permute-start | bytes 294920 | tf_op jit(solution)/shard_map/ppermute | solution.py:177
  80.4 5.3 %collective-permute-start.8 = (bf16[8,48,128]{2,1,0:T(8,128)(2,1)S(1)}, bf16[8,48,128]{2,1,0:T(8,128)(2,1)S(1)}, u32[]{:S(2)}, u32[]{:S(2)}) collective-permute-start(bf16[8,48,128]{2,1,0:T(8,128)(2,1)S(1)} %slice.18), channel_id=1, source_target_pairs={{0,112},{1,113},{2,114},{3,115},{4,116},{5,117},{6,118},{7,119},{8... | collective-permute-start | bytes 294920 | tf_op jit(solution)/shard_map/ppermute | solution.py:177
  85.8 2.2 %collective-permute-done.8.refs_8_ = bf16[8,48,128]{2,1,0:T(8,128)(2,1)S(1)} collective-permute-done((bf16[8,48,128]{2,1,0:T(8,128)(2,1)S(1)}, bf16[8,48,128]{2,1,0:T(8,128)(2,1)S(1)}, u32[]{:S(2)}, u32[]{:S(2)}) %collective-permute-start.8) | collective-permute-done | bytes 98336 | tf_op jit(solution)/shard_map/ppermute | solution.py:177
  88.0 0.9 broadcast_in_dim.9.refs_10_
  88.9 3.5 %forward.1 = (bf16[192,128]{1,0:T(8,128)(2,1)}, bf16[208,128]{1,0:T(8,128)(2,1)S(1)}) custom-call(s32[3]{0:T(128)S(1)} %pad_add_fusion.where, bf16[16,48,128]{2,1,0:T(8,128)(2,1)S(1)} %get-tuple-element.7.refs_0_, bf16[16,48,128]{2,1,0:T(8,128)(2,1)S(1)} %collective-permute-done.1.refs_1_, bf16[16,48,128]{2,1,0:T(8,128)(2,1)} %collective-permute-done.2.refs_2_, ...), custom_call_target="tpu_custom_call" | custom-call | tf_op jit(solution)/shard_map/forward/pallas_call | solution.py:180
  92.4 2.0 %collective-permute-start.9 = (bf16[208,128]{1,0:T(8,128)(2,1)S(1)}, bf16[208,128]{1,0:T(8,128)(2,1)S(1)}, u32[]{:S(2)}, u32[]{:S(2)}) collective-permute-start(bf16[208,128]{1,0:T(8,128)(2,1)S(1)} %get-tuple-element.5), channel_id=1, source_target_pairs={{0,256},{1,257},{2,258},{3,259},{4,260},{5,261},{6,262},{7,263},{8... | collective-permute-start | bytes 159752 | tf_op jit(solution)/shard_map/ppermute | solution.py:190
  94.4 3.8 %collective-permute-start.10 = (bf16[208,128]{1,0:T(8,128)(2,1)S(1)}, bf16[208,128]{1,0:T(8,128)(2,1)S(1)}, u32[]{:S(2)}, u32[]{:S(2)}) collective-permute-start(bf16[208,128]{1,0:T(8,128)(2,1)S(1)} %get-tuple-element.5), channel_id=1, source_target_pairs={{0,512},{1,513},{2,514},{3,515},{4,516},{5,517},{6,518},{7,519},{8... | collective-permute-start | bytes 159752 | tf_op jit(solution)/shard_map/ppermute | solution.py:190
  98.2 4.2 %collective-permute-start.11 = (bf16[208,128]{1,0:T(8,128)(2,1)S(1)}, bf16[208,128]{1,0:T(8,128)(2,1)S(1)}, u32[]{:S(2)}, u32[]{:S(2)}) collective-permute-start(bf16[208,128]{1,0:T(8,128)(2,1)S(1)} %get-tuple-element.5), channel_id=1, source_target_pairs={{0,768},{1,769},{2,770},{3,771},{4,772},{5,773},{6,774},{7,775},{8... | collective-permute-start | bytes 159752 | tf_op jit(solution)/shard_map/ppermute | solution.py:190
  103.2 2.2 %collective-permute-done.11 = bf16[208,128]{1,0:T(8,128)(2,1)S(1)} collective-permute-done((bf16[208,128]{1,0:T(8,128)(2,1)S(1)}, bf16[208,128]{1,0:T(8,128)(2,1)S(1)}, u32[]{:S(2)}, u32[]{:S(2)}) %collective-permute-start.11) | collective-permute-done | bytes 53280 | tf_op jit(solution)/shard_map/ppermute | solution.py:190
  105.5 9.5 %all-gather.1 = bf16[8,208,128]{2,1,0:T(8,128)(2,1)S(1)} all-gather(bf16[4,208,128]{2,1,0:T(8,128)(2,1)S(1)} %pad_maximum_fusion), channel_id=3, replica_groups={{0,128},{256,384},{512,640},{768,896},{1,129},{257,385},{513,641},{769,..., dimensions={0}, use_global_device_ids=true | all-gather | bytes 638976 | tf_op jit(solution)/shard_map/all_gather | solution.py:191
  115.2 1.4 %copy-done.2 = bf16[128,1,48,128]{3,2,1,0:T(8,128)(2,1)S(1)} copy-done((bf16[128,1,48,128]{3,2,1,0:T(8,128)(2,1)S(1)}, bf16[128,1,48,128]{3,2,1,0:T(8,128)(2,1)}, u32[]{:S(2)}) %copy-start.2) | copy-done | bytes 1572888
  116.6 2.8 %weight_grad.1 = f32[192,768]{1,0:T(8,128)} custom-call(s32[3]{0:T(128)S(1)} %pad_add_fusion.where, bf16[8,16,48,128]{3,2,1,0:T(8,128)(2,1)S(1)} %bitcast.31, bf16[2,4,208,128]{3,2,1,0:T(8,128)(2,1)S(1)} %bitcast.30, f32[768,128]{1,0:T(8,128)S(1)} %broadcast_in_dim.11.gain), custom_call_target="tpu_custom_call" | custom-call | tf_op jit(solution)/shard_map/weight_grad/pallas_call | solution.py:193
  (28 shorter events, 3.8 us)
Async XLA Ops:
  7.2 0.7 copy-start
  7.2 80.9 %copy-start.4 = (f32[6144]{0:T(1024)S(1)}, f32[6144]{0:T(1024)}, u32[]{:S(2)}) copy-start(f32[6144]{0:T(1024)} %param.7) | copy-start | bytes 73732
  7.2 107.8 %all-gather.4.cloned.1.call-start = ((), (), s32[]{:S(2)}) async-start(), calls=%async_computation.1 | async-start | bytes 1769472 | tf_op jit(solution)/shard_map/all_gather | solution.py:172
  8.7 6.1 %collective-permute-start = (bf16[48,128]{1,0:T(8,128)(2,1)S(1)}, bf16[48,128]{1,0:T(8,128)(2,1)S(1)}, u32[]{:S(2)}, u32[]{:S(2)}) collective-permute-start(bf16[48,128]{1,0:T(8,128)(2,1)S(1)} %bitcast.38), channel_id=1, source_target_pairs={{0,0},{1,1},{2,2},{3,3},{4,4},{5,5},{6,6},{7,7},{8,8},{9,9},{10,10... | collective-permute-start | bytes 36872 | tf_op jit(solution)/shard_map/ppermute | solution.py:167
  40.4 48.5 %copy-start.1 = (bf16[6144,192]{0,1:T(8,128)(2,1)S(1)}, bf16[6144,192]{0,1:T(8,128)(2,1)}, u32[]{:S(2)}) copy-start(bf16[6144,192]{0,1:T(8,128)(2,1)} %param.8) | copy-start | bytes 7077892
  40.4 48.5 %copy-start.3 = (bf16[1,128,192]{1,2,0:T(8,128)(2,1)S(1)}, bf16[1,128,192]{1,2,0:T(8,128)(2,1)}, u32[]{:S(2)}) copy-start(bf16[1,128,192]{1,2,0:T(8,128)(2,1)} %param.9) | copy-start | bytes 147460
  41.1 20.2 %collective-permute-start.1 = (bf16[16,48,128]{2,1,0:T(8,128)(2,1)S(1)}, bf16[16,48,128]{2,1,0:T(8,128)(2,1)S(1)}, u32[]{:S(2)}, u32[]{:S(2)}) collective-permute-start(bf16[16,48,128]{2,1,0:T(8,128)(2,1)S(1)} %get-tuple-element.7.refs_0_), channel_id=1, source_target_pairs={{0,16},{1,17},{2,18},{3,19},{4,20},{5,21},{6,22},{7,23},{8,24},{9,... | collective-permute-start | bytes 589832 | tf_op jit(solution)/shard_map/ppermute | solution.py:174
  46.2 17.1 %collective-permute-start.4 = (bf16[16,48,128]{2,1,0:T(8,128)(2,1)S(1)}, bf16[16,48,128]{2,1,0:T(8,128)(2,1)S(1)}, u32[]{:S(2)}, u32[]{:S(2)}) collective-permute-start(bf16[16,48,128]{2,1,0:T(8,128)(2,1)S(1)} %get-tuple-element.7.refs_0_), channel_id=1, source_target_pairs={{0,112},{1,113},{2,114},{3,115},{4,116},{5,117},{6,118},{7,119},{8... | collective-permute-start | bytes 589832 | tf_op jit(solution)/shard_map/ppermute | solution.py:174
  61.3 7.9 %collective-permute-start.2 = (bf16[16,48,128]{2,1,0:T(8,128)(2,1)S(1)}, bf16[16,48,128]{2,1,0:T(8,128)(2,1)}, u32[]{:S(2)}, u32[]{:S(2)}) collective-permute-start(bf16[16,48,128]{2,1,0:T(8,128)(2,1)S(1)} %collective-permute-done.1.refs_1_), channel_id=1, source_target_pairs={{0,16},{1,17},{2,18},{3,19},{4,20},{5,21},{6,22},{7,23},{8,24},{9,... | collective-permute-start | bytes 589832 | tf_op jit(solution)/shard_map/ppermute | solution.py:175
  63.2 7.9 %collective-permute-start.5 = (bf16[16,48,128]{2,1,0:T(8,128)(2,1)S(1)}, bf16[16,48,128]{2,1,0:T(8,128)(2,1)}, u32[]{:S(2)}, u32[]{:S(2)}) collective-permute-start(bf16[16,48,128]{2,1,0:T(8,128)(2,1)S(1)} %collective-permute-done.4.refs_4_), channel_id=1, source_target_pairs={{0,112},{1,113},{2,114},{3,115},{4,116},{5,117},{6,118},{7,119},{8... | collective-permute-start | bytes 589832 | tf_op jit(solution)/shard_map/ppermute | solution.py:175
  69.2 8.9 %collective-permute-start.3 = (bf16[16,48,128]{2,1,0:T(8,128)(2,1)}, bf16[16,48,128]{2,1,0:T(8,128)(2,1)S(1)}, u32[]{:S(2)}, u32[]{:S(2)}) collective-permute-start(bf16[16,48,128]{2,1,0:T(8,128)(2,1)} %collective-permute-done.2.refs_2_), channel_id=1, source_target_pairs={{0,16},{1,17},{2,18},{3,19},{4,20},{5,21},{6,22},{7,23},{8,24},{9,... | collective-permute-start | bytes 589832 | tf_op jit(solution)/shard_map/ppermute | solution.py:176
  71.1 9.3 %collective-permute-start.6 = (bf16[16,48,128]{2,1,0:T(8,128)(2,1)}, bf16[16,48,128]{2,1,0:T(8,128)(2,1)S(1)}, u32[]{:S(2)}, u32[]{:S(2)}) collective-permute-start(bf16[16,48,128]{2,1,0:T(8,128)(2,1)} %collective-permute-done.5.refs_5_), channel_id=1, source_target_pairs={{0,112},{1,113},{2,114},{3,115},{4,116},{5,117},{6,118},{7,119},{8... | collective-permute-start | bytes 589832 | tf_op jit(solution)/shard_map/ppermute | solution.py:176
  78.1 7.7 %collective-permute-start.7 = (bf16[8,48,128]{2,1,0:T(8,128)(2,1)S(1)}, bf16[8,48,128]{2,1,0:T(8,128)(2,1)S(1)}, u32[]{:S(2)}, u32[]{:S(2)}) collective-permute-start(bf16[8,48,128]{2,1,0:T(8,128)(2,1)S(1)} %slice.17), channel_id=1, source_target_pairs={{0,16},{1,17},{2,18},{3,19},{4,20},{5,21},{6,22},{7,23},{8,24},{9,... | collective-permute-start | bytes 294920 | tf_op jit(solution)/shard_map/ppermute | solution.py:177
  80.4 7.6 %collective-permute-start.8 = (bf16[8,48,128]{2,1,0:T(8,128)(2,1)S(1)}, bf16[8,48,128]{2,1,0:T(8,128)(2,1)S(1)}, u32[]{:S(2)}, u32[]{:S(2)}) collective-permute-start(bf16[8,48,128]{2,1,0:T(8,128)(2,1)S(1)} %slice.18), channel_id=1, source_target_pairs={{0,112},{1,113},{2,114},{3,115},{4,116},{5,117},{6,118},{7,119},{8... | collective-permute-start | bytes 294920 | tf_op jit(solution)/shard_map/ppermute | solution.py:177
  92.4 10.1 %collective-permute-start.9 = (bf16[208,128]{1,0:T(8,128)(2,1)S(1)}, bf16[208,128]{1,0:T(8,128)(2,1)S(1)}, u32[]{:S(2)}, u32[]{:S(2)}) collective-permute-start(bf16[208,128]{1,0:T(8,128)(2,1)S(1)} %get-tuple-element.5), channel_id=1, source_target_pairs={{0,256},{1,257},{2,258},{3,259},{4,260},{5,261},{6,262},{7,263},{8... | collective-permute-start | bytes 159752 | tf_op jit(solution)/shard_map/ppermute | solution.py:190
  94.4 8.8 %collective-permute-start.10 = (bf16[208,128]{1,0:T(8,128)(2,1)S(1)}, bf16[208,128]{1,0:T(8,128)(2,1)S(1)}, u32[]{:S(2)}, u32[]{:S(2)}) collective-permute-start(bf16[208,128]{1,0:T(8,128)(2,1)S(1)} %get-tuple-element.5), channel_id=1, source_target_pairs={{0,512},{1,513},{2,514},{3,515},{4,516},{5,517},{6,518},{7,519},{8... | collective-permute-start | bytes 159752 | tf_op jit(solution)/shard_map/ppermute | solution.py:190
  98.2 7.3 %collective-permute-start.11 = (bf16[208,128]{1,0:T(8,128)(2,1)S(1)}, bf16[208,128]{1,0:T(8,128)(2,1)S(1)}, u32[]{:S(2)}, u32[]{:S(2)}) collective-permute-start(bf16[208,128]{1,0:T(8,128)(2,1)S(1)} %get-tuple-element.5), channel_id=1, source_target_pairs={{0,768},{1,769},{2,770},{3,771},{4,772},{5,773},{6,774},{7,775},{8... | collective-permute-start | bytes 159752 | tf_op jit(solution)/shard_map/ppermute | solution.py:190
  115.2 1.4 %copy-start.2 = (bf16[128,1,48,128]{3,2,1,0:T(8,128)(2,1)S(1)}, bf16[128,1,48,128]{3,2,1,0:T(8,128)(2,1)}, u32[]{:S(2)}) copy-start(bf16[128,1,48,128]{3,2,1,0:T(8,128)(2,1)} %all-gather.4.cloned.1.call-done) | copy-start | bytes 4718596
Sparse Core Ops, SparseCore 0:
  41.2 48.3 all-gather.3

commit v3 on v1

--- a/solution.py
+++ b/solution.py
@@ -65,25 +65,25 @@
     return (preact * normal_cdf, normal_cdf + preact * density)
 
 
-def tiles(where, pieces, part):
-    me = where[1]
-    for k, refs in enumerate(pieces):
-        shift = (0, -1, -2, -3, 1, 2, 3, 4)[k]
+def tiles(me, pieces, part):
+    for shift, ref in zip((0, -1, -2, -3, -4, 1, 2, 3), pieces):
         ring = lax.rem(me + (shift + 8), 8)
         for j in range(8):
             for half in range(2):
-                if len(refs) == 1:
-                    yield refs[0].at[2 * j + half, part], ring, j, half
-                else:
-                    yield refs[j // 4].at[2 * (j % 4) + half, part], ring, j, half
+                yield ref.at[2 * j + half, part], ring, j, half
+
+
+def spread_kernel(piece, gain, spread):
+    for row in range(D // 128):
+        spread[row * 128 : (row + 1) * 128, :] = jnp.broadcast_to(gain[row : row + 1, :], (128, KEEP)).T
 
 
 def forward_kernel(where, *refs):
-    pieces = [refs[k : k + 1] for k in range(7)] + [refs[7:9]]
-    weight, gain, hidden_grad, hidden, payload, rows = refs[9:]
+    pieces = refs[:8]
+    weight, gain, hidden_grad, hidden, payload, rows = refs[8:]
     on_y = where[0] == 0
     total = jnp.zeros((8, KEEP), F32)
-    for tile, ring, j, half in tiles(where, pieces, 0):
+    for tile, ring, j, half in tiles(where[1], pieces, 0):
         value = tile[...]
         place = jnp.where(on_y, ring * 768 + j * 96, j * 768 + ring * 96) + half * 48
         rows[pl.ds(pl.multiple_of(place, 16), 48), :] = value
@@ -102,7 +102,7 @@
         preact += jnp.dot(weight[:, start : start + 256], normed, preferred_element_type=F32)
     activated, slope_full = gelu_pair(preact)
     hidden[...] = activated.astype(BF)
-    payload[0:192, :] = (hidden_grad[...].astype(F32) * slope_full).astype(BF)
+    slope = (hidden_grad[...].astype(F32) * slope_full).astype(BF)
     lines = []
     for value in (average, scale):
         for _ in range(3):
@@ -110,12 +110,16 @@
             lines.append(top)
             value = value - top
     lines.append(jnp.zeros((10, KEEP), F32))
-    payload[192:208, :] = jnp.concatenate(lines, axis=0).astype(BF)
+    lines = jnp.concatenate(lines, axis=0).astype(BF)
+    for copy in range(4):
+        payload[copy, 0:192, :] = slope
+        payload[copy, 192:208, :] = lines
 
 
 def grad_kernel(where, *refs):
-    pieces = [refs[k : k + 1] for k in range(7)] + [refs[7:9]]
-    payload, gain, out, normed, slopes, averages, scales = refs[9:]
+    pieces = refs[:8]
+    payload, gain, out, normed, slopes, averages, scales = refs[8:]
+    first = where[2] * 768
     on_y = where[0] == 0
     for image in range(8):
         ref = payload.at[image % 2, image // 2]
@@ -123,11 +127,11 @@
         lines = ref[192:208, :].astype(F32)
         averages[image : image + 1, :] = lines[0:1] + lines[1:2] + lines[2:3]
         scales[image : image + 1, :] = lines[3:4] + lines[4:5] + lines[5:6]
-    for tile, ring, j, half in tiles(where, pieces, 1):
+    for tile, ring, j, half in tiles(where[1], pieces, 1):
         image = jnp.where(on_y, ring, j)
         place = pl.multiple_of(jnp.where(on_y, j * 96, ring * 96) + half * 48, 16)
         centered = tile[...].astype(F32) - averages[pl.ds(image, 1), :]
-        value = centered * scales[pl.ds(image, 1), :] * gain[pl.ds(place, 48), :]
+        value = centered * scales[pl.ds(image, 1), :] * gain[pl.ds(pl.multiple_of(first + place, 16), 48), :]
         normed[pl.ds(place, 48), pl.ds(pl.multiple_of(image * KEEP, KEEP), KEEP)] = value.astype(BF)
     out[...] = lax.dot_general(
         slopes[...], normed[...], (((1,), (1,)), ((), ())), preferred_element_type=F32
@@ -141,9 +145,7 @@
 def shards(patches, keep_list, norm_gain, up_weight, hidden_grad):
     dp, mp = lax.axis_index("dp"), lax.axis_index("mp")
     core = dp % 2
-    where = jnp.stack([core, jnp.where(core == 0, mp // 16, (mp // 2) % 8)]).astype(jnp.int32)
-    gain_all = jnp.broadcast_to(norm_gain[:, None], (D, KEEP))
-    gain_block = jnp.broadcast_to(lax.dynamic_slice(norm_gain, (dp * 768,), (768,))[:, None], (768, KEEP))
+    where = jnp.stack([core, jnp.where(core == 0, mp // 16, (mp // 2) % 8), dp]).astype(jnp.int32)
 
     picked = (lax.broadcasted_iota(jnp.int32, (192, KEEP), 0) == keep_list).astype(BF)
     own = jnp.dot(patches[0].T, picked, preferred_element_type=F32).astype(BF)
@@ -154,29 +156,36 @@
     back = functools.partial(lax.ppermute, axis_name=AXES, perm=ring_pairs(-1))
     f1, b1 = ahead(both), back(both)
     f2, b2 = ahead(f1), back(b1)
+    gain_all = pl.pallas_call(
+        spread_kernel,
+        out_shape=jax.ShapeDtypeStruct((D, KEEP), F32),
+        in_specs=[pl.BlockSpec(memory_space=pl.ANY), VMEM],
+        out_specs=VMEM,
+        compiler_params=pltpu.CompilerParams(vmem_limit_bytes=24 * 2**20),
+        cost_estimate=pl.CostEstimate(flops=2 * 2**30, bytes_accessed=8 * 2**20, transcendentals=0),
+        name="spread",
+    )(b2, norm_gain.reshape(D // 128, 128))
     f3, b3 = ahead(f2), back(b2)
-    f4, b4 = ahead(f3[:8]), back(b3[8:])
-    pieces = (both, f1, f2, f3, b1, b2, b3, f4, b4)
+    f4 = ahead(f3)
+    pieces = (both, f1, f2, f3, f4, b1, b2, b3)
 
     hidden, payload = pl.pallas_call(
         forward_kernel,
-        out_shape=(jax.ShapeDtypeStruct((192, KEEP), BF), jax.ShapeDtypeStruct((208, KEEP), BF)),
-        in_specs=[SMEM] + [VMEM] * 12,
+        out_shape=(jax.ShapeDtypeStruct((192, KEEP), BF), jax.ShapeDtypeStruct((4, 208, KEEP), BF)),
+        in_specs=[SMEM] + [VMEM] * 11,
         out_specs=(VMEM, VMEM),
         scratch_shapes=[pltpu.VMEM((D, KEEP), BF)],
         compiler_params=pltpu.CompilerParams(vmem_limit_bytes=24 * 2**20),
         name="forward",
     )(where, *pieces, up_weight.T, gain_all, hidden_grad[0].T)
 
-    payload = lax.all_to_all(
-        jnp.broadcast_to(payload[None], (4, 208, KEEP)), "dp", 0, 0, axis_index_groups=[[0, 2, 4, 6], [1, 3, 5, 7]]
-    )
+    payload = lax.all_to_all(payload, "dp", 0, 0, axis_index_groups=[[0, 2, 4, 6], [1, 3, 5, 7]])
     payload = lax.all_gather(payload, "dp", axis_index_groups=[[0, 1], [2, 3], [4, 5], [6, 7]])
 
     grad = pl.pallas_call(
         grad_kernel,
         out_shape=jax.ShapeDtypeStruct((192, 768), F32),
-        in_specs=[SMEM] + [VMEM] * 11,
+        in_specs=[SMEM] + [VMEM] * 10,
         out_specs=VMEM,
         scratch_shapes=[
             pltpu.VMEM((768, 1024), BF),
@@ -186,7 +195,7 @@
         ],
         compiler_params=pltpu.CompilerParams(vmem_limit_bytes=24 * 2**20),
         name="weight_grad",
-    )(where, *pieces, payload, gain_block)
+    )(where, *pieces, payload, gain_all)
     return (hidden.T[None], grad.T)
 
 

time: 116 us -> 113 us (0.974)
  blocking collectives: 35.1 us -> 47.4 us
  starting transfers between devices: 47.8 us -> 39.4 us
  waiting for transfers between devices: 20.4 us -> 16.5 us
  local copies, waits for them, and re-layouts: 4.73 us -> 1.54 us
    all_to_all x0 -> x1, blocking collectives: none -> 11.3 us  [shards(): lax.all_to_all(payload, 'dp', 0, 0, axis_index_groups=[[0, 2, 4, 6], [1,...]
    all_to_all x1 -> x0, waiting for transfers between devices: 7.4 us -> none  [shards(): lax.all_to_all(jnp.broadcast_to(payload[None], (4, 208, KEEP)), 'dp', 0,...]
    ppermute x2 -> x1, starting transfers between devices: 6.93 us -> 1.91 us  [shards(): f4 = ahead(f3)]
    ppermute x2 -> x1, waiting for transfers between devices: 2.77 us -> 6.35 us  [shards(): f4 = ahead(f3)]
    all_to_all x1 -> x0, starting transfers between devices: 3.38 us -> none  [shards(): lax.all_to_all(jnp.broadcast_to(payload[None], (4, 208, KEEP)), 'dp', 0,...]
    broadcast_in_dim x3 -> x0, local copies, waits for them, and re-layouts: 2.46 us -> none  [the longest x1 1.6 us: shards(): gain_all = jnp.broadcast_to(norm_gain[:, None], (D, KEEP))]
  transfers between devices with their start and end apart: 10 -> 8, of which waited for: 7 -> 5; matrix products, arithmetic and copies ran while one was open for 1% -> 0% of each run, Pallas kernels for 0% -> 1%
where the time goes in v3:
time: 113 us
  blocking collectives  47.4 us (42%)
  starting transfers between devices  39.4 us (35%)
  waiting for transfers between devices  16.5 us (15%)
  Pallas kernels  6.45 us (6%)
  local copies, waits for them, and re-layouts  1.54 us (1%)
    all_to_all x1, blocking collectives, shards(): both = lax.all_to_all(both, AXES, 0, 0, axis_index_groups=first_groups())  25.5 us
    ppermute x2, starting transfers between devices, shards(): f1, b1 = (ahead(both), back(both))  19 us
    all_to_all x1, blocking collectives, shards(): lax.all_to_all(payload, 'dp', 0, 0, axis_index_groups=[[0, 2, 4, 6], [1,...  11.3 us
    all_gather x1, blocking collectives, shards(): lax.all_gather(payload, 'dp', axis_index_groups=[[0, 1], [2, 3], [4, 5],...  10.5 us
    ppermute x2, starting transfers between devices, shards(): f3, b3 = (ahead(f2), back(b2))  7.06 us
    ppermute x2, starting transfers between devices, shards(): f2, b2 = (ahead(f1), back(b1))  6.77 us
    ppermute x1, waiting for transfers between devices, shards(): f4 = ahead(f3)  6.35 us
    ppermute x1, starting transfers between devices, shards(): other = lax.ppermute(own, AXES, swap_pairs())  4.7 us
  transfers between devices with their start and end apart: 8, of which 5 were waited for; matrix products, arithmetic and copies ran while one was open for 0% of the time, Pallas kernels for 1%

profile of v3, /device:TPU:1, one launch (start us, length us, event | category | flops | bytes accessed | tf_op | source)
XLA Modules:
  0.0 113.0 jit_solution(3954639968461791638)
XLA Ops:
  0.6 0.7 copy-done
  1.4 0.8 convolution_convert_fusion
  2.2 4.7 %collective-permute-start = (bf16[48,128]{1,0:T(8,128)(2,1)S(1)}, bf16[48,128]{1,0:T(8,128)(2,1)S(1)}, u32[]{:S(2)}, u32[]{:S(2)}) collective-permute-start(bf16[48,128]{1,0:T(8,128)(2,1)S(1)} %bitcast.26), channel_id=1, source_target_pairs={{0,0},{1,1},{2,2},{3,3},{4,4},{5,5},{6,6},{7,7},{8,8},{9,9},{10,10... | collective-permute-start | bytes 36872 | tf_op jit(solution)/shard_map/ppermute | solution.py:152
  6.9 1.4 %collective-permute-done = bf16[48,128]{1,0:T(8,128)(2,1)S(1)} collective-permute-done((bf16[48,128]{1,0:T(8,128)(2,1)S(1)}, bf16[48,128]{1,0:T(8,128)(2,1)S(1)}, u32[]{:S(2)}, u32[]{:S(2)}) %collective-permute-start) | collective-permute-done | bytes 12320 | tf_op jit(solution)/shard_map/ppermute | solution.py:152
  8.3 0.1 broadcast_in_dim.4
  8.3 25.5 %all_to_all.10.refs_0_ = bf16[16,2,48,128]{3,2,1,0:T(8,128)(2,1)S(1)} all-to-all(bf16[16,2,48,128]{3,2,1,0:T(8,128)(2,1)S(1)} %broadcast_in_dim.4), channel_id=1, replica_groups={{0,1,2,3,4,5,6,7,8,9,10,11,12,13,14,15},{16,17,18,19,20,21,22,23,24,25,..., dimensions={0} | all-to-all | bytes 786432 | tf_op jit(solution)/shard_map/all_to_all | solution.py:154
  33.8 4.9 %collective-permute-start.1 = (bf16[16,2,48,128]{3,2,1,0:T(8,128)(2,1)S(1)}, bf16[16,2,48,128]{3,2,1,0:T(8,128)(2,1)S(1)}, u32[]{:S(2)}, u32[]{:S(2)}) collective-permute-start(bf16[16,2,48,128]{3,2,1,0:T(8,128)(2,1)S(1)} %all_to_all.10.refs_0_), channel_id=1, source_target_pairs={{0,16},{1,17},{2,18},{3,19},{4,20},{5,21},{6,22},{7,23},{8,24},{9,... | collective-permute-start | bytes 1179656 | tf_op jit(solution)/shard_map/ppermute | solution.py:157
  38.7 14.1 %collective-permute-start.5 = (bf16[16,2,48,128]{3,2,1,0:T(8,128)(2,1)S(1)}, bf16[16,2,48,128]{3,2,1,0:T(8,128)(2,1)S(1)}, u32[]{:S(2)}, u32[]{:S(2)}) collective-permute-start(bf16[16,2,48,128]{3,2,1,0:T(8,128)(2,1)S(1)} %all_to_all.10.refs_0_), channel_id=1, source_target_pairs={{0,112},{1,113},{2,114},{3,115},{4,116},{5,117},{6,118},{7,119},{8... | collective-permute-start | bytes 1179656 | tf_op jit(solution)/shard_map/ppermute | solution.py:157
  52.9 3.2 %collective-permute-done.1.refs_1_ = bf16[16,2,48,128]{3,2,1,0:T(8,128)(2,1)S(1)} collective-permute-done((bf16[16,2,48,128]{3,2,1,0:T(8,128)(2,1)S(1)}, bf16[16,2,48,128]{3,2,1,0:T(8,128)(2,1)S(1)}, u32[]{:S(2)}, u32[]{:S(2)}) %collective-permute-start.1) | collective-permute-done | bytes 393248 | tf_op jit(solution)/shard_map/ppermute | solution.py:157
  56.1 1.9 %collective-permute-start.2 = (bf16[16,2,48,128]{3,2,1,0:T(8,128)(2,1)S(1)}, bf16[16,2,48,128]{3,2,1,0:T(8,128)(2,1)S(1)}, u32[]{:S(2)}, u32[]{:S(2)}) collective-permute-start(bf16[16,2,48,128]{3,2,1,0:T(8,128)(2,1)S(1)} %collective-permute-done.1.refs_1_), channel_id=1, source_target_pairs={{0,16},{1,17},{2,18},{3,19},{4,20},{5,21},{6,22},{7,23},{8,24},{9,... | collective-permute-start | bytes 1179656 | tf_op jit(solution)/shard_map/ppermute | solution.py:158
  58.0 4.9 %collective-permute-start.6 = (bf16[16,2,48,128]{3,2,1,0:T(8,128)(2,1)S(1)}, bf16[16,2,48,128]{3,2,1,0:T(8,128)(2,1)S(1)}, u32[]{:S(2)}, u32[]{:S(2)}) collective-permute-start(bf16[16,2,48,128]{3,2,1,0:T(8,128)(2,1)S(1)} %collective-permute-done.5.refs_5_), channel_id=1, source_target_pairs={{0,112},{1,113},{2,114},{3,115},{4,116},{5,117},{6,118},{7,119},{8... | collective-permute-start | bytes 1179656 | tf_op jit(solution)/shard_map/ppermute | solution.py:158
  62.9 2.9 %collective-permute-done.2.refs_2_ = bf16[16,2,48,128]{3,2,1,0:T(8,128)(2,1)S(1)} collective-permute-done((bf16[16,2,48,128]{3,2,1,0:T(8,128)(2,1)S(1)}, bf16[16,2,48,128]{3,2,1,0:T(8,128)(2,1)S(1)}, u32[]{:S(2)}, u32[]{:S(2)}) %collective-permute-start.2) | collective-permute-done | bytes 393248 | tf_op jit(solution)/shard_map/ppermute | solution.py:158
  65.8 1.9 %collective-permute-start.3 = (bf16[16,2,48,128]{3,2,1,0:T(8,128)(2,1)S(1)}, bf16[16,2,48,128]{3,2,1,0:T(8,128)(2,1)S(1)}, u32[]{:S(2)}, u32[]{:S(2)}) collective-permute-start(bf16[16,2,48,128]{3,2,1,0:T(8,128)(2,1)S(1)} %collective-permute-done.2.refs_2_), channel_id=1, source_target_pairs={{0,16},{1,17},{2,18},{3,19},{4,20},{5,21},{6,22},{7,23},{8,24},{9,... | collective-permute-start | bytes 1179656 | tf_op jit(solution)/shard_map/ppermute | solution.py:168
  67.7 5.2 %collective-permute-start.7 = (bf16[16,2,48,128]{3,2,1,0:T(8,128)(2,1)S(1)}, bf16[16,2,48,128]{3,2,1,0:T(8,128)(2,1)S(1)}, u32[]{:S(2)}, u32[]{:S(2)}) collective-permute-start(bf16[16,2,48,128]{3,2,1,0:T(8,128)(2,1)S(1)} %collective-permute-done.6.piece.refs_6_), channel_id=1, source_target_pairs={{0,112},{1,113},{2,114},{3,115},{4,116},{5,117},{6,118},{7,119},{8... | collective-permute-start | bytes 1179656 | tf_op jit(solution)/shard_map/ppermute | solution.py:168
  72.9 2.6 %collective-permute-done.3.refs_3_ = bf16[16,2,48,128]{3,2,1,0:T(8,128)(2,1)S(1)} collective-permute-done((bf16[16,2,48,128]{3,2,1,0:T(8,128)(2,1)S(1)}, bf16[16,2,48,128]{3,2,1,0:T(8,128)(2,1)S(1)}, u32[]{:S(2)}, u32[]{:S(2)}) %collective-permute-start.3) | collective-permute-done | bytes 393248 | tf_op jit(solution)/shard_map/ppermute | solution.py:168
  75.5 1.9 %collective-permute-start.4 = (bf16[16,2,48,128]{3,2,1,0:T(8,128)(2,1)S(1)}, bf16[16,2,48,128]{3,2,1,0:T(8,128)(2,1)S(1)}, u32[]{:S(2)}, u32[]{:S(2)}) collective-permute-start(bf16[16,2,48,128]{3,2,1,0:T(8,128)(2,1)S(1)} %collective-permute-done.3.refs_3_), channel_id=1, source_target_pairs={{0,16},{1,17},{2,18},{3,19},{4,20},{5,21},{6,22},{7,23},{8,24},{9,... | collective-permute-start | bytes 1179656 | tf_op jit(solution)/shard_map/ppermute | solution.py:169
  77.5 0.1 pad_add_fusion.where
  77.6 0.7 copy-done.3
  78.3 0.9 spread.1.refs_9_
  79.2 6.4 %collective-permute-done.4.refs_4_ = bf16[16,2,48,128]{3,2,1,0:T(8,128)(2,1)S(1)} collective-permute-done((bf16[16,2,48,128]{3,2,1,0:T(8,128)(2,1)S(1)}, bf16[16,2,48,128]{3,2,1,0:T(8,128)(2,1)S(1)}, u32[]{:S(2)}, u32[]{:S(2)}) %collective-permute-start.4) | collective-permute-done | bytes 393248 | tf_op jit(solution)/shard_map/ppermute | solution.py:169
  85.5 3.0 %forward.1 = (bf16[192,128]{1,0:T(8,128)(2,1)}, bf16[4,208,128]{2,1,0:T(8,128)(2,1)S(1)}) custom-call(s32[3]{0:T(128)S(1)} %pad_add_fusion.where, bf16[16,2,48,128]{3,2,1,0:T(8,128)(2,1)S(1)} %all_to_all.10.refs_0_, bf16[16,2,48,128]{3,2,1,0:T(8,128)(2,1)S(1)} %collective-permute-done.1.refs_1_, bf16[16,2,48,128]{3,2,1,0:T(8,128)(2,1)S(1)} %collective-permute-done.2.refs_2_, ...), custom_call_target="tpu_custom_call" | custom-call | tf_op jit(solution)/shard_map/forward/pallas_call | solution.py:172
  88.5 11.3 %all_to_all.11 = bf16[4,208,128]{2,1,0:T(8,128)(2,1)S(1)} all-to-all(bf16[4,208,128]{2,1,0:T(8,128)(2,1)S(1)} %get-tuple-element.5), channel_id=1, replica_groups={{0,256,512,768},{128,384,640,896},{1,257,513,769},{129,385,641,897},{2,..., dimensions={0} | all-to-all | bytes 425984 | tf_op jit(solution)/shard_map/all_to_all | solution.py:182
  99.8 10.5 %all-gather = bf16[8,208,128]{2,1,0:T(8,128)(2,1)S(1)} all-gather(bf16[4,208,128]{2,1,0:T(8,128)(2,1)S(1)} %all_to_all.11), channel_id=2, replica_groups={{0,128},{256,384},{512,640},{768,896},{1,129},{257,385},{513,641},{769,..., dimensions={0}, use_global_device_ids=true | all-gather | bytes 638976 | tf_op jit(solution)/shard_map/all_gather | solution.py:183
  110.3 2.6 %weight_grad.1 = f32[192,768]{1,0:T(8,128)} custom-call(s32[3]{0:T(128)S(1)} %pad_add_fusion.where, bf16[16,2,48,128]{3,2,1,0:T(8,128)(2,1)S(1)} %all_to_all.10.refs_0_, bf16[16,2,48,128]{3,2,1,0:T(8,128)(2,1)S(1)} %collective-permute-done.1.refs_1_, bf16[16,2,48,128]{3,2,1,0:T(8,128)(2,1)S(1)} %collective-permute-done.2.refs_2_, ...), custom_call_target="tpu_custom_call" | custom-call | tf_op jit(solution)/shard_map/weight_grad/pallas_call | solution.py:185
  (10 shorter events, 0.0 us)
Async XLA Ops:
  0.6 0.7 copy-start
  2.2 6.1 %collective-permute-start = (bf16[48,128]{1,0:T(8,128)(2,1)S(1)}, bf16[48,128]{1,0:T(8,128)(2,1)S(1)}, u32[]{:S(2)}, u32[]{:S(2)}) collective-permute-start(bf16[48,128]{1,0:T(8,128)(2,1)S(1)} %bitcast.26), channel_id=1, source_target_pairs={{0,0},{1,1},{2,2},{3,3},{4,4},{5,5},{6,6},{7,7},{8,8},{9,9},{10,10... | collective-permute-start | bytes 36872 | tf_op jit(solution)/shard_map/ppermute | solution.py:152
  33.8 22.2 %collective-permute-start.1 = (bf16[16,2,48,128]{3,2,1,0:T(8,128)(2,1)S(1)}, bf16[16,2,48,128]{3,2,1,0:T(8,128)(2,1)S(1)}, u32[]{:S(2)}, u32[]{:S(2)}) collective-permute-start(bf16[16,2,48,128]{3,2,1,0:T(8,128)(2,1)S(1)} %all_to_all.10.refs_0_), channel_id=1, source_target_pairs={{0,16},{1,17},{2,18},{3,19},{4,20},{5,21},{6,22},{7,23},{8,24},{9,... | collective-permute-start | bytes 1179656 | tf_op jit(solution)/shard_map/ppermute | solution.py:157
  38.7 19.3 %collective-permute-start.5 = (bf16[16,2,48,128]{3,2,1,0:T(8,128)(2,1)S(1)}, bf16[16,2,48,128]{3,2,1,0:T(8,128)(2,1)S(1)}, u32[]{:S(2)}, u32[]{:S(2)}) collective-permute-start(bf16[16,2,48,128]{3,2,1,0:T(8,128)(2,1)S(1)} %all_to_all.10.refs_0_), channel_id=1, source_target_pairs={{0,112},{1,113},{2,114},{3,115},{4,116},{5,117},{6,118},{7,119},{8... | collective-permute-start | bytes 1179656 | tf_op jit(solution)/shard_map/ppermute | solution.py:157
  56.1 9.7 %collective-permute-start.2 = (bf16[16,2,48,128]{3,2,1,0:T(8,128)(2,1)S(1)}, bf16[16,2,48,128]{3,2,1,0:T(8,128)(2,1)S(1)}, u32[]{:S(2)}, u32[]{:S(2)}) collective-permute-start(bf16[16,2,48,128]{3,2,1,0:T(8,128)(2,1)S(1)} %collective-permute-done.1.refs_1_), channel_id=1, source_target_pairs={{0,16},{1,17},{2,18},{3,19},{4,20},{5,21},{6,22},{7,23},{8,24},{9,... | collective-permute-start | bytes 1179656 | tf_op jit(solution)/shard_map/ppermute | solution.py:158
  58.0 9.7 %collective-permute-start.6 = (bf16[16,2,48,128]{3,2,1,0:T(8,128)(2,1)S(1)}, bf16[16,2,48,128]{3,2,1,0:T(8,128)(2,1)S(1)}, u32[]{:S(2)}, u32[]{:S(2)}) collective-permute-start(bf16[16,2,48,128]{3,2,1,0:T(8,128)(2,1)S(1)} %collective-permute-done.5.refs_5_), channel_id=1, source_target_pairs={{0,112},{1,113},{2,114},{3,115},{4,116},{5,117},{6,118},{7,119},{8... | collective-permute-start | bytes 1179656 | tf_op jit(solution)/shard_map/ppermute | solution.py:158
  65.8 9.7 %collective-permute-start.3 = (bf16[16,2,48,128]{3,2,1,0:T(8,128)(2,1)S(1)}, bf16[16,2,48,128]{3,2,1,0:T(8,128)(2,1)S(1)}, u32[]{:S(2)}, u32[]{:S(2)}) collective-permute-start(bf16[16,2,48,128]{3,2,1,0:T(8,128)(2,1)S(1)} %collective-permute-done.2.refs_2_), channel_id=1, source_target_pairs={{0,16},{1,17},{2,18},{3,19},{4,20},{5,21},{6,22},{7,23},{8,24},{9,... | collective-permute-start | bytes 1179656 | tf_op jit(solution)/shard_map/ppermute | solution.py:168
  67.7 11.4 %collective-permute-start.7 = (bf16[16,2,48,128]{3,2,1,0:T(8,128)(2,1)S(1)}, bf16[16,2,48,128]{3,2,1,0:T(8,128)(2,1)S(1)}, u32[]{:S(2)}, u32[]{:S(2)}) collective-permute-start(bf16[16,2,48,128]{3,2,1,0:T(8,128)(2,1)S(1)} %collective-permute-done.6.piece.refs_6_), channel_id=1, source_target_pairs={{0,112},{1,113},{2,114},{3,115},{4,116},{5,117},{6,118},{7,119},{8... | collective-permute-start | bytes 1179656 | tf_op jit(solution)/shard_map/ppermute | solution.py:168
  75.5 10.0 %collective-permute-start.4 = (bf16[16,2,48,128]{3,2,1,0:T(8,128)(2,1)S(1)}, bf16[16,2,48,128]{3,2,1,0:T(8,128)(2,1)S(1)}, u32[]{:S(2)}, u32[]{:S(2)}) collective-permute-start(bf16[16,2,48,128]{3,2,1,0:T(8,128)(2,1)S(1)} %collective-permute-done.3.refs_3_), channel_id=1, source_target_pairs={{0,16},{1,17},{2,18},{3,19},{4,20},{5,21},{6,22},{7,23},{8,24},{9,... | collective-permute-start | bytes 1179656 | tf_op jit(solution)/shard_map/ppermute | solution.py:169
  77.6 0.7 copy-start.3
  78.3 7.2 %copy-start.1 = (bf16[6144,192]{0,1:T(8,128)(2,1)S(1)}, bf16[6144,192]{0,1:T(8,128)(2,1)}, u32[]{:S(2)}) copy-start(bf16[6144,192]{0,1:T(8,128)(2,1)} %param.8) | copy-start | bytes 7077892
  78.3 7.2 %copy-start.2 = (bf16[1,128,192]{1,2,0:T(8,128)(2,1)S(1)}, bf16[1,128,192]{1,2,0:T(8,128)(2,1)}, u32[]{:S(2)}) copy-start(bf16[1,128,192]{1,2,0:T(8,128)(2,1)} %param.9) | copy-start | bytes 147460

commit v4 on v3

--- a/solution.py
+++ b/solution.py
@@ -1,5 +1,3 @@
-import functools
-
 import jax
 import jax.numpy as jnp
 from jax import lax
@@ -152,10 +150,9 @@
     other = lax.ppermute(own, AXES, swap_pairs())
     both = jnp.broadcast_to(jnp.stack([own, other])[None], (16, 2, 48, KEEP))
     both = lax.all_to_all(both, AXES, 0, 0, axis_index_groups=first_groups())
-    ahead = functools.partial(lax.ppermute, axis_name=AXES, perm=ring_pairs(1))
-    back = functools.partial(lax.ppermute, axis_name=AXES, perm=ring_pairs(-1))
-    f1, b1 = ahead(both), back(both)
-    f2, b2 = ahead(f1), back(b1)
+    move = lambda piece, step: lax.ppermute(piece, AXES, ring_pairs(step))
+    f2, b2 = move(both, 2), move(both, -2)
+    f1, b1 = move(both, 1), move(both, -1)
     gain_all = pl.pallas_call(
         spread_kernel,
         out_shape=jax.ShapeDtypeStruct((D, KEEP), F32),
@@ -165,8 +162,8 @@
         cost_estimate=pl.CostEstimate(flops=2 * 2**30, bytes_accessed=8 * 2**20, transcendentals=0),
         name="spread",
     )(b2, norm_gain.reshape(D // 128, 128))
-    f3, b3 = ahead(f2), back(b2)
-    f4 = ahead(f3)
+    f3, b3 = move(f2, 1), move(b2, -1)
+    f4 = move(f3, 1)
     pieces = (both, f1, f2, f3, f4, b1, b2, b3)
 
     hidden, payload = pl.pallas_call(

time: 113 us -> 110 us (0.973)
  waiting for transfers between devices: 16.5 us -> 13.6 us
  blocking collectives: 47.4 us -> 46.2 us
    ppermute x7, waiting for transfers between devices: 15.1 us -> 12.2 us  [shards(): move = lambda piece, step: lax.ppermute(piece, AXES, ring_pairs(step))]
  transfers between devices with their start and end apart: 8 -> 8, of which waited for: 5 -> 4; matrix products, arithmetic and copies ran while one was open for 0% -> 0% of each run, Pallas kernels for 1% -> 1%
where the time goes in v4:
time: 110 us; the launch traced here: 109 us
  blocking collectives  46.2 us (42%)
  starting transfers between devices  39.8 us (36%)
  waiting for transfers between devices  13.6 us (12%)
  Pallas kernels  6.45 us (6%)
  local copies, waits for them, and re-layouts  1.54 us (1%)
    ppermute x7, starting transfers between devices, shards(): move = lambda piece, step: lax.ppermute(piece, AXES, ring_pairs(step))  35.1 us
    all_to_all x1, blocking collectives, shards(): both = lax.all_to_all(both, AXES, 0, 0, axis_index_groups=first_groups())  25.5 us
    ppermute x7, waiting for transfers between devices, shards(): move = lambda piece, step: lax.ppermute(piece, AXES, ring_pairs(step))  12.2 us
    all_to_all x1, blocking collectives, shards(): lax.all_to_all(payload, 'dp', 0, 0, axis_index_groups=[[0, 2, 4, 6], [1,...  10.9 us
    all_gather x1, blocking collectives, shards(): lax.all_gather(payload, 'dp', axis_index_groups=[[0, 1], [2, 3], [4, 5],...  9.76 us
    ppermute x1, starting transfers between devices, shards(): other = lax.ppermute(own, AXES, swap_pairs())  4.7 us
    pallas_call x1, Pallas kernels, shards(): pl.pallas_call(forward_kernel, out_shape=(jax.ShapeDtypeStruct((192, KEEP...  2.98 us
    pallas_call x1, Pallas kernels, shards(): pl.pallas_call(grad_kernel, out_shape=jax.ShapeDtypeStruct((192, 768), F3...  2.61 us
  transfers between devices with their start and end apart: 8, of which 4 were waited for; matrix products, arithmetic and copies ran while one was open for 0% of the time, Pallas kernels for 1%

profile of v4, /device:TPU:1, one launch (start us, length us, event | category | flops | bytes accessed | tf_op | source)
XLA Modules:
  0.0 109.3 jit_solution(15626130348796940081)
XLA Ops:
  0.6 0.0 copy-start
  0.6 0.7 copy-done
  1.4 0.8 convolution_convert_fusion
  2.2 4.7 %collective-permute-start = (bf16[48,128]{1,0:T(8,128)(2,1)S(1)}, bf16[48,128]{1,0:T(8,128)(2,1)S(1)}, u32[]{:S(2)}, u32[]{:S(2)}) collective-permute-start(bf16[48,128]{1,0:T(8,128)(2,1)S(1)} %bitcast.26), channel_id=1, source_target_pairs={{0,0},{1,1},{2,2},{3,3},{4,4},{5,5},{6,6},{7,7},{8,8},{9,9},{10,10... | collective-permute-start | bytes 36872 | tf_op jit(solution)/shard_map/ppermute | solution.py:150
  6.9 1.4 %collective-permute-done = bf16[48,128]{1,0:T(8,128)(2,1)S(1)} collective-permute-done((bf16[48,128]{1,0:T(8,128)(2,1)S(1)}, bf16[48,128]{1,0:T(8,128)(2,1)S(1)}, u32[]{:S(2)}, u32[]{:S(2)}) %collective-permute-start) | collective-permute-done | bytes 12320 | tf_op jit(solution)/shard_map/ppermute | solution.py:150
  8.3 0.1 broadcast_in_dim.4
  8.3 25.5 %all_to_all.10.refs_0_ = bf16[16,2,48,128]{3,2,1,0:T(8,128)(2,1)S(1)} all-to-all(bf16[16,2,48,128]{3,2,1,0:T(8,128)(2,1)S(1)} %broadcast_in_dim.4), channel_id=1, replica_groups={{0,1,2,3,4,5,6,7,8,9,10,11,12,13,14,15},{16,17,18,19,20,21,22,23,24,25,..., dimensions={0} | all-to-all | bytes 786432 | tf_op jit(solution)/shard_map/all_to_all | solution.py:152
  33.8 7.6 %collective-permute-start.2 = (bf16[16,2,48,128]{3,2,1,0:T(8,128)(2,1)S(1)}, bf16[16,2,48,128]{3,2,1,0:T(8,128)(2,1)S(1)}, u32[]{:S(2)}, u32[]{:S(2)}) collective-permute-start(bf16[16,2,48,128]{3,2,1,0:T(8,128)(2,1)S(1)} %all_to_all.10.refs_0_), channel_id=1, source_target_pairs={{0,32},{1,33},{2,34},{3,35},{4,36},{5,37},{6,38},{7,39},{8,40},{9,... | collective-permute-start | bytes 1179656 | tf_op jit(solution)/shard_map/ppermute | solution.py:153
  41.5 10.4 %collective-permute-start.6 = (bf16[16,2,48,128]{3,2,1,0:T(8,128)(2,1)S(1)}, bf16[16,2,48,128]{3,2,1,0:T(8,128)(2,1)S(1)}, u32[]{:S(2)}, u32[]{:S(2)}) collective-permute-start(bf16[16,2,48,128]{3,2,1,0:T(8,128)(2,1)S(1)} %all_to_all.10.refs_0_), channel_id=1, source_target_pairs={{0,96},{1,97},{2,98},{3,99},{4,100},{5,101},{6,102},{7,103},{8,104... | collective-permute-start | bytes 1179656 | tf_op jit(solution)/shard_map/ppermute | solution.py:153
  51.9 5.9 %collective-permute-done.2.refs_2_ = bf16[16,2,48,128]{3,2,1,0:T(8,128)(2,1)S(1)} collective-permute-done((bf16[16,2,48,128]{3,2,1,0:T(8,128)(2,1)S(1)}, bf16[16,2,48,128]{3,2,1,0:T(8,128)(2,1)S(1)}, u32[]{:S(2)}, u32[]{:S(2)}) %collective-permute-start.2) | collective-permute-done | bytes 393248 | tf_op jit(solution)/shard_map/ppermute | solution.py:153
  57.8 4.6 %collective-permute-start.3 = (bf16[16,2,48,128]{3,2,1,0:T(8,128)(2,1)S(1)}, bf16[16,2,48,128]{3,2,1,0:T(8,128)(2,1)S(1)}, u32[]{:S(2)}, u32[]{:S(2)}) collective-permute-start(bf16[16,2,48,128]{3,2,1,0:T(8,128)(2,1)S(1)} %collective-permute-done.2.refs_2_), channel_id=1, source_target_pairs={{0,16},{1,17},{2,18},{3,19},{4,20},{5,21},{6,22},{7,23},{8,24},{9,... | collective-permute-start | bytes 1179656 | tf_op jit(solution)/shard_map/ppermute | solution.py:153
  62.4 4.0 %collective-permute-start.5 = (bf16[16,2,48,128]{3,2,1,0:T(8,128)(2,1)S(1)}, bf16[16,2,48,128]{3,2,1,0:T(8,128)(2,1)S(1)}, u32[]{:S(2)}, u32[]{:S(2)}) collective-permute-start(bf16[16,2,48,128]{3,2,1,0:T(8,128)(2,1)S(1)} %all_to_all.10.refs_0_), channel_id=1, source_target_pairs={{0,112},{1,113},{2,114},{3,115},{4,116},{5,117},{6,118},{7,119},{8... | collective-permute-start | bytes 1179656 | tf_op jit(solution)/shard_map/ppermute | solution.py:153
  66.4 1.9 %collective-permute-start.1 = (bf16[16,2,48,128]{3,2,1,0:T(8,128)(2,1)S(1)}, bf16[16,2,48,128]{3,2,1,0:T(8,128)(2,1)S(1)}, u32[]{:S(2)}, u32[]{:S(2)}) collective-permute-start(bf16[16,2,48,128]{3,2,1,0:T(8,128)(2,1)S(1)} %all_to_all.10.refs_0_), channel_id=1, source_target_pairs={{0,16},{1,17},{2,18},{3,19},{4,20},{5,21},{6,22},{7,23},{8,24},{9,... | collective-permute-start | bytes 1179656 | tf_op jit(solution)/shard_map/ppermute | solution.py:153
  68.4 4.6 %collective-permute-start.7 = (bf16[16,2,48,128]{3,2,1,0:T(8,128)(2,1)S(1)}, bf16[16,2,48,128]{3,2,1,0:T(8,128)(2,1)S(1)}, u32[]{:S(2)}, u32[]{:S(2)}) collective-permute-start(bf16[16,2,48,128]{3,2,1,0:T(8,128)(2,1)S(1)} %collective-permute-done.6.piece.refs_6_), channel_id=1, source_target_pairs={{0,112},{1,113},{2,114},{3,115},{4,116},{5,117},{6,118},{7,119},{8... | collective-permute-start | bytes 1179656 | tf_op jit(solution)/shard_map/ppermute | solution.py:153
  72.9 1.9 %collective-permute-start.4 = (bf16[16,2,48,128]{3,2,1,0:T(8,128)(2,1)S(1)}, bf16[16,2,48,128]{3,2,1,0:T(8,128)(2,1)S(1)}, u32[]{:S(2)}, u32[]{:S(2)}) collective-permute-start(bf16[16,2,48,128]{3,2,1,0:T(8,128)(2,1)S(1)} %collective-permute-done.3.refs_3_), channel_id=1, source_target_pairs={{0,16},{1,17},{2,18},{3,19},{4,20},{5,21},{6,22},{7,23},{8,24},{9,... | collective-permute-start | bytes 1179656 | tf_op jit(solution)/shard_map/ppermute | solution.py:153
  74.9 0.1 pad_add_fusion.where
  75.0 0.7 copy-done.3
  75.7 0.9 spread.1.refs_9_
  76.6 1.0 collective-permute-done.7.refs_7_
  77.6 5.3 %collective-permute-done.4.refs_4_ = bf16[16,2,48,128]{3,2,1,0:T(8,128)(2,1)S(1)} collective-permute-done((bf16[16,2,48,128]{3,2,1,0:T(8,128)(2,1)S(1)}, bf16[16,2,48,128]{3,2,1,0:T(8,128)(2,1)S(1)}, u32[]{:S(2)}, u32[]{:S(2)}) %collective-permute-start.4) | collective-permute-done | bytes 393248 | tf_op jit(solution)/shard_map/ppermute | solution.py:153
  83.0 3.0 %forward.1 = (bf16[192,128]{1,0:T(8,128)(2,1)}, bf16[4,208,128]{2,1,0:T(8,128)(2,1)S(1)}) custom-call(s32[3]{0:T(128)S(1)} %pad_add_fusion.where, bf16[16,2,48,128]{3,2,1,0:T(8,128)(2,1)S(1)} %all_to_all.10.refs_0_, bf16[16,2,48,128]{3,2,1,0:T(8,128)(2,1)S(1)} %collective-permute-done.1.refs_1_, bf16[16,2,48,128]{3,2,1,0:T(8,128)(2,1)S(1)} %collective-permute-done.2.refs_2_, ...), custom_call_target="tpu_custom_call" | custom-call | tf_op jit(solution)/shard_map/forward/pallas_call | solution.py:169
  86.0 10.9 %all_to_all.11 = bf16[4,208,128]{2,1,0:T(8,128)(2,1)S(1)} all-to-all(bf16[4,208,128]{2,1,0:T(8,128)(2,1)S(1)} %get-tuple-element.5), channel_id=1, replica_groups={{0,256,512,768},{128,384,640,896},{1,257,513,769},{129,385,641,897},{2,..., dimensions={0} | all-to-all | bytes 425984 | tf_op jit(solution)/shard_map/all_to_all | solution.py:179
  96.9 9.8 %all-gather = bf16[8,208,128]{2,1,0:T(8,128)(2,1)S(1)} all-gather(bf16[4,208,128]{2,1,0:T(8,128)(2,1)S(1)} %all_to_all.11), channel_id=2, replica_groups={{0,128},{256,384},{512,640},{768,896},{1,129},{257,385},{513,641},{769,..., dimensions={0}, use_global_device_ids=true | all-gather | bytes 638976 | tf_op jit(solution)/shard_map/all_gather | solution.py:180
  106.7 2.6 %weight_grad.1 = f32[192,768]{1,0:T(8,128)} custom-call(s32[3]{0:T(128)S(1)} %pad_add_fusion.where, bf16[16,2,48,128]{3,2,1,0:T(8,128)(2,1)S(1)} %all_to_all.10.refs_0_, bf16[16,2,48,128]{3,2,1,0:T(8,128)(2,1)S(1)} %collective-permute-done.1.refs_1_, bf16[16,2,48,128]{3,2,1,0:T(8,128)(2,1)S(1)} %collective-permute-done.2.refs_2_, ...), custom_call_target="tpu_custom_call" | custom-call | tf_op jit(solution)/shard_map/weight_grad/pallas_call | solution.py:182
  (10 shorter events, 0.0 us)
Async XLA Ops:
  0.6 0.7 copy-start
  2.2 6.1 %collective-permute-start = (bf16[48,128]{1,0:T(8,128)(2,1)S(1)}, bf16[48,128]{1,0:T(8,128)(2,1)S(1)}, u32[]{:S(2)}, u32[]{:S(2)}) collective-permute-start(bf16[48,128]{1,0:T(8,128)(2,1)S(1)} %bitcast.26), channel_id=1, source_target_pairs={{0,0},{1,1},{2,2},{3,3},{4,4},{5,5},{6,6},{7,7},{8,8},{9,9},{10,10... | collective-permute-start | bytes 36872 | tf_op jit(solution)/shard_map/ppermute | solution.py:150
  33.8 23.9 %collective-permute-start.2 = (bf16[16,2,48,128]{3,2,1,0:T(8,128)(2,1)S(1)}, bf16[16,2,48,128]{3,2,1,0:T(8,128)(2,1)S(1)}, u32[]{:S(2)}, u32[]{:S(2)}) collective-permute-start(bf16[16,2,48,128]{3,2,1,0:T(8,128)(2,1)S(1)} %all_to_all.10.refs_0_), channel_id=1, source_target_pairs={{0,32},{1,33},{2,34},{3,35},{4,36},{5,37},{6,38},{7,39},{8,40},{9,... | collective-permute-start | bytes 1179656 | tf_op jit(solution)/shard_map/ppermute | solution.py:153
  41.5 26.9 %collective-permute-start.6 = (bf16[16,2,48,128]{3,2,1,0:T(8,128)(2,1)S(1)}, bf16[16,2,48,128]{3,2,1,0:T(8,128)(2,1)S(1)}, u32[]{:S(2)}, u32[]{:S(2)}) collective-permute-start(bf16[16,2,48,128]{3,2,1,0:T(8,128)(2,1)S(1)} %all_to_all.10.refs_0_), channel_id=1, source_target_pairs={{0,96},{1,97},{2,98},{3,99},{4,100},{5,101},{6,102},{7,103},{8,104... | collective-permute-start | bytes 1179656 | tf_op jit(solution)/shard_map/ppermute | solution.py:153
  57.8 15.2 %collective-permute-start.3 = (bf16[16,2,48,128]{3,2,1,0:T(8,128)(2,1)S(1)}, bf16[16,2,48,128]{3,2,1,0:T(8,128)(2,1)S(1)}, u32[]{:S(2)}, u32[]{:S(2)}) collective-permute-start(bf16[16,2,48,128]{3,2,1,0:T(8,128)(2,1)S(1)} %collective-permute-done.2.refs_2_), channel_id=1, source_target_pairs={{0,16},{1,17},{2,18},{3,19},{4,20},{5,21},{6,22},{7,23},{8,24},{9,... | collective-permute-start | bytes 1179656 | tf_op jit(solution)/shard_map/ppermute | solution.py:153
  62.4 14.2 %collective-permute-start.5 = (bf16[16,2,48,128]{3,2,1,0:T(8,128)(2,1)S(1)}, bf16[16,2,48,128]{3,2,1,0:T(8,128)(2,1)S(1)}, u32[]{:S(2)}, u32[]{:S(2)}) collective-permute-start(bf16[16,2,48,128]{3,2,1,0:T(8,128)(2,1)S(1)} %all_to_all.10.refs_0_), channel_id=1, source_target_pairs={{0,112},{1,113},{2,114},{3,115},{4,116},{5,117},{6,118},{7,119},{8... | collective-permute-start | bytes 1179656 | tf_op jit(solution)/shard_map/ppermute | solution.py:153
  66.4 10.2 %collective-permute-start.1 = (bf16[16,2,48,128]{3,2,1,0:T(8,128)(2,1)S(1)}, bf16[16,2,48,128]{3,2,1,0:T(8,128)(2,1)S(1)}, u32[]{:S(2)}, u32[]{:S(2)}) collective-permute-start(bf16[16,2,48,128]{3,2,1,0:T(8,128)(2,1)S(1)} %all_to_all.10.refs_0_), channel_id=1, source_target_pairs={{0,16},{1,17},{2,18},{3,19},{4,20},{5,21},{6,22},{7,23},{8,24},{9,... | collective-permute-start | bytes 1179656 | tf_op jit(solution)/shard_map/ppermute | solution.py:153
  68.4 9.3 %collective-permute-start.7 = (bf16[16,2,48,128]{3,2,1,0:T(8,128)(2,1)S(1)}, bf16[16,2,48,128]{3,2,1,0:T(8,128)(2,1)S(1)}, u32[]{:S(2)}, u32[]{:S(2)}) collective-permute-start(bf16[16,2,48,128]{3,2,1,0:T(8,128)(2,1)S(1)} %collective-permute-done.6.piece.refs_6_), channel_id=1, source_target_pairs={{0,112},{1,113},{2,114},{3,115},{4,116},{5,117},{6,118},{7,119},{8... | collective-permute-start | bytes 1179656 | tf_op jit(solution)/shard_map/ppermute | solution.py:153
  72.9 10.0 %collective-permute-start.4 = (bf16[16,2,48,128]{3,2,1,0:T(8,128)(2,1)S(1)}, bf16[16,2,48,128]{3,2,1,0:T(8,128)(2,1)S(1)}, u32[]{:S(2)}, u32[]{:S(2)}) collective-permute-start(bf16[16,2,48,128]{3,2,1,0:T(8,128)(2,1)S(1)} %collective-permute-done.3.refs_3_), channel_id=1, source_target_pairs={{0,16},{1,17},{2,18},{3,19},{4,20},{5,21},{6,22},{7,23},{8,24},{9,... | collective-permute-start | bytes 1179656 | tf_op jit(solution)/shard_map/ppermute | solution.py:153
  75.0 0.7 copy-start.3
  75.7 7.2 %copy-start.1 = (bf16[6144,192]{0,1:T(8,128)(2,1)S(1)}, bf16[6144,192]{0,1:T(8,128)(2,1)}, u32[]{:S(2)}) copy-start(bf16[6144,192]{0,1:T(8,128)(2,1)} %param.8) | copy-start | bytes 7077892
  75.7 7.2 %copy-start.2 = (bf16[1,128,192]{1,2,0:T(8,128)(2,1)S(1)}, bf16[1,128,192]{1,2,0:T(8,128)(2,1)}, u32[]{:S(2)}) copy-start(bf16[1,128,192]{1,2,0:T(8,128)(2,1)} %param.9) | copy-start | bytes 147460

commit v5 on v4

--- a/solution.py
+++ b/solution.py
@@ -151,8 +151,8 @@
     both = jnp.broadcast_to(jnp.stack([own, other])[None], (16, 2, 48, KEEP))
     both = lax.all_to_all(both, AXES, 0, 0, axis_index_groups=first_groups())
     move = lambda piece, step: lax.ppermute(piece, AXES, ring_pairs(step))
-    f2, b2 = move(both, 2), move(both, -2)
-    f1, b1 = move(both, 1), move(both, -1)
+    f2, b1 = move(both, 2), move(both, -1)
+    f1, b2 = move(both, 1), move(b1, -1)
     gain_all = pl.pallas_call(
         spread_kernel,
         out_shape=jax.ShapeDtypeStruct((D, KEEP), F32),

time: 110 us -> 110 us (level)
  waiting for transfers between devices: 13.6 us -> 16.9 us
  blocking collectives: 46.2 us -> 44.1 us
    ppermute x7, waiting for transfers between devices: 12.2 us -> 15.5 us  [shards(): move = lambda piece, step: lax.ppermute(piece, AXES, ring_pairs(step))]
    all_gather x1, blocking collectives: 9.76 us -> 7.62 us  [shards(): lax.all_gather(payload, 'dp', axis_index_groups=[[0, 1], [2, 3], [4, 5],...]
  transfers between devices with their start and end apart: 8 -> 8, of which waited for: 4 -> 6; matrix products, arithmetic and copies ran while one was open for 0% -> 0% of each run, Pallas kernels for 1% -> 1%
where the time goes in v5:
time: 110 us
  blocking collectives  44.1 us (40%)
  starting transfers between devices  39.3 us (36%)
  waiting for transfers between devices  16.9 us (15%)
  Pallas kernels  6.45 us (6%)
  local copies, waits for them, and re-layouts  1.54 us (1%)
    ppermute x7, starting transfers between devices, shards(): move = lambda piece, step: lax.ppermute(piece, AXES, ring_pairs(step))  34.6 us
    all_to_all x1, blocking collectives, shards(): both = lax.all_to_all(both, AXES, 0, 0, axis_index_groups=first_groups())  25.5 us
    ppermute x7, waiting for transfers between devices, shards(): move = lambda piece, step: lax.ppermute(piece, AXES, ring_pairs(step))  15.5 us
    all_to_all x1, blocking collectives, shards(): lax.all_to_all(payload, 'dp', 0, 0, axis_index_groups=[[0, 2, 4, 6], [1,...  10.9 us
    all_gather x1, blocking collectives, shards(): lax.all_gather(payload, 'dp', axis_index_groups=[[0, 1], [2, 3], [4, 5],...  7.62 us
    ppermute x1, starting transfers between devices, shards(): other = lax.ppermute(own, AXES, swap_pairs())  4.7 us
    pallas_call x1, Pallas kernels, shards(): pl.pallas_call(forward_kernel, out_shape=(jax.ShapeDtypeStruct((192, KEEP...  2.98 us
    pallas_call x1, Pallas kernels, shards(): pl.pallas_call(grad_kernel, out_shape=jax.ShapeDtypeStruct((192, 768), F3...  2.61 us
  transfers between devices with their start and end apart: 8, of which 6 were waited for; matrix products, arithmetic and copies ran while one was open for 0% of the time, Pallas kernels for 1%

profile of v5, /device:TPU:1, one launch (start us, length us, event | category | flops | bytes accessed | tf_op | source)
XLA Modules:
  0.0 109.9 jit_solution(13068561057431800632)
XLA Ops:
  0.6 0.7 copy-done
  1.4 0.8 convolution_convert_fusion
  2.2 4.7 %collective-permute-start = (bf16[48,128]{1,0:T(8,128)(2,1)S(1)}, bf16[48,128]{1,0:T(8,128)(2,1)S(1)}, u32[]{:S(2)}, u32[]{:S(2)}) collective-permute-start(bf16[48,128]{1,0:T(8,128)(2,1)S(1)} %bitcast.26), channel_id=1, source_target_pairs={{0,0},{1,1},{2,2},{3,3},{4,4},{5,5},{6,6},{7,7},{8,8},{9,9},{10,10... | collective-permute-start | bytes 36872 | tf_op jit(solution)/shard_map/ppermute | solution.py:150
  6.9 1.4 %collective-permute-done = bf16[48,128]{1,0:T(8,128)(2,1)S(1)} collective-permute-done((bf16[48,128]{1,0:T(8,128)(2,1)S(1)}, bf16[48,128]{1,0:T(8,128)(2,1)S(1)}, u32[]{:S(2)}, u32[]{:S(2)}) %collective-permute-start) | collective-permute-done | bytes 12320 | tf_op jit(solution)/shard_map/ppermute | solution.py:150
  8.3 25.5 %all_to_all.10.refs_0_ = bf16[16,2,48,128]{3,2,1,0:T(8,128)(2,1)S(1)} all-to-all(bf16[16,2,48,128]{3,2,1,0:T(8,128)(2,1)S(1)} %broadcast_in_dim.4), channel_id=1, replica_groups={{0,1,2,3,4,5,6,7,8,9,10,11,12,13,14,15},{16,17,18,19,20,21,22,23,24,25,..., dimensions={0} | all-to-all | bytes 786432 | tf_op jit(solution)/shard_map/all_to_all | solution.py:152
  33.8 17.0 %collective-permute-start.5 = (bf16[16,2,48,128]{3,2,1,0:T(8,128)(2,1)S(1)}, bf16[16,2,48,128]{3,2,1,0:T(8,128)(2,1)S(1)}, u32[]{:S(2)}, u32[]{:S(2)}) collective-permute-start(bf16[16,2,48,128]{3,2,1,0:T(8,128)(2,1)S(1)} %all_to_all.10.refs_0_), channel_id=1, source_target_pairs={{0,112},{1,113},{2,114},{3,115},{4,116},{5,117},{6,118},{7,119},{8... | collective-permute-start | bytes 1179656 | tf_op jit(solution)/shard_map/ppermute | solution.py:153
  50.9 1.9 %collective-permute-start.2 = (bf16[16,2,48,128]{3,2,1,0:T(8,128)(2,1)S(1)}, bf16[16,2,48,128]{3,2,1,0:T(8,128)(2,1)S(1)}, u32[]{:S(2)}, u32[]{:S(2)}) collective-permute-start(bf16[16,2,48,128]{3,2,1,0:T(8,128)(2,1)S(1)} %all_to_all.10.refs_0_), channel_id=1, source_target_pairs={{0,32},{1,33},{2,34},{3,35},{4,36},{5,37},{6,38},{7,39},{8,40},{9,... | collective-permute-start | bytes 1179656 | tf_op jit(solution)/shard_map/ppermute | solution.py:153
  52.8 2.8 %collective-permute-done.5.refs_5_ = bf16[16,2,48,128]{3,2,1,0:T(8,128)(2,1)S(1)} collective-permute-done((bf16[16,2,48,128]{3,2,1,0:T(8,128)(2,1)S(1)}, bf16[16,2,48,128]{3,2,1,0:T(8,128)(2,1)S(1)}, u32[]{:S(2)}, u32[]{:S(2)}) %collective-permute-start.5) | collective-permute-done | bytes 393248 | tf_op jit(solution)/shard_map/ppermute | solution.py:153
  55.6 5.3 %collective-permute-start.6 = (bf16[16,2,48,128]{3,2,1,0:T(8,128)(2,1)S(1)}, bf16[16,2,48,128]{3,2,1,0:T(8,128)(2,1)S(1)}, u32[]{:S(2)}, u32[]{:S(2)}) collective-permute-start(bf16[16,2,48,128]{3,2,1,0:T(8,128)(2,1)S(1)} %collective-permute-done.5.refs_5_), channel_id=1, source_target_pairs={{0,112},{1,113},{2,114},{3,115},{4,116},{5,117},{6,118},{7,119},{8... | collective-permute-start | bytes 1179656 | tf_op jit(solution)/shard_map/ppermute | solution.py:153
  60.9 4.8 %collective-permute-done.2.refs_2_ = bf16[16,2,48,128]{3,2,1,0:T(8,128)(2,1)S(1)} collective-permute-done((bf16[16,2,48,128]{3,2,1,0:T(8,128)(2,1)S(1)}, bf16[16,2,48,128]{3,2,1,0:T(8,128)(2,1)S(1)}, u32[]{:S(2)}, u32[]{:S(2)}) %collective-permute-start.2) | collective-permute-done | bytes 393248 | tf_op jit(solution)/shard_map/ppermute | solution.py:153
  65.7 1.9 %collective-permute-start.3 = (bf16[16,2,48,128]{3,2,1,0:T(8,128)(2,1)S(1)}, bf16[16,2,48,128]{3,2,1,0:T(8,128)(2,1)S(1)}, u32[]{:S(2)}, u32[]{:S(2)}) collective-permute-start(bf16[16,2,48,128]{3,2,1,0:T(8,128)(2,1)S(1)} %collective-permute-done.2.refs_2_), channel_id=1, source_target_pairs={{0,16},{1,17},{2,18},{3,19},{4,20},{5,21},{6,22},{7,23},{8,24},{9,... | collective-permute-start | bytes 1179656 | tf_op jit(solution)/shard_map/ppermute | solution.py:153
  67.6 1.9 %collective-permute-start.1 = (bf16[16,2,48,128]{3,2,1,0:T(8,128)(2,1)S(1)}, bf16[16,2,48,128]{3,2,1,0:T(8,128)(2,1)S(1)}, u32[]{:S(2)}, u32[]{:S(2)}) collective-permute-start(bf16[16,2,48,128]{3,2,1,0:T(8,128)(2,1)S(1)} %all_to_all.10.refs_0_), channel_id=1, source_target_pairs={{0,16},{1,17},{2,18},{3,19},{4,20},{5,21},{6,22},{7,23},{8,24},{9,... | collective-permute-start | bytes 1179656 | tf_op jit(solution)/shard_map/ppermute | solution.py:153
  69.5 4.6 %collective-permute-start.7 = (bf16[16,2,48,128]{3,2,1,0:T(8,128)(2,1)S(1)}, bf16[16,2,48,128]{3,2,1,0:T(8,128)(2,1)S(1)}, u32[]{:S(2)}, u32[]{:S(2)}) collective-permute-start(bf16[16,2,48,128]{3,2,1,0:T(8,128)(2,1)S(1)} %collective-permute-done.6.piece.refs_6_), channel_id=1, source_target_pairs={{0,112},{1,113},{2,114},{3,115},{4,116},{5,117},{6,118},{7,119},{8... | collective-permute-start | bytes 1179656 | tf_op jit(solution)/shard_map/ppermute | solution.py:153
  74.1 1.6 %collective-permute-done.3.refs_3_ = bf16[16,2,48,128]{3,2,1,0:T(8,128)(2,1)S(1)} collective-permute-done((bf16[16,2,48,128]{3,2,1,0:T(8,128)(2,1)S(1)}, bf16[16,2,48,128]{3,2,1,0:T(8,128)(2,1)S(1)}, u32[]{:S(2)}, u32[]{:S(2)}) %collective-permute-start.3) | collective-permute-done | bytes 393248 | tf_op jit(solution)/shard_map/ppermute | solution.py:153
  75.7 1.9 %collective-permute-start.4 = (bf16[16,2,48,128]{3,2,1,0:T(8,128)(2,1)S(1)}, bf16[16,2,48,128]{3,2,1,0:T(8,128)(2,1)S(1)}, u32[]{:S(2)}, u32[]{:S(2)}) collective-permute-start(bf16[16,2,48,128]{3,2,1,0:T(8,128)(2,1)S(1)} %collective-permute-done.3.refs_3_), channel_id=1, source_target_pairs={{0,16},{1,17},{2,18},{3,19},{4,20},{5,21},{6,22},{7,23},{8,24},{9,... | collective-permute-start | bytes 1179656 | tf_op jit(solution)/shard_map/ppermute | solution.py:153
  77.6 0.1 pad_add_fusion.where
  77.7 0.7 copy-done.3
  78.5 0.9 spread.1.refs_9_
  79.3 0.4 collective-permute-done.1.refs_1_
  79.7 6.0 %collective-permute-done.4.refs_4_ = bf16[16,2,48,128]{3,2,1,0:T(8,128)(2,1)S(1)} collective-permute-done((bf16[16,2,48,128]{3,2,1,0:T(8,128)(2,1)S(1)}, bf16[16,2,48,128]{3,2,1,0:T(8,128)(2,1)S(1)}, u32[]{:S(2)}, u32[]{:S(2)}) %collective-permute-start.4) | collective-permute-done | bytes 393248 | tf_op jit(solution)/shard_map/ppermute | solution.py:153
  85.7 3.0 %forward.1 = (bf16[192,128]{1,0:T(8,128)(2,1)}, bf16[4,208,128]{2,1,0:T(8,128)(2,1)S(1)}) custom-call(s32[3]{0:T(128)S(1)} %pad_add_fusion.where, bf16[16,2,48,128]{3,2,1,0:T(8,128)(2,1)S(1)} %all_to_all.10.refs_0_, bf16[16,2,48,128]{3,2,1,0:T(8,128)(2,1)S(1)} %collective-permute-done.1.refs_1_, bf16[16,2,48,128]{3,2,1,0:T(8,128)(2,1)S(1)} %collective-permute-done.2.refs_2_, ...), custom_call_target="tpu_custom_call" | custom-call | tf_op jit(solution)/shard_map/forward/pallas_call | solution.py:169
  88.7 10.9 %all_to_all.11 = bf16[4,208,128]{2,1,0:T(8,128)(2,1)S(1)} all-to-all(bf16[4,208,128]{2,1,0:T(8,128)(2,1)S(1)} %get-tuple-element.5), channel_id=1, replica_groups={{0,256,512,768},{128,384,640,896},{1,257,513,769},{129,385,641,897},{2,..., dimensions={0} | all-to-all | bytes 425984 | tf_op jit(solution)/shard_map/all_to_all | solution.py:179
  99.6 7.6 %all-gather = bf16[8,208,128]{2,1,0:T(8,128)(2,1)S(1)} all-gather(bf16[4,208,128]{2,1,0:T(8,128)(2,1)S(1)} %all_to_all.11), channel_id=2, replica_groups={{0,128},{256,384},{512,640},{768,896},{1,129},{257,385},{513,641},{769,..., dimensions={0}, use_global_device_ids=true | all-gather | bytes 638976 | tf_op jit(solution)/shard_map/all_gather | solution.py:180
  107.2 2.6 %weight_grad.1 = f32[192,768]{1,0:T(8,128)} custom-call(s32[3]{0:T(128)S(1)} %pad_add_fusion.where, bf16[16,2,48,128]{3,2,1,0:T(8,128)(2,1)S(1)} %all_to_all.10.refs_0_, bf16[16,2,48,128]{3,2,1,0:T(8,128)(2,1)S(1)} %collective-permute-done.1.refs_1_, bf16[16,2,48,128]{3,2,1,0:T(8,128)(2,1)S(1)} %collective-permute-done.2.refs_2_, ...), custom_call_target="tpu_custom_call" | custom-call | tf_op jit(solution)/shard_map/weight_grad/pallas_call | solution.py:182
  (10 shorter events, 0.1 us)
Async XLA Ops:
  0.6 0.7 copy-start
  2.2 6.1 %collective-permute-start = (bf16[48,128]{1,0:T(8,128)(2,1)S(1)}, bf16[48,128]{1,0:T(8,128)(2,1)S(1)}, u32[]{:S(2)}, u32[]{:S(2)}) collective-permute-start(bf16[48,128]{1,0:T(8,128)(2,1)S(1)} %bitcast.26), channel_id=1, source_target_pairs={{0,0},{1,1},{2,2},{3,3},{4,4},{5,5},{6,6},{7,7},{8,8},{9,9},{10,10... | collective-permute-start | bytes 36872 | tf_op jit(solution)/shard_map/ppermute | solution.py:150
  33.8 21.7 %collective-permute-start.5 = (bf16[16,2,48,128]{3,2,1,0:T(8,128)(2,1)S(1)}, bf16[16,2,48,128]{3,2,1,0:T(8,128)(2,1)S(1)}, u32[]{:S(2)}, u32[]{:S(2)}) collective-permute-start(bf16[16,2,48,128]{3,2,1,0:T(8,128)(2,1)S(1)} %all_to_all.10.refs_0_), channel_id=1, source_target_pairs={{0,112},{1,113},{2,114},{3,115},{4,116},{5,117},{6,118},{7,119},{8... | collective-permute-start | bytes 1179656 | tf_op jit(solution)/shard_map/ppermute | solution.py:153
  50.9 14.8 %collective-permute-start.2 = (bf16[16,2,48,128]{3,2,1,0:T(8,128)(2,1)S(1)}, bf16[16,2,48,128]{3,2,1,0:T(8,128)(2,1)S(1)}, u32[]{:S(2)}, u32[]{:S(2)}) collective-permute-start(bf16[16,2,48,128]{3,2,1,0:T(8,128)(2,1)S(1)} %all_to_all.10.refs_0_), channel_id=1, source_target_pairs={{0,32},{1,33},{2,34},{3,35},{4,36},{5,37},{6,38},{7,39},{8,40},{9,... | collective-permute-start | bytes 1179656 | tf_op jit(solution)/shard_map/ppermute | solution.py:153
  55.6 13.9 %collective-permute-start.6 = (bf16[16,2,48,128]{3,2,1,0:T(8,128)(2,1)S(1)}, bf16[16,2,48,128]{3,2,1,0:T(8,128)(2,1)S(1)}, u32[]{:S(2)}, u32[]{:S(2)}) collective-permute-start(bf16[16,2,48,128]{3,2,1,0:T(8,128)(2,1)S(1)} %collective-permute-done.5.refs_5_), channel_id=1, source_target_pairs={{0,112},{1,113},{2,114},{3,115},{4,116},{5,117},{6,118},{7,119},{8... | collective-permute-start | bytes 1179656 | tf_op jit(solution)/shard_map/ppermute | solution.py:153
  65.7 10.0 %collective-permute-start.3 = (bf16[16,2,48,128]{3,2,1,0:T(8,128)(2,1)S(1)}, bf16[16,2,48,128]{3,2,1,0:T(8,128)(2,1)S(1)}, u32[]{:S(2)}, u32[]{:S(2)}) collective-permute-start(bf16[16,2,48,128]{3,2,1,0:T(8,128)(2,1)S(1)} %collective-permute-done.2.refs_2_), channel_id=1, source_target_pairs={{0,16},{1,17},{2,18},{3,19},{4,20},{5,21},{6,22},{7,23},{8,24},{9,... | collective-permute-start | bytes 1179656 | tf_op jit(solution)/shard_map/ppermute | solution.py:153
  67.6 12.2 %collective-permute-start.1 = (bf16[16,2,48,128]{3,2,1,0:T(8,128)(2,1)S(1)}, bf16[16,2,48,128]{3,2,1,0:T(8,128)(2,1)S(1)}, u32[]{:S(2)}, u32[]{:S(2)}) collective-permute-start(bf16[16,2,48,128]{3,2,1,0:T(8,128)(2,1)S(1)} %all_to_all.10.refs_0_), channel_id=1, source_target_pairs={{0,16},{1,17},{2,18},{3,19},{4,20},{5,21},{6,22},{7,23},{8,24},{9,... | collective-permute-start | bytes 1179656 | tf_op jit(solution)/shard_map/ppermute | solution.py:153
  69.5 10.2 %collective-permute-start.7 = (bf16[16,2,48,128]{3,2,1,0:T(8,128)(2,1)S(1)}, bf16[16,2,48,128]{3,2,1,0:T(8,128)(2,1)S(1)}, u32[]{:S(2)}, u32[]{:S(2)}) collective-permute-start(bf16[16,2,48,128]{3,2,1,0:T(8,128)(2,1)S(1)} %collective-permute-done.6.piece.refs_6_), channel_id=1, source_target_pairs={{0,112},{1,113},{2,114},{3,115},{4,116},{5,117},{6,118},{7,119},{8... | collective-permute-start | bytes 1179656 | tf_op jit(solution)/shard_map/ppermute | solution.py:153
  75.7 10.0 %collective-permute-start.4 = (bf16[16,2,48,128]{3,2,1,0:T(8,128)(2,1)S(1)}, bf16[16,2,48,128]{3,2,1,0:T(8,128)(2,1)S(1)}, u32[]{:S(2)}, u32[]{:S(2)}) collective-permute-start(bf16[16,2,48,128]{3,2,1,0:T(8,128)(2,1)S(1)} %collective-permute-done.3.refs_3_), channel_id=1, source_target_pairs={{0,16},{1,17},{2,18},{3,19},{4,20},{5,21},{6,22},{7,23},{8,24},{9,... | collective-permute-start | bytes 1179656 | tf_op jit(solution)/shard_map/ppermute | solution.py:153
  77.7 0.7 copy-start.3
  78.5 7.2 %copy-start.1 = (bf16[6144,192]{0,1:T(8,128)(2,1)S(1)}, bf16[6144,192]{0,1:T(8,128)(2,1)}, u32[]{:S(2)}) copy-start(bf16[6144,192]{0,1:T(8,128)(2,1)} %param.8) | copy-start | bytes 7077892
  78.5 7.2 %copy-start.2 = (bf16[1,128,192]{1,2,0:T(8,128)(2,1)S(1)}, bf16[1,128,192]{1,2,0:T(8,128)(2,1)}, u32[]{:S(2)}) copy-start(bf16[1,128,192]{1,2,0:T(8,128)(2,1)} %param.9) | copy-start | bytes 147460

commit v6 on v4

--- a/solution.py
+++ b/solution.py
@@ -64,11 +64,11 @@
 
 
 def tiles(me, pieces, part):
-    for shift, ref in zip((0, -1, -2, -3, -4, 1, 2, 3), pieces):
+    for shift, ref, places in zip((0, -1, -2, -3, 1, 2, 3, 4, 4), pieces, [range(8)] * 7 + [range(4), range(4, 8)]):
         ring = lax.rem(me + (shift + 8), 8)
-        for j in range(8):
+        for j in places:
             for half in range(2):
-                yield ref.at[2 * j + half, part], ring, j, half
+                yield ref.at[2 * (j - places[0]) + half, part], ring, j, half
 
 
 def spread_kernel(piece, gain, spread):
@@ -77,8 +77,8 @@
 
 
 def forward_kernel(where, *refs):
-    pieces = refs[:8]
-    weight, gain, hidden_grad, hidden, payload, rows = refs[8:]
+    pieces = refs[:9]
+    weight, gain, hidden_grad, hidden, payload, rows = refs[9:]
     on_y = where[0] == 0
     total = jnp.zeros((8, KEEP), F32)
     for tile, ring, j, half in tiles(where[1], pieces, 0):
@@ -115,8 +115,8 @@
 
 
 def grad_kernel(where, *refs):
-    pieces = refs[:8]
-    payload, gain, out, normed, slopes, averages, scales = refs[8:]
+    pieces = refs[:9]
+    payload, gain, out, normed, slopes, averages, scales = refs[9:]
     first = where[2] * 768
     on_y = where[0] == 0
     for image in range(8):
@@ -163,13 +163,13 @@
         name="spread",
     )(b2, norm_gain.reshape(D // 128, 128))
     f3, b3 = move(f2, 1), move(b2, -1)
-    f4 = move(f3, 1)
-    pieces = (both, f1, f2, f3, f4, b1, b2, b3)
+    f4, b4 = move(f2[:8], 2), move(b2[8:], -2)
+    pieces = (both, f1, f2, f3, b1, b2, b3, f4, b4)
 
     hidden, payload = pl.pallas_call(
         forward_kernel,
         out_shape=(jax.ShapeDtypeStruct((192, KEEP), BF), jax.ShapeDtypeStruct((4, 208, KEEP), BF)),
-        in_specs=[SMEM] + [VMEM] * 11,
+        in_specs=[SMEM] + [VMEM] * 12,
         out_specs=(VMEM, VMEM),
         scratch_shapes=[pltpu.VMEM((D, KEEP), BF)],
         compiler_params=pltpu.CompilerParams(vmem_limit_bytes=24 * 2**20),
@@ -182,7 +182,7 @@
     grad = pl.pallas_call(
         grad_kernel,
         out_shape=jax.ShapeDtypeStruct((192, 768), F32),
-        in_specs=[SMEM] + [VMEM] * 10,
+        in_specs=[SMEM] + [VMEM] * 11,
         out_specs=VMEM,
         scratch_shapes=[
             pltpu.VMEM((768, 1024), BF),

time: 110 us -> 107 us (0.973)
  waiting for transfers between devices: 13.6 us -> 8.16 us
  starting transfers between devices: 39.8 us -> 43.7 us
    ppermute x7 -> x8, waiting for transfers between devices: 12.2 us -> 6.8 us  [shards(): move = lambda piece, step: lax.ppermute(piece, AXES, ring_pairs(step))]
    ppermute x7 -> x8, starting transfers between devices: 35.1 us -> 39 us  [shards(): move = lambda piece, step: lax.ppermute(piece, AXES, ring_pairs(step))]
  transfers between devices with their start and end apart: 8 -> 9, of which waited for: 4 -> 4; matrix products, arithmetic and copies ran while one was open for 0% -> 0% of each run, Pallas kernels for 1% -> 1%
where the time goes in v6:
time: 107 us
  blocking collectives  45.2 us (42%)
  starting transfers between devices  43.7 us (41%)
  waiting for transfers between devices  8.16 us (8%)
  Pallas kernels  6.46 us (6%)
  local copies, waits for them, and re-layouts  1.56 us (1%)
    ppermute x8, starting transfers between devices, shards(): move = lambda piece, step: lax.ppermute(piece, AXES, ring_pairs(step))  39 us
    all_to_all x1, blocking collectives, shards(): both = lax.all_to_all(both, AXES, 0, 0, axis_index_groups=first_groups())  25.5 us
    all_to_all x1, blocking collectives, shards(): lax.all_to_all(payload, 'dp', 0, 0, axis_index_groups=[[0, 2, 4, 6], [1,...  10.9 us
    all_gather x1, blocking collectives, shards(): lax.all_gather(payload, 'dp', axis_index_groups=[[0, 1], [2, 3], [4, 5],...  8.69 us
    ppermute x8, waiting for transfers between devices, shards(): move = lambda piece, step: lax.ppermute(piece, AXES, ring_pairs(step))  6.8 us
    ppermute x1, starting transfers between devices, shards(): other = lax.ppermute(own, AXES, swap_pairs())  4.7 us
    pallas_call x1, Pallas kernels, shards(): pl.pallas_call(forward_kernel, out_shape=(jax.ShapeDtypeStruct((192, KEEP...  2.98 us
    pallas_call x1, Pallas kernels, shards(): pl.pallas_call(grad_kernel, out_shape=jax.ShapeDtypeStruct((192, 768), F3...  2.62 us
  transfers between devices with their start and end apart: 9, of which 4 were waited for; matrix products, arithmetic and copies ran while one was open for 0% of the time, Pallas kernels for 1%

profile of v6, /device:TPU:1, one launch (start us, length us, event | category | flops | bytes accessed | tf_op | source)
XLA Modules:
  0.0 106.8 jit_solution(4939324286924516570)
XLA Ops:
  0.6 0.7 copy-done
  1.4 0.8 convolution_convert_fusion
  2.2 4.7 %collective-permute-start = (bf16[48,128]{1,0:T(8,128)(2,1)S(1)}, bf16[48,128]{1,0:T(8,128)(2,1)S(1)}, u32[]{:S(2)}, u32[]{:S(2)}) collective-permute-start(bf16[48,128]{1,0:T(8,128)(2,1)S(1)} %bitcast.26), channel_id=1, source_target_pairs={{0,0},{1,1},{2,2},{3,3},{4,4},{5,5},{6,6},{7,7},{8,8},{9,9},{10,10... | collective-permute-start | bytes 36872 | tf_op jit(solution)/shard_map/ppermute | solution.py:150
  6.9 1.4 %collective-permute-done = bf16[48,128]{1,0:T(8,128)(2,1)S(1)} collective-permute-done((bf16[48,128]{1,0:T(8,128)(2,1)S(1)}, bf16[48,128]{1,0:T(8,128)(2,1)S(1)}, u32[]{:S(2)}, u32[]{:S(2)}) %collective-permute-start) | collective-permute-done | bytes 12320 | tf_op jit(solution)/shard_map/ppermute | solution.py:150
  8.3 0.1 broadcast_in_dim.4
  8.3 25.5 %all_to_all.10.refs_0_ = bf16[16,2,48,128]{3,2,1,0:T(8,128)(2,1)S(1)} all-to-all(bf16[16,2,48,128]{3,2,1,0:T(8,128)(2,1)S(1)} %broadcast_in_dim.4), channel_id=1, replica_groups={{0,1,2,3,4,5,6,7,8,9,10,11,12,13,14,15},{16,17,18,19,20,21,22,23,24,25,..., dimensions={0} | all-to-all | bytes 786432 | tf_op jit(solution)/shard_map/all_to_all | solution.py:152
  33.8 16.1 %collective-permute-start.5 = (bf16[16,2,48,128]{3,2,1,0:T(8,128)(2,1)S(1)}, bf16[16,2,48,128]{3,2,1,0:T(8,128)(2,1)S(1)}, u32[]{:S(2)}, u32[]{:S(2)}) collective-permute-start(bf16[16,2,48,128]{3,2,1,0:T(8,128)(2,1)S(1)} %all_to_all.10.refs_0_), channel_id=1, source_target_pairs={{0,96},{1,97},{2,98},{3,99},{4,100},{5,101},{6,102},{7,103},{8,104... | collective-permute-start | bytes 1179656 | tf_op jit(solution)/shard_map/ppermute | solution.py:153
  49.9 1.9 %collective-permute-start.2 = (bf16[16,2,48,128]{3,2,1,0:T(8,128)(2,1)S(1)}, bf16[16,2,48,128]{3,2,1,0:T(8,128)(2,1)S(1)}, u32[]{:S(2)}, u32[]{:S(2)}) collective-permute-start(bf16[16,2,48,128]{3,2,1,0:T(8,128)(2,1)S(1)} %all_to_all.10.refs_0_), channel_id=1, source_target_pairs={{0,32},{1,33},{2,34},{3,35},{4,36},{5,37},{6,38},{7,39},{8,40},{9,... | collective-permute-start | bytes 1179656 | tf_op jit(solution)/shard_map/ppermute | solution.py:153
  51.9 6.4 %collective-permute-start.4 = (bf16[16,2,48,128]{3,2,1,0:T(8,128)(2,1)S(1)}, bf16[16,2,48,128]{3,2,1,0:T(8,128)(2,1)S(1)}, u32[]{:S(2)}, u32[]{:S(2)}) collective-permute-start(bf16[16,2,48,128]{3,2,1,0:T(8,128)(2,1)S(1)} %all_to_all.10.refs_0_), channel_id=1, source_target_pairs={{0,112},{1,113},{2,114},{3,115},{4,116},{5,117},{6,118},{7,119},{8... | collective-permute-start | bytes 1179656 | tf_op jit(solution)/shard_map/ppermute | solution.py:153
  58.3 1.9 %collective-permute-start.1 = (bf16[16,2,48,128]{3,2,1,0:T(8,128)(2,1)S(1)}, bf16[16,2,48,128]{3,2,1,0:T(8,128)(2,1)S(1)}, u32[]{:S(2)}, u32[]{:S(2)}) collective-permute-start(bf16[16,2,48,128]{3,2,1,0:T(8,128)(2,1)S(1)} %all_to_all.10.refs_0_), channel_id=1, source_target_pairs={{0,16},{1,17},{2,18},{3,19},{4,20},{5,21},{6,22},{7,23},{8,24},{9,... | collective-permute-start | bytes 1179656 | tf_op jit(solution)/shard_map/ppermute | solution.py:153
  60.2 4.6 %collective-permute-start.6 = (bf16[16,2,48,128]{3,2,1,0:T(8,128)(2,1)S(1)}, bf16[16,2,48,128]{3,2,1,0:T(8,128)(2,1)S(1)}, u32[]{:S(2)}, u32[]{:S(2)}) collective-permute-start(bf16[16,2,48,128]{3,2,1,0:T(8,128)(2,1)S(1)} %collective-permute-done.5.piece.refs_5_), channel_id=1, source_target_pairs={{0,112},{1,113},{2,114},{3,115},{4,116},{5,117},{6,118},{7,119},{8... | collective-permute-start | bytes 1179656 | tf_op jit(solution)/shard_map/ppermute | solution.py:153
  64.8 0.3 collective-permute-done.2.refs_2_
  65.1 1.9 %collective-permute-start.3 = (bf16[16,2,48,128]{3,2,1,0:T(8,128)(2,1)S(1)}, bf16[16,2,48,128]{3,2,1,0:T(8,128)(2,1)S(1)}, u32[]{:S(2)}, u32[]{:S(2)}) collective-permute-start(bf16[16,2,48,128]{3,2,1,0:T(8,128)(2,1)S(1)} %collective-permute-done.2.refs_2_), channel_id=1, source_target_pairs={{0,16},{1,17},{2,18},{3,19},{4,20},{5,21},{6,22},{7,23},{8,24},{9,... | collective-permute-start | bytes 1179656 | tf_op jit(solution)/shard_map/ppermute | solution.py:153
  67.0 0.1 pad_add_fusion.where
  67.1 3.4 %collective-permute-start.8 = (bf16[8,2,48,128]{3,2,1,0:T(8,128)(2,1)S(1)}, bf16[8,2,48,128]{3,2,1,0:T(8,128)(2,1)S(1)}, u32[]{:S(2)}, u32[]{:S(2)}) collective-permute-start(bf16[8,2,48,128]{3,2,1,0:T(8,128)(2,1)S(1)} %slice.9), channel_id=1, source_target_pairs={{0,96},{1,97},{2,98},{3,99},{4,100},{5,101},{6,102},{7,103},{8,104... | collective-permute-start | bytes 589832 | tf_op jit(solution)/shard_map/ppermute | solution.py:153
  70.6 2.8 %collective-permute-start.7 = (bf16[8,2,48,128]{3,2,1,0:T(8,128)(2,1)S(1)}, bf16[8,2,48,128]{3,2,1,0:T(8,128)(2,1)S(1)}, u32[]{:S(2)}, u32[]{:S(2)}) collective-permute-start(bf16[8,2,48,128]{3,2,1,0:T(8,128)(2,1)S(1)} %slice.8), channel_id=1, source_target_pairs={{0,32},{1,33},{2,34},{3,35},{4,36},{5,37},{6,38},{7,39},{8,40},{9,... | collective-permute-start | bytes 589832 | tf_op jit(solution)/shard_map/ppermute | solution.py:153
  73.4 0.7 copy-done.3
  74.1 0.9 spread.1.refs_10_
  75.0 0.9 collective-permute-done.8.refs_8_
  75.8 5.6 %collective-permute-done.7.refs_7_ = bf16[8,2,48,128]{3,2,1,0:T(8,128)(2,1)S(1)} collective-permute-done((bf16[8,2,48,128]{3,2,1,0:T(8,128)(2,1)S(1)}, bf16[8,2,48,128]{3,2,1,0:T(8,128)(2,1)S(1)}, u32[]{:S(2)}, u32[]{:S(2)}) %collective-permute-start.7) | collective-permute-done | bytes 196640 | tf_op jit(solution)/shard_map/ppermute | solution.py:153
  81.5 3.0 %forward.1 = (bf16[192,128]{1,0:T(8,128)(2,1)}, bf16[4,208,128]{2,1,0:T(8,128)(2,1)S(1)}) custom-call(s32[3]{0:T(128)S(1)} %pad_add_fusion.where, bf16[16,2,48,128]{3,2,1,0:T(8,128)(2,1)S(1)} %all_to_all.10.refs_0_, bf16[16,2,48,128]{3,2,1,0:T(8,128)(2,1)S(1)} %collective-permute-done.1.refs_1_, bf16[16,2,48,128]{3,2,1,0:T(8,128)(2,1)S(1)} %collective-permute-done.2.refs_2_, ...), custom_call_target="tpu_custom_call" | custom-call | tf_op jit(solution)/shard_map/forward/pallas_call | solution.py:169
  84.5 10.9 %all_to_all.11 = bf16[4,208,128]{2,1,0:T(8,128)(2,1)S(1)} all-to-all(bf16[4,208,128]{2,1,0:T(8,128)(2,1)S(1)} %get-tuple-element.5), channel_id=1, replica_groups={{0,256,512,768},{128,384,640,896},{1,257,513,769},{129,385,641,897},{2,..., dimensions={0} | all-to-all | bytes 425984 | tf_op jit(solution)/shard_map/all_to_all | solution.py:179
  95.4 8.7 %all-gather = bf16[8,208,128]{2,1,0:T(8,128)(2,1)S(1)} all-gather(bf16[4,208,128]{2,1,0:T(8,128)(2,1)S(1)} %all_to_all.11), channel_id=2, replica_groups={{0,128},{256,384},{512,640},{768,896},{1,129},{257,385},{513,641},{769,..., dimensions={0}, use_global_device_ids=true | all-gather | bytes 638976 | tf_op jit(solution)/shard_map/all_gather | solution.py:180
  104.1 2.6 %weight_grad.1 = f32[192,768]{1,0:T(8,128)} custom-call(s32[3]{0:T(128)S(1)} %pad_add_fusion.where, bf16[16,2,48,128]{3,2,1,0:T(8,128)(2,1)S(1)} %all_to_all.10.refs_0_, bf16[16,2,48,128]{3,2,1,0:T(8,128)(2,1)S(1)} %collective-permute-done.1.refs_1_, bf16[16,2,48,128]{3,2,1,0:T(8,128)(2,1)S(1)} %collective-permute-done.2.refs_2_, ...), custom_call_target="tpu_custom_call" | custom-call | tf_op jit(solution)/shard_map/weight_grad/pallas_call | solution.py:182
  (14 shorter events, 0.1 us)
Async XLA Ops:
  0.6 0.7 copy-start
  2.2 6.1 %collective-permute-start = (bf16[48,128]{1,0:T(8,128)(2,1)S(1)}, bf16[48,128]{1,0:T(8,128)(2,1)S(1)}, u32[]{:S(2)}, u32[]{:S(2)}) collective-permute-start(bf16[48,128]{1,0:T(8,128)(2,1)S(1)} %bitcast.26), channel_id=1, source_target_pairs={{0,0},{1,1},{2,2},{3,3},{4,4},{5,5},{6,6},{7,7},{8,8},{9,9},{10,10... | collective-permute-start | bytes 36872 | tf_op jit(solution)/shard_map/ppermute | solution.py:150
  33.8 26.4 %collective-permute-start.5 = (bf16[16,2,48,128]{3,2,1,0:T(8,128)(2,1)S(1)}, bf16[16,2,48,128]{3,2,1,0:T(8,128)(2,1)S(1)}, u32[]{:S(2)}, u32[]{:S(2)}) collective-permute-start(bf16[16,2,48,128]{3,2,1,0:T(8,128)(2,1)S(1)} %all_to_all.10.refs_0_), channel_id=1, source_target_pairs={{0,96},{1,97},{2,98},{3,99},{4,100},{5,101},{6,102},{7,103},{8,104... | collective-permute-start | bytes 1179656 | tf_op jit(solution)/shard_map/ppermute | solution.py:153
  49.9 15.1 %collective-permute-start.2 = (bf16[16,2,48,128]{3,2,1,0:T(8,128)(2,1)S(1)}, bf16[16,2,48,128]{3,2,1,0:T(8,128)(2,1)S(1)}, u32[]{:S(2)}, u32[]{:S(2)}) collective-permute-start(bf16[16,2,48,128]{3,2,1,0:T(8,128)(2,1)S(1)} %all_to_all.10.refs_0_), channel_id=1, source_target_pairs={{0,32},{1,33},{2,34},{3,35},{4,36},{5,37},{6,38},{7,39},{8,40},{9,... | collective-permute-start | bytes 1179656 | tf_op jit(solution)/shard_map/ppermute | solution.py:153
  51.9 18.7 %collective-permute-start.4 = (bf16[16,2,48,128]{3,2,1,0:T(8,128)(2,1)S(1)}, bf16[16,2,48,128]{3,2,1,0:T(8,128)(2,1)S(1)}, u32[]{:S(2)}, u32[]{:S(2)}) collective-permute-start(bf16[16,2,48,128]{3,2,1,0:T(8,128)(2,1)S(1)} %all_to_all.10.refs_0_), channel_id=1, source_target_pairs={{0,112},{1,113},{2,114},{3,115},{4,116},{5,117},{6,118},{7,119},{8... | collective-permute-start | bytes 1179656 | tf_op jit(solution)/shard_map/ppermute | solution.py:153
  58.3 16.7 %collective-permute-start.1 = (bf16[16,2,48,128]{3,2,1,0:T(8,128)(2,1)S(1)}, bf16[16,2,48,128]{3,2,1,0:T(8,128)(2,1)S(1)}, u32[]{:S(2)}, u32[]{:S(2)}) collective-permute-start(bf16[16,2,48,128]{3,2,1,0:T(8,128)(2,1)S(1)} %all_to_all.10.refs_0_), channel_id=1, source_target_pairs={{0,16},{1,17},{2,18},{3,19},{4,20},{5,21},{6,22},{7,23},{8,24},{9,... | collective-permute-start | bytes 1179656 | tf_op jit(solution)/shard_map/ppermute | solution.py:153
  60.2 21.3 %collective-permute-start.6 = (bf16[16,2,48,128]{3,2,1,0:T(8,128)(2,1)S(1)}, bf16[16,2,48,128]{3,2,1,0:T(8,128)(2,1)S(1)}, u32[]{:S(2)}, u32[]{:S(2)}) collective-permute-start(bf16[16,2,48,128]{3,2,1,0:T(8,128)(2,1)S(1)} %collective-permute-done.5.piece.refs_5_), channel_id=1, source_target_pairs={{0,112},{1,113},{2,114},{3,115},{4,116},{5,117},{6,118},{7,119},{8... | collective-permute-start | bytes 1179656 | tf_op jit(solution)/shard_map/ppermute | solution.py:153
  65.1 16.4 %collective-permute-start.3 = (bf16[16,2,48,128]{3,2,1,0:T(8,128)(2,1)S(1)}, bf16[16,2,48,128]{3,2,1,0:T(8,128)(2,1)S(1)}, u32[]{:S(2)}, u32[]{:S(2)}) collective-permute-start(bf16[16,2,48,128]{3,2,1,0:T(8,128)(2,1)S(1)} %collective-permute-done.2.refs_2_), channel_id=1, source_target_pairs={{0,16},{1,17},{2,18},{3,19},{4,20},{5,21},{6,22},{7,23},{8,24},{9,... | collective-permute-start | bytes 1179656 | tf_op jit(solution)/shard_map/ppermute | solution.py:153
  67.1 8.7 %collective-permute-start.8 = (bf16[8,2,48,128]{3,2,1,0:T(8,128)(2,1)S(1)}, bf16[8,2,48,128]{3,2,1,0:T(8,128)(2,1)S(1)}, u32[]{:S(2)}, u32[]{:S(2)}) collective-permute-start(bf16[8,2,48,128]{3,2,1,0:T(8,128)(2,1)S(1)} %slice.9), channel_id=1, source_target_pairs={{0,96},{1,97},{2,98},{3,99},{4,100},{5,101},{6,102},{7,103},{8,104... | collective-permute-start | bytes 589832 | tf_op jit(solution)/shard_map/ppermute | solution.py:153
  70.6 10.9 %collective-permute-start.7 = (bf16[8,2,48,128]{3,2,1,0:T(8,128)(2,1)S(1)}, bf16[8,2,48,128]{3,2,1,0:T(8,128)(2,1)S(1)}, u32[]{:S(2)}, u32[]{:S(2)}) collective-permute-start(bf16[8,2,48,128]{3,2,1,0:T(8,128)(2,1)S(1)} %slice.8), channel_id=1, source_target_pairs={{0,32},{1,33},{2,34},{3,35},{4,36},{5,37},{6,38},{7,39},{8,40},{9,... | collective-permute-start | bytes 589832 | tf_op jit(solution)/shard_map/ppermute | solution.py:153
  73.4 0.7 copy-start.3
  74.1 7.4 %copy-start.1 = (bf16[6144,192]{0,1:T(8,128)(2,1)S(1)}, bf16[6144,192]{0,1:T(8,128)(2,1)}, u32[]{:S(2)}) copy-start(bf16[6144,192]{0,1:T(8,128)(2,1)} %param.8) | copy-start | bytes 7077892
  74.1 7.4 %copy-start.2 = (bf16[1,128,192]{1,2,0:T(8,128)(2,1)S(1)}, bf16[1,128,192]{1,2,0:T(8,128)(2,1)}, u32[]{:S(2)}) copy-start(bf16[1,128,192]{1,2,0:T(8,128)(2,1)} %param.9) | copy-start | bytes 147460

commit v7 on v4

--- a/solution.py
+++ b/solution.py
@@ -64,11 +64,15 @@
 
 
 def tiles(me, pieces, part):
-    for shift, ref in zip((0, -1, -2, -3, -4, 1, 2, 3), pieces):
+    for shift, ref in zip((0, -1, -2, -3, 1, 2, 3, 4), pieces):
         ring = lax.rem(me + (shift + 8), 8)
         for j in range(8):
             for half in range(2):
-                yield ref.at[2 * j + half, part], ring, j, half
+                yield ref.at[2 * j + half] if shift == 4 or part == 1 else ref.at[2 * j + half, 0], ring, j, half
+
+
+def part_kernel(part, bundle, out):
+    out[...] = bundle[:, part]
 
 
 def spread_kernel(piece, gain, spread):
@@ -115,8 +119,13 @@
 
 
 def grad_kernel(where, *refs):
-    pieces = refs[:8]
-    payload, gain, out, normed, slopes, averages, scales = refs[8:]
+    payload, gain, out, normed, slopes, averages, scales, landed, arrived = refs[8:]
+    copies = []
+    for k in range(8):
+        source = refs[k] if k == 7 else refs[k].at[:, 1]
+        copies.append(pltpu.make_async_copy(source, landed.at[k], arrived.at[k]))
+        copies[k].start()
+    pieces = [landed.at[k] for k in range(8)]
     first = where[2] * 768
     on_y = where[0] == 0
     for image in range(8):
@@ -125,6 +134,8 @@
         lines = ref[192:208, :].astype(F32)
         averages[image : image + 1, :] = lines[0:1] + lines[1:2] + lines[2:3]
         scales[image : image + 1, :] = lines[3:4] + lines[4:5] + lines[5:6]
+    for copy in copies:
+        copy.wait()
     for tile, ring, j, half in tiles(where[1], pieces, 1):
         image = jnp.where(on_y, ring, j)
         place = pl.multiple_of(jnp.where(on_y, j * 96, ring * 96) + half * 48, 16)
@@ -138,6 +149,18 @@
 
 VMEM = pl.BlockSpec(memory_space=pltpu.VMEM)
 SMEM = pl.BlockSpec(memory_space=pltpu.SMEM)
+ANY = pl.BlockSpec(memory_space=pltpu.HBM)
+
+
+def part_of(part, bundle):
+    return pl.pallas_call(
+        lambda *refs: part_kernel(part, *refs),
+        out_shape=jax.ShapeDtypeStruct((16, 48, KEEP), BF),
+        in_specs=[VMEM],
+        out_specs=VMEM,
+        compiler_params=pltpu.CompilerParams(vmem_limit_bytes=24 * 2**20),
+        name="own_part" if part == 0 else "other_part",
+    )(bundle)
 
 
 def shards(patches, keep_list, norm_gain, up_weight, hidden_grad):
@@ -163,8 +186,8 @@
         name="spread",
     )(b2, norm_gain.reshape(D // 128, 128))
     f3, b3 = move(f2, 1), move(b2, -1)
-    f4 = move(f3, 1)
-    pieces = (both, f1, f2, f3, f4, b1, b2, b3)
+    f4, b4 = move(part_of(0, f2), 2), move(part_of(1, b2), -2)
+    pieces = (both, f1, f2, f3, b1, b2, b3)
 
     hidden, payload = pl.pallas_call(
         forward_kernel,
@@ -174,7 +197,7 @@
         scratch_shapes=[pltpu.VMEM((D, KEEP), BF)],
         compiler_params=pltpu.CompilerParams(vmem_limit_bytes=24 * 2**20),
         name="forward",
-    )(where, *pieces, up_weight.T, gain_all, hidden_grad[0].T)
+    )(where, *pieces, f4, up_weight.T, gain_all, hidden_grad[0].T)
 
     payload = lax.all_to_all(payload, "dp", 0, 0, axis_index_groups=[[0, 2, 4, 6], [1, 3, 5, 7]])
     payload = lax.all_gather(payload, "dp", axis_index_groups=[[0, 1], [2, 3], [4, 5], [6, 7]])
@@ -182,17 +205,19 @@
     grad = pl.pallas_call(
         grad_kernel,
         out_shape=jax.ShapeDtypeStruct((192, 768), F32),
-        in_specs=[SMEM] + [VMEM] * 10,
+        in_specs=[SMEM] + [ANY] * 8 + [VMEM] * 2,
         out_specs=VMEM,
         scratch_shapes=[
             pltpu.VMEM((768, 1024), BF),
             pltpu.VMEM((192, 1024), BF),
             pltpu.VMEM((8, KEEP), F32),
             pltpu.VMEM((8, KEEP), F32),
+            pltpu.VMEM((8, 16, 48, KEEP), BF),
+            pltpu.SemaphoreType.DMA((8,)),
         ],
         compiler_params=pltpu.CompilerParams(vmem_limit_bytes=24 * 2**20),
         name="weight_grad",
-    )(where, *pieces, payload, gain_all)
+    )(where, *pieces, b4, payload, gain_all)
     return (hidden.T[None], grad.T)
 
 

time: 110 us -> 109 us (level); the launches traced: 109 us -> 107 us
  blocking collectives: 46.2 us -> 33.1 us
  starting transfers between devices: 39.8 us -> 45.7 us
  Pallas kernels: 6.45 us -> 11.9 us
    all_to_all x1 -> x0, blocking collectives: 10.9 us -> none  [shards(): lax.all_to_all(payload, 'dp', 0, 0, axis_index_groups=[[0, 2, 4, 6], [1,...]
    ppermute x7 -> x8, waiting for transfers between devices: 12.2 us -> 7.92 us  [shards(): move = lambda piece, step: lax.ppermute(piece, AXES, ring_pairs(step))]
    all_to_all x0 -> x1, starting transfers between devices: none -> 4.01 us  [shards(): lax.all_to_all(payload, 'dp', 0, 0, axis_index_groups=[[0, 2, 4, 6], [1,...]
    all_to_all x0 -> x1, waiting for transfers between devices: none -> 3.96 us  [shards(): lax.all_to_all(payload, 'dp', 0, 0, axis_index_groups=[[0, 2, 4, 6], [1,...]
    pallas_call x0 -> x2, Pallas kernels: none -> 2.69 us  [part_of(): pl.pallas_call(lambda *refs: part_kernel(part, *refs), out_shape=jax.Shap...]
    all_gather x1, blocking collectives: 9.76 us -> 7.43 us  [shards(): lax.all_gather(payload, 'dp', axis_index_groups=[[0, 1], [2, 3], [4, 5],...]
    ppermute x7 -> x8, starting transfers between devices: 35.1 us -> 36.9 us  [shards(): move = lambda piece, step: lax.ppermute(piece, AXES, ring_pairs(step))]
    pallas_call x1, Pallas kernels: 2.61 us -> 4.06 us  [shards(): pl.pallas_call(grad_kernel, out_shape=jax.ShapeDtypeStruct((192, 768), F3...]
  transfers between devices with their start and end apart: 8 -> 10, of which waited for: 4 -> 4; matrix products, arithmetic and copies ran while one was open for 0% -> 0% of each run, Pallas kernels for 1% -> 3%
where the time goes in v7:
time: 109 us; the launch traced here: 107 us
  starting transfers between devices  45.7 us (42%)
  blocking collectives  33.1 us (30%)
  waiting for transfers between devices  13.2 us (12%)
  Pallas kernels  11.9 us (11%)
  local copies, waits for them, and re-layouts  1.53 us (1%)
    ppermute x8, starting transfers between devices, shards(): move = lambda piece, step: lax.ppermute(piece, AXES, ring_pairs(step))  36.9 us
    all_to_all x1, blocking collectives, shards(): both = lax.all_to_all(both, AXES, 0, 0, axis_index_groups=first_groups())  25.6 us
    ppermute x8, waiting for transfers between devices, shards(): move = lambda piece, step: lax.ppermute(piece, AXES, ring_pairs(step))  7.92 us
    all_gather x1, blocking collectives, shards(): lax.all_gather(payload, 'dp', axis_index_groups=[[0, 1], [2, 3], [4, 5],...  7.43 us
    ppermute x1, starting transfers between devices, shards(): other = lax.ppermute(own, AXES, swap_pairs())  4.7 us
    pallas_call x1, Pallas kernels, shards(): pl.pallas_call(forward_kernel, out_shape=(jax.ShapeDtypeStruct((192, KEEP...  4.27 us
    pallas_call x1, Pallas kernels, shards(): pl.pallas_call(grad_kernel, out_shape=jax.ShapeDtypeStruct((192, 768), F3...  4.06 us
    all_to_all x1, starting transfers between devices, shards(): lax.all_to_all(payload, 'dp', 0, 0, axis_index_groups=[[0, 2, 4, 6], [1,...  4.01 us
  transfers between devices with their start and end apart: 10, of which 4 were waited for; matrix products, arithmetic and copies ran while one was open for 0% of the time, Pallas kernels for 3%

profile of v7, /device:TPU:1, one launch (start us, length us, event | category | flops | bytes accessed | tf_op | source)
XLA Modules:
  0.0 107.1 jit_solution(15342607095421316105)
XLA Ops:
  0.6 0.7 copy-done
  1.4 0.8 convolution_convert_fusion
  2.2 4.7 %collective-permute-start = (bf16[48,128]{1,0:T(8,128)(2,1)S(1)}, bf16[48,128]{1,0:T(8,128)(2,1)S(1)}, u32[]{:S(2)}, u32[]{:S(2)}) collective-permute-start(bf16[48,128]{1,0:T(8,128)(2,1)S(1)} %bitcast.26), channel_id=1, source_target_pairs={{0,0},{1,1},{2,2},{3,3},{4,4},{5,5},{6,6},{7,7},{8,8},{9,9},{10,10... | collective-permute-start | bytes 36872 | tf_op jit(solution)/shard_map/ppermute | solution.py:173
  6.9 1.4 %collective-permute-done = bf16[48,128]{1,0:T(8,128)(2,1)S(1)} collective-permute-done((bf16[48,128]{1,0:T(8,128)(2,1)S(1)}, bf16[48,128]{1,0:T(8,128)(2,1)S(1)}, u32[]{:S(2)}, u32[]{:S(2)}) %collective-permute-start) | collective-permute-done | bytes 12320 | tf_op jit(solution)/shard_map/ppermute | solution.py:173
  8.3 25.6 %all_to_all.10.refs_0_ = bf16[16,2,48,128]{3,2,1,0:T(8,128)(2,1)} all-to-all(bf16[16,2,48,128]{3,2,1,0:T(8,128)(2,1)S(1)} %broadcast_in_dim.4), channel_id=1, replica_groups={{0,1,2,3,4,5,6,7,8,9,10,11,12,13,14,15},{16,17,18,19,20,21,22,23,24,25,..., dimensions={0} | all-to-all | bytes 786432 | tf_op jit(solution)/shard_map/all_to_all | solution.py:175
  33.9 16.1 %collective-permute-start.5 = (bf16[16,2,48,128]{3,2,1,0:T(8,128)(2,1)}, bf16[16,2,48,128]{3,2,1,0:T(8,128)(2,1)}, u32[]{:S(2)}, u32[]{:S(2)}) collective-permute-start(bf16[16,2,48,128]{3,2,1,0:T(8,128)(2,1)} %all_to_all.10.refs_0_), channel_id=1, source_target_pairs={{0,96},{1,97},{2,98},{3,99},{4,100},{5,101},{6,102},{7,103},{8,104... | collective-permute-start | bytes 1179656 | tf_op jit(solution)/shard_map/ppermute | solution.py:176
  50.1 1.9 %collective-permute-start.2 = (bf16[16,2,48,128]{3,2,1,0:T(8,128)(2,1)}, bf16[16,2,48,128]{3,2,1,0:T(8,128)(2,1)}, u32[]{:S(2)}, u32[]{:S(2)}) collective-permute-start(bf16[16,2,48,128]{3,2,1,0:T(8,128)(2,1)} %all_to_all.10.refs_0_), channel_id=1, source_target_pairs={{0,32},{1,33},{2,34},{3,35},{4,36},{5,37},{6,38},{7,39},{8,40},{9,... | collective-permute-start | bytes 1179656 | tf_op jit(solution)/shard_map/ppermute | solution.py:176
  52.0 6.4 %collective-permute-start.4 = (bf16[16,2,48,128]{3,2,1,0:T(8,128)(2,1)}, bf16[16,2,48,128]{3,2,1,0:T(8,128)(2,1)}, u32[]{:S(2)}, u32[]{:S(2)}) collective-permute-start(bf16[16,2,48,128]{3,2,1,0:T(8,128)(2,1)} %all_to_all.10.refs_0_), channel_id=1, source_target_pairs={{0,112},{1,113},{2,114},{3,115},{4,116},{5,117},{6,118},{7,119},{8... | collective-permute-start | bytes 1179656 | tf_op jit(solution)/shard_map/ppermute | solution.py:176
  58.4 1.9 %collective-permute-start.1 = (bf16[16,2,48,128]{3,2,1,0:T(8,128)(2,1)}, bf16[16,2,48,128]{3,2,1,0:T(8,128)(2,1)}, u32[]{:S(2)}, u32[]{:S(2)}) collective-permute-start(bf16[16,2,48,128]{3,2,1,0:T(8,128)(2,1)} %all_to_all.10.refs_0_), channel_id=1, source_target_pairs={{0,16},{1,17},{2,18},{3,19},{4,20},{5,21},{6,22},{7,23},{8,24},{9,... | collective-permute-start | bytes 1179656 | tf_op jit(solution)/shard_map/ppermute | solution.py:176
  60.3 4.6 %collective-permute-start.6 = (bf16[16,2,48,128]{3,2,1,0:T(8,128)(2,1)}, bf16[16,2,48,128]{3,2,1,0:T(8,128)(2,1)}, u32[]{:S(2)}, u32[]{:S(2)}) collective-permute-start(bf16[16,2,48,128]{3,2,1,0:T(8,128)(2,1)} %collective-permute-done.5.piece.refs_5_.refs_0_), channel_id=1, source_target_pairs={{0,112},{1,113},{2,114},{3,115},{4,116},{5,117},{6,118},{7,119},{8... | collective-permute-start | bytes 1179656 | tf_op jit(solution)/shard_map/ppermute | solution.py:176
  64.9 0.6 collective-permute-done.2.refs_0_.refs_2_
  65.5 1.9 %collective-permute-start.3 = (bf16[16,2,48,128]{3,2,1,0:T(8,128)(2,1)}, bf16[16,2,48,128]{3,2,1,0:T(8,128)(2,1)}, u32[]{:S(2)}, u32[]{:S(2)}) collective-permute-start(bf16[16,2,48,128]{3,2,1,0:T(8,128)(2,1)} %collective-permute-done.2.refs_0_.refs_2_), channel_id=1, source_target_pairs={{0,16},{1,17},{2,18},{3,19},{4,20},{5,21},{6,22},{7,23},{8,24},{9,... | collective-permute-start | bytes 1179656 | tf_op jit(solution)/shard_map/ppermute | solution.py:176
  67.5 1.0 own_part.1
  68.6 1.9 %collective-permute-start.7 = (bf16[16,48,128]{2,1,0:T(8,128)(2,1)S(1)}, bf16[16,48,128]{2,1,0:T(8,128)(2,1)S(1)}, u32[]{:S(2)}, u32[]{:S(2)}) collective-permute-start(bf16[16,48,128]{2,1,0:T(8,128)(2,1)S(1)} %own_part.1), channel_id=1, source_target_pairs={{0,32},{1,33},{2,34},{3,35},{4,36},{5,37},{6,38},{7,39},{8,40},{9,... | collective-permute-start | bytes 589832 | tf_op jit(solution)/shard_map/ppermute | solution.py:176
  70.5 0.7 copy-done.3
  71.2 0.9 spread.1.refs_9_
  72.1 7.3 %collective-permute-done.7.refs_7_ = bf16[16,48,128]{2,1,0:T(8,128)(2,1)S(1)} collective-permute-done((bf16[16,48,128]{2,1,0:T(8,128)(2,1)S(1)}, bf16[16,48,128]{2,1,0:T(8,128)(2,1)S(1)}, u32[]{:S(2)}, u32[]{:S(2)}) %collective-permute-start.7) | collective-permute-done | bytes 196640 | tf_op jit(solution)/shard_map/ppermute | solution.py:176
  79.5 4.3 %forward.1 = (bf16[192,128]{1,0:T(8,128)(2,1)}, bf16[4,208,128]{2,1,0:T(8,128)(2,1)}) custom-call(s32[3]{0:T(128)S(1)} %pad_add_fusion.where, bf16[16,2,48,128]{3,2,1,0:T(8,128)(2,1)} %all_to_all.10.refs_0_, bf16[16,2,48,128]{3,2,1,0:T(8,128)(2,1)} %collective-permute-done.1.refs_1_, bf16[16,2,48,128]{3,2,1,0:T(8,128)(2,1)} %collective-permute-done.2.refs_0_.refs_2_, ...), custom_call_target="tpu_custom_call" | custom-call | tf_op jit(solution)/shard_map/forward/pallas_call | solution.py:192
  83.7 4.0 %all-to-all-start.1 = ((bf16[4,208,128]{2,1,0:T(8,128)(2,1)}), bf16[4,208,128]{2,1,0:T(8,128)(2,1)}, u32[]{:S(2)}, u32[]{:S(2)}) async-start(bf16[4,208,128]{2,1,0:T(8,128)(2,1)} %get-tuple-element.5), calls=%async_computation.1 | async-start | bytes 425984 | tf_op jit(solution)/shard_map/all_to_all | solution.py:202
  87.7 1.7 %other_part.1 = bf16[16,48,128]{2,1,0:T(8,128)(2,1)} custom-call(bf16[16,2,48,128]{3,2,1,0:T(8,128)(2,1)} %collective-permute-done.5.piece.refs_5_.refs_0_), custom_call_target="tpu_custom_call" | custom-call | tf_op jit(solution)/shard_map/other_part/pallas_call | solution.py:156
  89.4 2.2 %collective-permute-start.8 = (bf16[16,48,128]{2,1,0:T(8,128)(2,1)}, bf16[16,48,128]{2,1,0:T(8,128)(2,1)S(1)}, u32[]{:S(2)}, u32[]{:S(2)}) collective-permute-start(bf16[16,48,128]{2,1,0:T(8,128)(2,1)} %other_part.1), channel_id=1, source_target_pairs={{0,96},{1,97},{2,98},{3,99},{4,100},{5,101},{6,102},{7,103},{8,104... | collective-permute-start | bytes 589832 | tf_op jit(solution)/shard_map/ppermute | solution.py:176
  91.6 4.0 %all-to-all-done.1 = bf16[4,208,128]{2,1,0:T(8,128)(2,1)} async-done(((bf16[4,208,128]{2,1,0:T(8,128)(2,1)}), bf16[4,208,128]{2,1,0:T(8,128)(2,1)}, u32[]{:S(2)}, u32[]{:S(2)}) %all-to-all-start.1) | async-done | bytes 213024 | tf_op jit(solution)/shard_map/all_to_all | solution.py:202
  95.6 7.4 %all-gather = bf16[8,208,128]{2,1,0:T(8,128)(2,1)S(1)} all-gather(bf16[4,208,128]{2,1,0:T(8,128)(2,1)} %all-to-all-done.1), channel_id=2, replica_groups={{0,128},{256,384},{512,640},{768,896},{1,129},{257,385},{513,641},{769,..., dimensions={0}, use_global_device_ids=true | all-gather | bytes 638976 | tf_op jit(solution)/shard_map/all_gather | solution.py:203
  103.0 4.1 %weight_grad.1 = f32[192,768]{1,0:T(8,128)} custom-call(s32[3]{0:T(128)S(1)} %pad_add_fusion.where, bf16[16,2,48,128]{3,2,1,0:T(8,128)(2,1)} %all_to_all.10.refs_0_, bf16[16,2,48,128]{3,2,1,0:T(8,128)(2,1)} %collective-permute-done.1.refs_1_, bf16[16,2,48,128]{3,2,1,0:T(8,128)(2,1)} %collective-permute-done.2.refs_0_.refs_2_, ...), custom_call_target="tpu_custom_call" | custom-call | tf_op jit(solution)/shard_map/weight_grad/pallas_call | solution.py:205
  (15 shorter events, 0.2 us)
Async XLA Ops:
  0.6 0.7 copy-start
  2.2 6.1 %collective-permute-start = (bf16[48,128]{1,0:T(8,128)(2,1)S(1)}, bf16[48,128]{1,0:T(8,128)(2,1)S(1)}, u32[]{:S(2)}, u32[]{:S(2)}) collective-permute-start(bf16[48,128]{1,0:T(8,128)(2,1)S(1)} %bitcast.26), channel_id=1, source_target_pairs={{0,0},{1,1},{2,2},{3,3},{4,4},{5,5},{6,6},{7,7},{8,8},{9,9},{10,10... | collective-permute-start | bytes 36872 | tf_op jit(solution)/shard_map/ppermute | solution.py:173
  33.9 26.4 %collective-permute-start.5 = (bf16[16,2,48,128]{3,2,1,0:T(8,128)(2,1)}, bf16[16,2,48,128]{3,2,1,0:T(8,128)(2,1)}, u32[]{:S(2)}, u32[]{:S(2)}) collective-permute-start(bf16[16,2,48,128]{3,2,1,0:T(8,128)(2,1)} %all_to_all.10.refs_0_), channel_id=1, source_target_pairs={{0,96},{1,97},{2,98},{3,99},{4,100},{5,101},{6,102},{7,103},{8,104... | collective-permute-start | bytes 1179656 | tf_op jit(solution)/shard_map/ppermute | solution.py:176
  50.1 15.4 %collective-permute-start.2 = (bf16[16,2,48,128]{3,2,1,0:T(8,128)(2,1)}, bf16[16,2,48,128]{3,2,1,0:T(8,128)(2,1)}, u32[]{:S(2)}, u32[]{:S(2)}) collective-permute-start(bf16[16,2,48,128]{3,2,1,0:T(8,128)(2,1)} %all_to_all.10.refs_0_), channel_id=1, source_target_pairs={{0,32},{1,33},{2,34},{3,35},{4,36},{5,37},{6,38},{7,39},{8,40},{9,... | collective-permute-start | bytes 1179656 | tf_op jit(solution)/shard_map/ppermute | solution.py:176
  52.0 20.1 %collective-permute-start.4 = (bf16[16,2,48,128]{3,2,1,0:T(8,128)(2,1)}, bf16[16,2,48,128]{3,2,1,0:T(8,128)(2,1)}, u32[]{:S(2)}, u32[]{:S(2)}) collective-permute-start(bf16[16,2,48,128]{3,2,1,0:T(8,128)(2,1)} %all_to_all.10.refs_0_), channel_id=1, source_target_pairs={{0,112},{1,113},{2,114},{3,115},{4,116},{5,117},{6,118},{7,119},{8... | collective-permute-start | bytes 1179656 | tf_op jit(solution)/shard_map/ppermute | solution.py:176
  58.4 13.7 %collective-permute-start.1 = (bf16[16,2,48,128]{3,2,1,0:T(8,128)(2,1)}, bf16[16,2,48,128]{3,2,1,0:T(8,128)(2,1)}, u32[]{:S(2)}, u32[]{:S(2)}) collective-permute-start(bf16[16,2,48,128]{3,2,1,0:T(8,128)(2,1)} %all_to_all.10.refs_0_), channel_id=1, source_target_pairs={{0,16},{1,17},{2,18},{3,19},{4,20},{5,21},{6,22},{7,23},{8,24},{9,... | collective-permute-start | bytes 1179656 | tf_op jit(solution)/shard_map/ppermute | solution.py:176
  60.3 19.1 %collective-permute-start.6 = (bf16[16,2,48,128]{3,2,1,0:T(8,128)(2,1)}, bf16[16,2,48,128]{3,2,1,0:T(8,128)(2,1)}, u32[]{:S(2)}, u32[]{:S(2)}) collective-permute-start(bf16[16,2,48,128]{3,2,1,0:T(8,128)(2,1)} %collective-permute-done.5.piece.refs_5_.refs_0_), channel_id=1, source_target_pairs={{0,112},{1,113},{2,114},{3,115},{4,116},{5,117},{6,118},{7,119},{8... | collective-permute-start | bytes 1179656 | tf_op jit(solution)/shard_map/ppermute | solution.py:176
  65.5 13.9 %collective-permute-start.3 = (bf16[16,2,48,128]{3,2,1,0:T(8,128)(2,1)}, bf16[16,2,48,128]{3,2,1,0:T(8,128)(2,1)}, u32[]{:S(2)}, u32[]{:S(2)}) collective-permute-start(bf16[16,2,48,128]{3,2,1,0:T(8,128)(2,1)} %collective-permute-done.2.refs_0_.refs_2_), channel_id=1, source_target_pairs={{0,16},{1,17},{2,18},{3,19},{4,20},{5,21},{6,22},{7,23},{8,24},{9,... | collective-permute-start | bytes 1179656 | tf_op jit(solution)/shard_map/ppermute | solution.py:176
  68.6 10.9 %collective-permute-start.7 = (bf16[16,48,128]{2,1,0:T(8,128)(2,1)S(1)}, bf16[16,48,128]{2,1,0:T(8,128)(2,1)S(1)}, u32[]{:S(2)}, u32[]{:S(2)}) collective-permute-start(bf16[16,48,128]{2,1,0:T(8,128)(2,1)S(1)} %own_part.1), channel_id=1, source_target_pairs={{0,32},{1,33},{2,34},{3,35},{4,36},{5,37},{6,38},{7,39},{8,40},{9,... | collective-permute-start | bytes 589832 | tf_op jit(solution)/shard_map/ppermute | solution.py:176
  70.5 0.7 copy-start.3
  71.2 8.2 %copy-start.1 = (bf16[6144,192]{0,1:T(8,128)(2,1)S(1)}, bf16[6144,192]{0,1:T(8,128)(2,1)}, u32[]{:S(2)}) copy-start(bf16[6144,192]{0,1:T(8,128)(2,1)} %param.8) | copy-start | bytes 7077892
  71.2 8.2 %copy-start.2 = (bf16[1,128,192]{1,2,0:T(8,128)(2,1)S(1)}, bf16[1,128,192]{1,2,0:T(8,128)(2,1)}, u32[]{:S(2)}) copy-start(bf16[1,128,192]{1,2,0:T(8,128)(2,1)} %param.9) | copy-start | bytes 147460
  83.7 11.9 %all-to-all-start.1 = ((bf16[4,208,128]{2,1,0:T(8,128)(2,1)}), bf16[4,208,128]{2,1,0:T(8,128)(2,1)}, u32[]{:S(2)}, u32[]{:S(2)}) async-start(bf16[4,208,128]{2,1,0:T(8,128)(2,1)} %get-tuple-element.5), calls=%async_computation.1 | async-start | bytes 425984 | tf_op jit(solution)/shard_map/all_to_all | solution.py:202
  89.4 13.6 %collective-permute-start.8 = (bf16[16,48,128]{2,1,0:T(8,128)(2,1)}, bf16[16,48,128]{2,1,0:T(8,128)(2,1)S(1)}, u32[]{:S(2)}, u32[]{:S(2)}) collective-permute-start(bf16[16,48,128]{2,1,0:T(8,128)(2,1)} %other_part.1), channel_id=1, source_target_pairs={{0,96},{1,97},{2,98},{3,99},{4,100},{5,101},{6,102},{7,103},{8,104... | collective-permute-start | bytes 589832 | tf_op jit(solution)/shard_map/ppermute | solution.py:176

commit v8 on v6

--- a/solution.py
+++ b/solution.py
@@ -109,9 +109,8 @@
             value = value - top
     lines.append(jnp.zeros((10, KEEP), F32))
     lines = jnp.concatenate(lines, axis=0).astype(BF)
-    for copy in range(4):
-        payload[copy, 0:192, :] = slope
-        payload[copy, 192:208, :] = lines
+    payload[0:192, :] = slope
+    payload[192:208, :] = lines
 
 
 def grad_kernel(where, *refs):
@@ -120,7 +119,7 @@
     first = where[2] * 768
     on_y = where[0] == 0
     for image in range(8):
-        ref = payload.at[image % 2, image // 2]
+        ref = payload.at[image]
         slopes[:, image * KEEP : (image + 1) * KEEP] = ref[0:192, :]
         lines = ref[192:208, :].astype(F32)
         averages[image : image + 1, :] = lines[0:1] + lines[1:2] + lines[2:3]
@@ -168,7 +167,7 @@
 
     hidden, payload = pl.pallas_call(
         forward_kernel,
-        out_shape=(jax.ShapeDtypeStruct((192, KEEP), BF), jax.ShapeDtypeStruct((4, 208, KEEP), BF)),
+        out_shape=(jax.ShapeDtypeStruct((192, KEEP), BF), jax.ShapeDtypeStruct((208, KEEP), BF)),
         in_specs=[SMEM] + [VMEM] * 12,
         out_specs=(VMEM, VMEM),
         scratch_shapes=[pltpu.VMEM((D, KEEP), BF)],
@@ -176,8 +175,7 @@
         name="forward",
     )(where, *pieces, up_weight.T, gain_all, hidden_grad[0].T)
 
-    payload = lax.all_to_all(payload, "dp", 0, 0, axis_index_groups=[[0, 2, 4, 6], [1, 3, 5, 7]])
-    payload = lax.all_gather(payload, "dp", axis_index_groups=[[0, 1], [2, 3], [4, 5], [6, 7]])
+    payload = lax.all_gather(payload, "dp")
 
     grad = pl.pallas_call(
         grad_kernel,

time: 107 us -> 107 us (level)
    all_to_all x1 -> x0, blocking collectives: 10.9 us -> none  [shards(): lax.all_to_all(payload, 'dp', 0, 0, axis_index_groups=[[0, 2, 4, 6], [1,...]
    all_gather x1, blocking collectives: 8.69 us -> 19.1 us  [shards(): payload = lax.all_gather(payload, 'dp')]
where the time goes in v8:
time: 107 us; the launch traced here: 106 us
  blocking collectives  44.6 us (42%)
  starting transfers between devices  43.7 us (41%)
  waiting for transfers between devices  8.16 us (8%)
  Pallas kernels  6.5 us (6%)
  local copies, waits for them, and re-layouts  1.56 us (1%)
    ppermute x8, starting transfers between devices, shards(): move = lambda piece, step: lax.ppermute(piece, AXES, ring_pairs(step))  39 us
    all_to_all x1, blocking collectives, shards(): both = lax.all_to_all(both, AXES, 0, 0, axis_index_groups=first_groups())  25.5 us
    all_gather x1, blocking collectives, shards(): payload = lax.all_gather(payload, 'dp')  19.1 us
    ppermute x8, waiting for transfers between devices, shards(): move = lambda piece, step: lax.ppermute(piece, AXES, ring_pairs(step))  6.8 us
    ppermute x1, starting transfers between devices, shards(): other = lax.ppermute(own, AXES, swap_pairs())  4.7 us
    pallas_call x1, Pallas kernels, shards(): pl.pallas_call(forward_kernel, out_shape=(jax.ShapeDtypeStruct((192, KEEP...  3.02 us
    pallas_call x1, Pallas kernels, shards(): pl.pallas_call(grad_kernel, out_shape=jax.ShapeDtypeStruct((192, 768), F3...  2.62 us
  transfers between devices with their start and end apart: 9, of which 4 were waited for; matrix products, arithmetic and copies ran while one was open for 0% of the time, Pallas kernels for 1%

profile of v8, /device:TPU:1, one launch (start us, length us, event | category | flops | bytes accessed | tf_op | source)
XLA Modules:
  0.0 106.2 jit_solution(12396446973342032029)
XLA Ops:
  0.6 0.0 copy-start
  0.6 0.7 copy-done
  1.4 0.8 convolution_convert_fusion
  2.2 4.7 %collective-permute-start = (bf16[48,128]{1,0:T(8,128)(2,1)S(1)}, bf16[48,128]{1,0:T(8,128)(2,1)S(1)}, u32[]{:S(2)}, u32[]{:S(2)}) collective-permute-start(bf16[48,128]{1,0:T(8,128)(2,1)S(1)} %bitcast.26), channel_id=1, source_target_pairs={{0,0},{1,1},{2,2},{3,3},{4,4},{5,5},{6,6},{7,7},{8,8},{9,9},{10,10... | collective-permute-start | bytes 36872 | tf_op jit(solution)/shard_map/ppermute | solution.py:149
  6.9 1.4 %collective-permute-done = bf16[48,128]{1,0:T(8,128)(2,1)S(1)} collective-permute-done((bf16[48,128]{1,0:T(8,128)(2,1)S(1)}, bf16[48,128]{1,0:T(8,128)(2,1)S(1)}, u32[]{:S(2)}, u32[]{:S(2)}) %collective-permute-start) | collective-permute-done | bytes 12320 | tf_op jit(solution)/shard_map/ppermute | solution.py:149
  8.3 0.1 broadcast_in_dim.4
  8.3 25.5 %all_to_all.5.refs_0_ = bf16[16,2,48,128]{3,2,1,0:T(8,128)(2,1)S(1)} all-to-all(bf16[16,2,48,128]{3,2,1,0:T(8,128)(2,1)S(1)} %broadcast_in_dim.4), channel_id=1, replica_groups={{0,1,2,3,4,5,6,7,8,9,10,11,12,13,14,15},{16,17,18,19,20,21,22,23,24,25,..., dimensions={0} | all-to-all | bytes 786432 | tf_op jit(solution)/shard_map/all_to_all | solution.py:151
  33.8 16.1 %collective-permute-start.5 = (bf16[16,2,48,128]{3,2,1,0:T(8,128)(2,1)S(1)}, bf16[16,2,48,128]{3,2,1,0:T(8,128)(2,1)S(1)}, u32[]{:S(2)}, u32[]{:S(2)}) collective-permute-start(bf16[16,2,48,128]{3,2,1,0:T(8,128)(2,1)S(1)} %all_to_all.5.refs_0_), channel_id=1, source_target_pairs={{0,96},{1,97},{2,98},{3,99},{4,100},{5,101},{6,102},{7,103},{8,104... | collective-permute-start | bytes 1179656 | tf_op jit(solution)/shard_map/ppermute | solution.py:152
  49.9 1.9 %collective-permute-start.2 = (bf16[16,2,48,128]{3,2,1,0:T(8,128)(2,1)S(1)}, bf16[16,2,48,128]{3,2,1,0:T(8,128)(2,1)S(1)}, u32[]{:S(2)}, u32[]{:S(2)}) collective-permute-start(bf16[16,2,48,128]{3,2,1,0:T(8,128)(2,1)S(1)} %all_to_all.5.refs_0_), channel_id=1, source_target_pairs={{0,32},{1,33},{2,34},{3,35},{4,36},{5,37},{6,38},{7,39},{8,40},{9,... | collective-permute-start | bytes 1179656 | tf_op jit(solution)/shard_map/ppermute | solution.py:152
  51.9 6.4 %collective-permute-start.4 = (bf16[16,2,48,128]{3,2,1,0:T(8,128)(2,1)S(1)}, bf16[16,2,48,128]{3,2,1,0:T(8,128)(2,1)S(1)}, u32[]{:S(2)}, u32[]{:S(2)}) collective-permute-start(bf16[16,2,48,128]{3,2,1,0:T(8,128)(2,1)S(1)} %all_to_all.5.refs_0_), channel_id=1, source_target_pairs={{0,112},{1,113},{2,114},{3,115},{4,116},{5,117},{6,118},{7,119},{8... | collective-permute-start | bytes 1179656 | tf_op jit(solution)/shard_map/ppermute | solution.py:152
  58.3 1.9 %collective-permute-start.1 = (bf16[16,2,48,128]{3,2,1,0:T(8,128)(2,1)S(1)}, bf16[16,2,48,128]{3,2,1,0:T(8,128)(2,1)S(1)}, u32[]{:S(2)}, u32[]{:S(2)}) collective-permute-start(bf16[16,2,48,128]{3,2,1,0:T(8,128)(2,1)S(1)} %all_to_all.5.refs_0_), channel_id=1, source_target_pairs={{0,16},{1,17},{2,18},{3,19},{4,20},{5,21},{6,22},{7,23},{8,24},{9,... | collective-permute-start | bytes 1179656 | tf_op jit(solution)/shard_map/ppermute | solution.py:152
  60.2 4.6 %collective-permute-start.6 = (bf16[16,2,48,128]{3,2,1,0:T(8,128)(2,1)S(1)}, bf16[16,2,48,128]{3,2,1,0:T(8,128)(2,1)S(1)}, u32[]{:S(2)}, u32[]{:S(2)}) collective-permute-start(bf16[16,2,48,128]{3,2,1,0:T(8,128)(2,1)S(1)} %collective-permute-done.5.piece.refs_5_), channel_id=1, source_target_pairs={{0,112},{1,113},{2,114},{3,115},{4,116},{5,117},{6,118},{7,119},{8... | collective-permute-start | bytes 1179656 | tf_op jit(solution)/shard_map/ppermute | solution.py:152
  64.8 0.3 collective-permute-done.2.refs_2_
  65.1 1.9 %collective-permute-start.3 = (bf16[16,2,48,128]{3,2,1,0:T(8,128)(2,1)S(1)}, bf16[16,2,48,128]{3,2,1,0:T(8,128)(2,1)S(1)}, u32[]{:S(2)}, u32[]{:S(2)}) collective-permute-start(bf16[16,2,48,128]{3,2,1,0:T(8,128)(2,1)S(1)} %collective-permute-done.2.refs_2_), channel_id=1, source_target_pairs={{0,16},{1,17},{2,18},{3,19},{4,20},{5,21},{6,22},{7,23},{8,24},{9,... | collective-permute-start | bytes 1179656 | tf_op jit(solution)/shard_map/ppermute | solution.py:152
  67.0 0.1 pad_add_fusion.where
  67.1 3.4 %collective-permute-start.8 = (bf16[8,2,48,128]{3,2,1,0:T(8,128)(2,1)S(1)}, bf16[8,2,48,128]{3,2,1,0:T(8,128)(2,1)S(1)}, u32[]{:S(2)}, u32[]{:S(2)}) collective-permute-start(bf16[8,2,48,128]{3,2,1,0:T(8,128)(2,1)S(1)} %slice.9), channel_id=1, source_target_pairs={{0,96},{1,97},{2,98},{3,99},{4,100},{5,101},{6,102},{7,103},{8,104... | collective-permute-start | bytes 589832 | tf_op jit(solution)/shard_map/ppermute | solution.py:152
  70.6 2.8 %collective-permute-start.7 = (bf16[8,2,48,128]{3,2,1,0:T(8,128)(2,1)S(1)}, bf16[8,2,48,128]{3,2,1,0:T(8,128)(2,1)S(1)}, u32[]{:S(2)}, u32[]{:S(2)}) collective-permute-start(bf16[8,2,48,128]{3,2,1,0:T(8,128)(2,1)S(1)} %slice.8), channel_id=1, source_target_pairs={{0,32},{1,33},{2,34},{3,35},{4,36},{5,37},{6,38},{7,39},{8,40},{9,... | collective-permute-start | bytes 589832 | tf_op jit(solution)/shard_map/ppermute | solution.py:152
  73.4 0.7 copy-done.3
  74.1 0.9 spread.1.refs_10_
  75.0 0.9 collective-permute-done.8.refs_8_
  75.8 5.6 %collective-permute-done.7.refs_7_ = bf16[8,2,48,128]{3,2,1,0:T(8,128)(2,1)S(1)} collective-permute-done((bf16[8,2,48,128]{3,2,1,0:T(8,128)(2,1)S(1)}, bf16[8,2,48,128]{3,2,1,0:T(8,128)(2,1)S(1)}, u32[]{:S(2)}, u32[]{:S(2)}) %collective-permute-start.7) | collective-permute-done | bytes 196640 | tf_op jit(solution)/shard_map/ppermute | solution.py:152
  81.5 3.0 %forward.1 = (bf16[192,128]{1,0:T(8,128)(2,1)}, bf16[208,128]{1,0:T(8,128)(2,1)S(1)}) custom-call(s32[3]{0:T(128)S(1)} %pad_add_fusion.where, bf16[16,2,48,128]{3,2,1,0:T(8,128)(2,1)S(1)} %all_to_all.5.refs_0_, bf16[16,2,48,128]{3,2,1,0:T(8,128)(2,1)S(1)} %collective-permute-done.1.refs_1_, bf16[16,2,48,128]{3,2,1,0:T(8,128)(2,1)S(1)} %collective-permute-done.2.refs_2_, ...), custom_call_target="tpu_custom_call" | custom-call | tf_op jit(solution)/shard_map/forward/pallas_call | solution.py:168
  84.5 19.1 %all-gather = bf16[1664,128]{1,0:T(8,128)(2,1)S(1)} all-gather(bf16[208,128]{1,0:T(8,128)(2,1)S(1)} %get-tuple-element.5), channel_id=2, replica_groups=mesh['dp'=8,'mp'=128] {'dp'}, dimensions={0}, use_global_device_ids=true | all-gather | bytes 479232 | tf_op jit(solution)/shard_map/all_gather | solution.py:178
  103.6 2.6 %weight_grad.1 = f32[192,768]{1,0:T(8,128)} custom-call(s32[3]{0:T(128)S(1)} %pad_add_fusion.where, bf16[16,2,48,128]{3,2,1,0:T(8,128)(2,1)S(1)} %all_to_all.5.refs_0_, bf16[16,2,48,128]{3,2,1,0:T(8,128)(2,1)S(1)} %collective-permute-done.1.refs_1_, bf16[16,2,48,128]{3,2,1,0:T(8,128)(2,1)S(1)} %collective-permute-done.2.refs_2_, ...), custom_call_target="tpu_custom_call" | custom-call | tf_op jit(solution)/shard_map/weight_grad/pallas_call | solution.py:180
  (13 shorter events, 0.1 us)
Async XLA Ops:
  0.6 0.7 copy-start
  2.2 6.1 %collective-permute-start = (bf16[48,128]{1,0:T(8,128)(2,1)S(1)}, bf16[48,128]{1,0:T(8,128)(2,1)S(1)}, u32[]{:S(2)}, u32[]{:S(2)}) collective-permute-start(bf16[48,128]{1,0:T(8,128)(2,1)S(1)} %bitcast.26), channel_id=1, source_target_pairs={{0,0},{1,1},{2,2},{3,3},{4,4},{5,5},{6,6},{7,7},{8,8},{9,9},{10,10... | collective-permute-start | bytes 36872 | tf_op jit(solution)/shard_map/ppermute | solution.py:149
  33.8 26.4 %collective-permute-start.5 = (bf16[16,2,48,128]{3,2,1,0:T(8,128)(2,1)S(1)}, bf16[16,2,48,128]{3,2,1,0:T(8,128)(2,1)S(1)}, u32[]{:S(2)}, u32[]{:S(2)}) collective-permute-start(bf16[16,2,48,128]{3,2,1,0:T(8,128)(2,1)S(1)} %all_to_all.5.refs_0_), channel_id=1, source_target_pairs={{0,96},{1,97},{2,98},{3,99},{4,100},{5,101},{6,102},{7,103},{8,104... | collective-permute-start | bytes 1179656 | tf_op jit(solution)/shard_map/ppermute | solution.py:152
  49.9 15.1 %collective-permute-start.2 = (bf16[16,2,48,128]{3,2,1,0:T(8,128)(2,1)S(1)}, bf16[16,2,48,128]{3,2,1,0:T(8,128)(2,1)S(1)}, u32[]{:S(2)}, u32[]{:S(2)}) collective-permute-start(bf16[16,2,48,128]{3,2,1,0:T(8,128)(2,1)S(1)} %all_to_all.5.refs_0_), channel_id=1, source_target_pairs={{0,32},{1,33},{2,34},{3,35},{4,36},{5,37},{6,38},{7,39},{8,40},{9,... | collective-permute-start | bytes 1179656 | tf_op jit(solution)/shard_map/ppermute | solution.py:152
  51.9 18.7 %collective-permute-start.4 = (bf16[16,2,48,128]{3,2,1,0:T(8,128)(2,1)S(1)}, bf16[16,2,48,128]{3,2,1,0:T(8,128)(2,1)S(1)}, u32[]{:S(2)}, u32[]{:S(2)}) collective-permute-start(bf16[16,2,48,128]{3,2,1,0:T(8,128)(2,1)S(1)} %all_to_all.5.refs_0_), channel_id=1, source_target_pairs={{0,112},{1,113},{2,114},{3,115},{4,116},{5,117},{6,118},{7,119},{8... | collective-permute-start | bytes 1179656 | tf_op jit(solution)/shard_map/ppermute | solution.py:152
  58.3 16.7 %collective-permute-start.1 = (bf16[16,2,48,128]{3,2,1,0:T(8,128)(2,1)S(1)}, bf16[16,2,48,128]{3,2,1,0:T(8,128)(2,1)S(1)}, u32[]{:S(2)}, u32[]{:S(2)}) collective-permute-start(bf16[16,2,48,128]{3,2,1,0:T(8,128)(2,1)S(1)} %all_to_all.5.refs_0_), channel_id=1, source_target_pairs={{0,16},{1,17},{2,18},{3,19},{4,20},{5,21},{6,22},{7,23},{8,24},{9,... | collective-permute-start | bytes 1179656 | tf_op jit(solution)/shard_map/ppermute | solution.py:152
  60.2 21.3 %collective-permute-start.6 = (bf16[16,2,48,128]{3,2,1,0:T(8,128)(2,1)S(1)}, bf16[16,2,48,128]{3,2,1,0:T(8,128)(2,1)S(1)}, u32[]{:S(2)}, u32[]{:S(2)}) collective-permute-start(bf16[16,2,48,128]{3,2,1,0:T(8,128)(2,1)S(1)} %collective-permute-done.5.piece.refs_5_), channel_id=1, source_target_pairs={{0,112},{1,113},{2,114},{3,115},{4,116},{5,117},{6,118},{7,119},{8... | collective-permute-start | bytes 1179656 | tf_op jit(solution)/shard_map/ppermute | solution.py:152
  65.1 16.4 %collective-permute-start.3 = (bf16[16,2,48,128]{3,2,1,0:T(8,128)(2,1)S(1)}, bf16[16,2,48,128]{3,2,1,0:T(8,128)(2,1)S(1)}, u32[]{:S(2)}, u32[]{:S(2)}) collective-permute-start(bf16[16,2,48,128]{3,2,1,0:T(8,128)(2,1)S(1)} %collective-permute-done.2.refs_2_), channel_id=1, source_target_pairs={{0,16},{1,17},{2,18},{3,19},{4,20},{5,21},{6,22},{7,23},{8,24},{9,... | collective-permute-start | bytes 1179656 | tf_op jit(solution)/shard_map/ppermute | solution.py:152
  67.1 8.7 %collective-permute-start.8 = (bf16[8,2,48,128]{3,2,1,0:T(8,128)(2,1)S(1)}, bf16[8,2,48,128]{3,2,1,0:T(8,128)(2,1)S(1)}, u32[]{:S(2)}, u32[]{:S(2)}) collective-permute-start(bf16[8,2,48,128]{3,2,1,0:T(8,128)(2,1)S(1)} %slice.9), channel_id=1, source_target_pairs={{0,96},{1,97},{2,98},{3,99},{4,100},{5,101},{6,102},{7,103},{8,104... | collective-permute-start | bytes 589832 | tf_op jit(solution)/shard_map/ppermute | solution.py:152
  70.6 10.9 %collective-permute-start.7 = (bf16[8,2,48,128]{3,2,1,0:T(8,128)(2,1)S(1)}, bf16[8,2,48,128]{3,2,1,0:T(8,128)(2,1)S(1)}, u32[]{:S(2)}, u32[]{:S(2)}) collective-permute-start(bf16[8,2,48,128]{3,2,1,0:T(8,128)(2,1)S(1)} %slice.8), channel_id=1, source_target_pairs={{0,32},{1,33},{2,34},{3,35},{4,36},{5,37},{6,38},{7,39},{8,40},{9,... | collective-permute-start | bytes 589832 | tf_op jit(solution)/shard_map/ppermute | solution.py:152
  73.4 0.7 copy-start.3
  74.1 7.4 %copy-start.1 = (bf16[6144,192]{0,1:T(8,128)(2,1)S(1)}, bf16[6144,192]{0,1:T(8,128)(2,1)}, u32[]{:S(2)}) copy-start(bf16[6144,192]{0,1:T(8,128)(2,1)} %param.8) | copy-start | bytes 7077892
  74.1 7.4 %copy-start.2 = (bf16[1,128,192]{1,2,0:T(8,128)(2,1)S(1)}, bf16[1,128,192]{1,2,0:T(8,128)(2,1)}, u32[]{:S(2)}) copy-start(bf16[1,128,192]{1,2,0:T(8,128)(2,1)} %param.9) | copy-start | bytes 147460
